TPU v7x, 32 devices: a whole 2x2x4 slice. The times are simulated.
32 devices in a mesh: fsdp: 8 (over y, x, core), tp: 4 (over z).
Axes of the slice: x: 2, y: 2, z: 4, core: 2. Of those that a mesh axis runs over, the one named last changes fastest.
Arguments:
- tokens: bfloat16 [1024, 4096], P('fsdp'), may hold values from -6 to 6
- gate_packed: bfloat16 [4096, 7680], P('fsdp', 'tp'), may hold values from -0.125 to 0.125
- up_packed: bfloat16 [4096, 7680], P('fsdp', 'tp'), may hold values from -0.125 to 0.125
- col_slots: int32 [32, 60], P(None, 'tp'), may hold values from 0 to 29, as said below
- readout: bfloat16 [15360], P('tp'), may hold values from -0.046875 to 0.046875
- base_logp: float32 [1024], P('fsdp'), may hold values from -4 to 0
- ref_logp: float32 [1024], P('fsdp'), may hold values from -4 to 0
- seq_lengths: int32 [8, 4], P('fsdp'), may hold values from 1 to 64, 128 in all within a row
- pair_index: int32 [16, 2], P('fsdp'), may hold values from 0 to 31, as said below
- noise_flags: int32 [16], P('fsdp'), may hold values 0 or 1
Outputs:
- hidden: bfloat16 [1024, 15360], P('fsdp', 'tp')
- pair_loss: float32 [16], P('fsdp')
Inputs may be any that keep to these rules, and one draw needn't show every extreme that they name: `col_slots`: within each block row and tp shard the 15 entries are distinct and increasing, below 30. `seq_lengths`: each fsdp index's 4 lengths sum to 128. `pair_index`: every sequence number appears exactly once.
All inputs are finite; a program needn't handle non-finite values. No bound on the sum of `noise_flags` on one device may be relied on, other than what follows from the above.
Results may differ from a plain program's by a relative error of at most 0.0014.
Values may be sent and summed in bfloat16 or wider, within the bound.
No kernel may reach another device: no remote copies, remote signals or barrier semaphores. Data moves between devices by JAX's collectives and lax.ppermute only.
A program may use at most 128 MiB of HBM per device.

v0:
```python
import jax
import jax.numpy as jnp
from jax import lax
from jax.sharding import PartitionSpec as P

BLK = 128


beta_scale = 0.1
smooth_rate = 0.1


def shards(
    tokens,
    gate_packed,
    up_packed,
    col_slots,
    readout,
    base_logp,
    ref_logp,
    seq_lengths,
    pair_index,
    noise_flags,
):
    tok_rows = tokens.shape[0]
    block_size = BLK
    slot_count = col_slots.shape[1]
    panel_width = 2 * slot_count * block_size
    column_ids = jnp.arange(2 * slot_count, dtype=jnp.int32)
    gate_whole, up_whole = (
        lax.all_gather(gate_packed, "fsdp", axis=0, tiled=True),
        lax.all_gather(up_packed, "fsdp", axis=0, tiled=True),
    )
    row_count = col_slots.shape[0]
    all_place = (col_slots[:, :, None] == column_ids[None, None, :]).astype(jnp.bfloat16)

    def dense_panel(packed):
        blocks = packed.reshape(row_count, block_size, slot_count, block_size)
        widened = jnp.einsum(
            "rnjc,rjm->rnmc", blocks, all_place, preferred_element_type=jnp.bfloat16
        )
        return widened.reshape(row_count * block_size, panel_width)

    gate_sum = jnp.dot(tokens, dense_panel(gate_whole), preferred_element_type=jnp.float32)
    up_sum = jnp.dot(tokens, dense_panel(up_whole), preferred_element_type=jnp.float32)
    hidden = (jax.nn.silu(gate_sum) * up_sum).astype(jnp.bfloat16)
    partial_term = jnp.dot(hidden, readout, preferred_element_type=jnp.float32)
    lengths = seq_lengths[0]
    seq_ends = jnp.cumsum(lengths)
    seq_starts = seq_ends - lengths
    positions = jnp.arange(tok_rows, dtype=jnp.int32)
    member = (positions[None, :] >= seq_starts[:, None]) & (positions[None, :] < seq_ends[:, None])
    local_term = base_logp - ref_logp
    contrib = lax.psum(partial_term, "tp")
    seq_ratio = jnp.sum(
        jnp.where(member, (local_term + contrib)[None, :], jnp.float32(0.0)), axis=1
    )
    all_ratios = lax.all_gather(seq_ratio, "fsdp", axis=0, tiled=True)
    seq_ids = jnp.arange(all_ratios.shape[0], dtype=jnp.int32)
    chosen = jnp.sum(
        jnp.where(pair_index[:, 0:1] == seq_ids[None, :], all_ratios[None, :], jnp.float32(0.0)),
        axis=1,
    )
    rejected = jnp.sum(
        jnp.where(pair_index[:, 1:2] == seq_ids[None, :], all_ratios[None, :], jnp.float32(0.0)),
        axis=1,
    )
    sign_flip = 1.0 - 2.0 * noise_flags.astype(jnp.float32)
    margin = beta_scale * sign_flip * (chosen - rejected)
    pair_loss = -(1.0 - smooth_rate) * jax.nn.log_sigmoid(
        margin
    ) - smooth_rate * jax.nn.log_sigmoid(-margin)
    return (hidden, pair_loss)


def solution(mesh):
    in_specs = (
        P("fsdp", None),
        P("fsdp", "tp"),
        P("fsdp", "tp"),
        P(None, "tp"),
        P("tp"),
        P("fsdp"),
        P("fsdp"),
        P("fsdp", None),
        P("fsdp", None),
        P("fsdp"),
    )
    out_specs = (P("fsdp", "tp"), P("fsdp"))
    return jax.shard_map(shards, mesh=mesh, in_specs=in_specs, out_specs=out_specs, check_vma=False)
```

profile of v0, /device:TPU:0, one launch (start us, length us, event | category | flops | bytes accessed | tf_op | source)
XLA Modules:
  0.0 347.4 jit_solution(14619711805992807)
XLA Ops:
  7.2 0.7 all-gather.3.cloned.1.call-update
  8.0 0.7 all-gather.5.cloned.1.call-update
  8.7 0.8 copy.22
  9.4 0.7 reshape.59
  10.2 0.8 reduce-window.7
  11.0 1.2 dynamic-slice
  12.9 1.0 slice_reduce_fusion
  13.8 0.7 bitcast_subtract_fusion
  14.5 83.6 %all-gather.3.cloned.1.call-done = bf16[4096,1920]{1,0:T(8,128)(2,1)} async-done(((bf16[512,1920]{1,0:T(8,128)(2,1)}), bf16[4096,1920]{1,0:T(8,128)(2,1)}) %all-gather.3.cloned.1.call-update) | async-done | bytes 15728656 | tf_op jit(solution)/shard_map/all_gather | solution.py:31
  98.1 27.4 %reshape.61 = bf16[32,128,15,128]{3,2,1,0:T(8,128)(2,1)} reshape(bf16[4096,1920]{1,0:T(8,128)(2,1)} %all-gather.3.cloned.1.call-done) | data formatting | bytes 31457280 | tf_op jit(solution)/shard_map/reshape | solution.py:38
  125.4 21.3 %fusion.21 = bf16[32,30,128,128]{3,1,2,0:T(8,128)(2,1)} fusion(bf16[32,128,15,128]{3,2,1,0:T(8,128)(2,1)} %reshape.61, s32[32,15]{1,0:T(8,128)S(1)} %copy.22), kind=kOutput, calls=%fused_computation.14 | convolution fusion | flops 471873600 | bytes 47187840 | tf_op jit(solution)/shard_map/rnjc,rjm->rnmc/dot_general | solution.py:39
  146.7 38.7 %all-gather.5.cloned.1.call-done = bf16[4096,1920]{1,0:T(8,128)(2,1)} async-done(((bf16[512,1920]{1,0:T(8,128)(2,1)}), bf16[4096,1920]{1,0:T(8,128)(2,1)}) %all-gather.5.cloned.1.call-update) | async-done | bytes 15728656 | tf_op jit(solution)/shard_map/all_gather | solution.py:32
  185.4 27.2 %reshape.63 = bf16[32,128,15,128]{3,2,1,0:T(8,128)(2,1)} reshape(bf16[4096,1920]{1,0:T(8,128)(2,1)} %all-gather.5.cloned.1.call-done) | data formatting | bytes 31457280 | tf_op jit(solution)/shard_map/reshape | solution.py:38
  212.6 20.0 %fusion.19 = bf16[32,30,128,128]{3,1,2,0:T(8,128)(2,1)} fusion(bf16[32,128,15,128]{3,2,1,0:T(8,128)(2,1)} %reshape.63, s32[32,15]{1,0:T(8,128)S(1)} %copy.22), kind=kOutput, calls=%fused_computation.13 | convolution fusion | flops 471873600 | bytes 47187840 | tf_op jit(solution)/shard_map/rnjc,rjm->rnmc/dot_general | solution.py:39
  232.6 40.9 %fusion.6 = f32[128,3840]{0,1:T(8,128)} fusion(bf16[128,4096]{1,0:T(8,128)(2,1)S(1)} %copy-done, bf16[512,8,30,128]{3,2,1,0:T(8,128)(2,1)} %bitcast.48), kind=kOutput, calls=%fused_computation.6 | convolution fusion | flops 4026531840 | bytes 34471936 | tf_op jit(solution)/shard_map/dot_general | solution.py:44
  273.4 40.9 %fusion.15 = bf16[128,3840]{0,1:T(8,128)(2,1)S(1)} fusion(bf16[128,4096]{1,0:T(8,128)(2,1)S(1)} %copy-done, bf16[512,8,30,128]{3,2,1,0:T(8,128)(2,1)} %bitcast.49, f32[128,3840]{0,1:T(8,128)} %fusion.6), kind=kOutput, calls=%fused_computation.9 | convolution fusion | flops 4029480960 | bytes 35454976 | tf_op jit(solution)/shard_map/dot_general | solution.py:45
  314.3 1.3 copy.29
  315.6 0.2 convolution_bitcast_fusion
  315.9 11.7 %psum.7 = f32[128]{0:T(128)S(1)} all-reduce(f32[128]{0:T(128)S(1)} %convolution_bitcast_fusion), channel_id=1, replica_groups=mesh['fsdp'=8,'tp'=4] {'tp'}, use_global_device_ids=true, to_apply=%region_1.2 | all-reduce | flops 128 | bytes 1024 | tf_op jit(solution)/shard_map/psum | solution.py:54
  327.6 0.2 select_reduce_fusion
  327.8 0.2 dynamic-update-slice
  328.0 11.8 %all-reduce = f32[32]{0:T(128)S(1)} all-reduce(f32[32]{0:T(128)S(1)} %dynamic-update-slice), channel_id=1, replica_groups=mesh['fsdp'=8,'tp'=4] {'fsdp'}, use_global_device_ids=true, to_apply=%add | all-reduce | flops 32 | bytes 256
  339.8 0.2 fusion.27
  340.0 0.5 multiply_subtract_fusion
  (12 shorter events, 0.1 us)
Async XLA Ops:
  7.2 225.4 %copy-start = (bf16[128,4096]{1,0:T(8,128)(2,1)S(1)}, bf16[128,4096]{1,0:T(8,128)(2,1)}, u32[]{:S(2)}) copy-start(bf16[128,4096]{1,0:T(8,128)(2,1)} %param.10) | copy-start | bytes 3145732
  7.2 90.9 %all-gather.3.cloned.1.call-start = ((), (), s32[]{:S(2)}) async-start(), calls=%async_computation | async-start | bytes 17694720 | tf_op jit(solution)/shard_map/all_gather | solution.py:31
  7.9 177.5 %all-gather.5.cloned.1.call-start = ((), (), s32[]{:S(2)}) async-start(), calls=%async_computation.1 | async-start | bytes 17694720 | tf_op jit(solution)/shard_map/all_gather | solution.py:32
  273.4 54.1 %copy-start.1 = (f32[128]{0:T(128)S(1)}, f32[128]{0:T(128)}, u32[]{:S(2)}) copy-start(f32[128]{0:T(128)} %param.15) | copy-start | bytes 1540
  273.4 54.1 %copy-start.2 = (f32[128]{0:T(128)S(1)}, f32[128]{0:T(128)}, u32[]{:S(2)}) copy-start(f32[128]{0:T(128)} %param.16) | copy-start | bytes 1540
  273.4 66.6 %copy-start.3 = (s32[2]{0:T(128)S(1)}, s32[2]{0:T(128)}, u32[]{:S(2)}) copy-start(s32[2]{0:T(128)} %param.19) | copy-start | bytes 28
Sparse Core Ops, SparseCore 0:
  9.9 88.1 all-gather.2
  100.0 85.4 all-gather.4
where the time goes:
time: 349 us; the launch traced here: 347 us
  waiting for transfers between devices  124 us (36%)
  matrix products  123 us (35%)
  local copies, waits for them, and re-layouts  59.8 us (17%)
  blocking collectives  23.5 us (7%)
  between operations  14.7 us (4%)
    all_gather x1, waiting for transfers between devices, shards(): lax.all_gather(gate_packed, 'fsdp', axis=0, tiled=True)  83.6 us
    reshape x2, local copies, waits for them, and re-layouts, dense_panel(): blocks = packed.reshape(row_count, block_size, slot_count, block_size)  54.5 us
    dot_general x2, matrix products, dense_panel(): jnp.einsum('rnjc,rjm->rnmc', blocks, all_place, preferred_element_type=jn...  41.2 us
    dot_general x1, matrix products, shards(): jnp.dot(tokens, dense_panel(up_whole), preferred_element_type=jnp.float32)  40.9 us
    dot_general x1, matrix products, shards(): jnp.dot(tokens, dense_panel(gate_whole), preferred_element_type=jnp.float32)  40.9 us
    all_gather x1, waiting for transfers between devices, shards(): lax.all_gather(up_packed, 'fsdp', axis=0, tiled=True)  38.7 us
    unnamed x1, blocking collectives  11.8 us
    psum x1, blocking collectives, shards(): contrib = lax.psum(partial_term, 'tp')  11.7 us
  transfers between devices with their start and end apart: 2, of which 2 were waited for; matrix products, arithmetic and copies ran while one was open for 15% of the time, Pallas kernels for 0%

commit v1 on v0

v1 whole, which is shorter than its diff:
```python
import functools

import jax
import jax.numpy as jnp
from jax import lax
from jax.experimental import pallas as pl
from jax.experimental.pallas import tpu as pltpu
from jax.sharding import PartitionSpec as P

BLK = 128
CORE, X, Y = 1, 2, 4


beta_scale = 0.1
smooth_rate = 0.1


def swap(value, mask):
    return lax.ppermute(value, "fsdp", [(i, i ^ mask) for i in range(8)])


def slot_map(col_slots):
    slots = col_slots.shape[1]
    columns = jnp.arange(2 * slots, dtype=jnp.int32)
    hit = col_slots[:, :, None] == columns[None, None, :]
    number = jnp.arange(1, slots + 1, dtype=jnp.int32)[None, :, None]
    return jnp.sum(jnp.where(hit, number, 0), axis=1) - 1


def partial_kernel(chunks_ref, near_ref, slots_ref, own_tok, near_tok, *refs):
    sources, (own_out, near_out, panel, dense) = refs[:4], refs[4:]
    tokens, depth = own_tok.shape[0], sources[0].shape[0]
    rows = depth // BLK
    for s in range(4):
        own_at = pl.multiple_of(chunks_ref[s] * depth, depth)
        near_at = pl.multiple_of(near_ref[s] * depth, depth)
        panel[:tokens, s * depth : (s + 1) * depth] = own_tok[:, pl.ds(own_at, depth)]
        panel[tokens:, s * depth : (s + 1) * depth] = near_tok[:, pl.ds(near_at, depth)]

    @pl.loop(0, own_out.shape[1] // (2 * BLK))
    def _(pair):
        total = jnp.zeros((2 * tokens, 2 * BLK), jnp.float32)
        for s in range(4):
            for r in range(rows):
                for h in range(2):
                    slot = slots_ref[chunks_ref[s] * rows + r, 2 * pair + h]
                    at = pl.multiple_of(jnp.maximum(slot, 0) * BLK, BLK)
                    block = sources[s][r * BLK : (r + 1) * BLK, pl.ds(at, BLK)]
                    dense[s, r * BLK : (r + 1) * BLK, h * BLK : (h + 1) * BLK] = jnp.where(
                        slot >= 0, block, jnp.zeros_like(block)
                    )
            total += jnp.dot(
                panel[:, s * depth : (s + 1) * depth], dense[s], preferred_element_type=jnp.float32
            )
        at = pl.ds(pl.multiple_of(pair * 2 * BLK, 2 * BLK), 2 * BLK)
        own_out[:, at] = total[:tokens]
        near_out[:, at] = total[tokens:]


def partial_sums(chunks, near, slots, own_tok, near_tok, sources):
    tokens, depth = own_tok.shape[0], sources[0].shape[0]
    width = slots.shape[1] * BLK
    smem, vmem = pl.BlockSpec(memory_space=pltpu.SMEM), pl.BlockSpec(memory_space=pltpu.VMEM)
    out = jax.ShapeDtypeStruct((tokens, width), jnp.float32)
    return pl.pallas_call(
        partial_kernel,
        out_shape=(out, out),
        in_specs=[smem] * 3 + [vmem] * 6,
        out_specs=(vmem, vmem),
        scratch_shapes=[
            pltpu.VMEM((2 * tokens, 4 * depth), jnp.bfloat16),
            pltpu.VMEM((4, depth, 2 * BLK), jnp.bfloat16),
        ],
        compiler_params=pltpu.CompilerParams(vmem_limit_bytes=40 << 20),
        cost_estimate=pl.CostEstimate(
            flops=2 * 2 * tokens * 4 * depth * width,
            bytes_accessed=4 * depth * width + 2 * tokens * width * 4,
            transcendentals=0,
        ),
    )(chunks, near, slots, own_tok, near_tok, *sources)


def pair_losses(token_terms, seq_lengths, pair_index, noise_flags):
    lengths = seq_lengths[0]
    seq_ends = jnp.cumsum(lengths)
    seq_starts = seq_ends - lengths
    positions = jnp.arange(token_terms.shape[0], dtype=jnp.int32)
    member = (positions[None, :] >= seq_starts[:, None]) & (positions[None, :] < seq_ends[:, None])
    share = jnp.sum(jnp.where(member, token_terms[None, :], jnp.float32(0.0)), axis=1)
    n_fsdp, n_tp = lax.axis_size("fsdp"), lax.axis_size("tp")
    spread = jnp.broadcast_to(share, (n_fsdp * n_tp, share.shape[0]))
    shares = lax.all_to_all(spread, ("fsdp", "tp"), 0, 0, tiled=True)
    ratios = jnp.sum(shares.reshape(n_fsdp, n_tp, share.shape[0]), axis=1).reshape(-1)
    seq_ids = jnp.arange(ratios.shape[0], dtype=jnp.int32)
    picked = jnp.sum(
        jnp.where(pair_index[:, :, None] == seq_ids, ratios, jnp.float32(0.0)), axis=2
    )
    sign_flip = 1.0 - 2.0 * noise_flags.astype(jnp.float32)
    margin = beta_scale * sign_flip * (picked[:, 0] - picked[:, 1])
    return -(1.0 - smooth_rate) * jax.nn.log_sigmoid(margin) - smooth_rate * jax.nn.log_sigmoid(
        -margin
    )


def gathered_sums(tokens, gate_packed, up_packed, col_slots):
    slot_count, row_count = col_slots.shape[1], col_slots.shape[0]
    column_ids = jnp.arange(2 * slot_count, dtype=jnp.int32)
    place = (col_slots[:, :, None] == column_ids[None, None, :]).astype(jnp.bfloat16)

    def product(packed):
        whole = lax.all_gather(packed, "fsdp", axis=0, tiled=True)
        blocks = whole.reshape(row_count, BLK, slot_count, BLK)
        dense = jnp.einsum("rnjc,rjm->rnmc", blocks, place, preferred_element_type=jnp.bfloat16)
        dense = dense.reshape(row_count * BLK, 2 * slot_count * BLK)
        return jnp.dot(tokens, dense, preferred_element_type=jnp.float32)

    return product(gate_packed), product(up_packed)


def exchanged_sums(tokens, gate_packed, up_packed, col_slots):
    me = lax.axis_index("fsdp")
    x_at, y_at = (me >> 1) & 1, (me >> 2) & 1
    count = tokens.shape[0]
    quarters = tokens.reshape(count, 2, 2, -1)
    half = tokens.shape[1] // 2
    to_y = lax.dynamic_index_in_dim(quarters, 1 - y_at, 1, keepdims=False).reshape(count, half)
    to_x = lax.dynamic_index_in_dim(quarters, 1 - x_at, 2, keepdims=False).reshape(count, half)
    from_y, from_x = swap(to_y, Y), swap(to_x, X)
    gate_x, up_y = swap(gate_packed, X), swap(up_packed, Y)
    gate_sources = (gate_packed, swap(gate_packed, CORE), gate_x, swap(gate_x, CORE))
    up_sources = (up_packed, swap(up_packed, CORE), up_y, swap(up_y, CORE))
    slots = slot_map(col_slots)
    gate_chunks = me ^ jnp.array([0, CORE, X, X | CORE], jnp.int32)
    up_chunks = me ^ jnp.array([0, CORE, Y, Y | CORE], jnp.int32)
    gate_near = gate_chunks & 3
    up_near = ((up_chunks >> 1) & 2) | (up_chunks & 1)
    gate_own, gate_other = partial_sums(gate_chunks, gate_near, slots, tokens, from_y, gate_sources)
    up_own, up_other = partial_sums(up_chunks, up_near, slots, tokens, from_x, up_sources)
    gate_in = swap(gate_other.astype(jnp.float16), Y)
    up_in = swap(up_other.astype(jnp.float16), X)
    return gate_own + gate_in.astype(jnp.float32), up_own + up_in.astype(jnp.float32)


def shards(
    tokens,
    gate_packed,
    up_packed,
    col_slots,
    readout,
    base_logp,
    ref_logp,
    seq_lengths,
    pair_index,
    noise_flags,
):
    whole_blocks = gate_packed.shape[0] % BLK == 0
    sums = exchanged_sums if lax.axis_size("fsdp") == 8 and whole_blocks else gathered_sums
    gate_sum, up_sum = sums(tokens, gate_packed, up_packed, col_slots)
    hidden = (jax.nn.silu(gate_sum) * up_sum).astype(jnp.bfloat16)
    contrib = jnp.dot(hidden, readout, preferred_element_type=jnp.float32)
    local_term = jnp.where(lax.axis_index("tp") == 0, base_logp - ref_logp, jnp.float32(0.0))
    return hidden, pair_losses(local_term + contrib, seq_lengths, pair_index, noise_flags)


def solution(mesh):
    in_specs = (
        P("fsdp", None),
        P("fsdp", "tp"),
        P("fsdp", "tp"),
        P(None, "tp"),
        P("tp"),
        P("fsdp"),
        P("fsdp"),
        P("fsdp", None),
        P("fsdp", None),
        P("fsdp"),
    )
    out_specs = (P("fsdp", "tp"), P("fsdp"))
    return jax.shard_map(shards, mesh=mesh, in_specs=in_specs, out_specs=out_specs, check_vma=False)
```

time: 349 us -> 137 us (0.39)
  matrix products: 123 us -> 0.36 us
  waiting for transfers between devices: 124 us -> 71.6 us
  local copies, waits for them, and re-layouts: 59.8 us -> 12.2 us
  Pallas kernels: 0 us -> 22.8 us
  between operations: 14.7 us -> 0.89 us
  blocking collectives: 23.5 us -> 12.4 us
  starting transfers between devices: 0.08 us -> 10.1 us
  other arithmetic: 2.44 us -> 6.53 us
    dot_general x5 -> x1, matrix products: 123 us -> 0.36 us  [shards(): contrib = jnp.dot(hidden, readout, preferred_element_type=jnp.float32)]
    all_gather x2 -> x0, waiting for transfers between devices: 122 us -> none  [the longest x1 83.6 us: shards(): lax.all_gather(gate_packed, 'fsdp', axis=0, tiled=True)]
    ppermute x0 -> x10, waiting for transfers between devices: none -> 71.6 us  [swap(): return lax.ppermute(value, 'fsdp', [(i, i ^ mask) for i in range(8)])]
    reshape x2, local copies, waits for them, and re-layouts: 54.5 us -> 1.91 us  [the longest x1 1.83 us: exchanged_sums(): quarters = tokens.reshape(count, 2, 2, -1)]
    pallas_call x0 -> x2, Pallas kernels: none -> 22.8 us  [partial_sums(): pl.pallas_call(partial_kernel, out_shape=(out, out), in_specs=[smem] * 3...]
    all_to_all x0 -> x1, blocking collectives: none -> 12.4 us  [pair_losses(): shares = lax.all_to_all(spread, ('fsdp', 'tp'), 0, 0, tiled=True)]
    unnamed x1 -> x0, blocking collectives: 11.8 us -> none
    psum x1 -> x0, blocking collectives: 11.7 us -> none  [shards(): contrib = lax.psum(partial_term, 'tp')]
  transfers between devices with their start and end apart: 2 -> 10, of which waited for: 2 -> 5; matrix products, arithmetic and copies ran while one was open for 15% -> 8% of each run, Pallas kernels for 0% -> 17%
where the time goes in v1:
time: 137 us
  waiting for transfers between devices  71.6 us (52%)
  Pallas kernels  22.8 us (17%)
  blocking collectives  12.4 us (9%)
  local copies, waits for them, and re-layouts  12.2 us (9%)
  starting transfers between devices  10.1 us (7%)
  other arithmetic  6.53 us (5%)
    ppermute x10, waiting for transfers between devices, swap(): return lax.ppermute(value, 'fsdp', [(i, i ^ mask) for i in range(8)])  71.6 us
    pallas_call x2, Pallas kernels, partial_sums(): pl.pallas_call(partial_kernel, out_shape=(out, out), in_specs=[smem] * 3...  22.8 us
    all_to_all x1, blocking collectives, pair_losses(): shares = lax.all_to_all(spread, ('fsdp', 'tp'), 0, 0, tiled=True)  12.4 us
    ppermute x10, starting transfers between devices, swap(): return lax.ppermute(value, 'fsdp', [(i, i ^ mask) for i in range(8)])  10.1 us
    dynamic_slice x1, local copies, waits for them, and re-layouts, exchanged_sums(): lax.dynamic_index_in_dim(quarters, 1 - x_at, 2, keepdims=False)  4.96 us
    unnamed x37, local copies, waits for them, and re-layouts  4.95 us
    convert_element_type x1, other arithmetic, shards(): hidden = (jax.nn.silu(gate_sum) * up_sum).astype(jnp.bfloat16)  2.81 us
  transfers between devices with their start and end apart: 10, of which 5 were waited for; matrix products, arithmetic and copies ran while one was open for 8% of the time, Pallas kernels for 17%

profile of v1, /device:TPU:0, one launch (start us, length us, event | category | flops | bytes accessed | tf_op | source)
XLA Modules:
  0.0 136.9 jit_solution(18252704969948093762)
XLA Ops:
  0.6 3.0 %collective-permute-start.2 = (bf16[512,1920]{1,0:T(8,128)(2,1)}, bf16[512,1920]{1,0:T(8,128)(2,1)S(1)}, u32[]{:S(2)}, u32[]{:S(2)}) collective-permute-start(bf16[512,1920]{1,0:T(8,128)(2,1)} %refs_0_.2), channel_id=1, source_target_pairs={{0,8},{4,12},{8,0},{12,4},{16,24},{20,28},{24,16},{28,20},{1,9},{5... | collective-permute-start | bytes 5898248 | tf_op jit(solution)/shard_map/ppermute | solution.py:19
  3.6 1.5 %collective-permute-start.7 = (bf16[512,1920]{1,0:T(8,128)(2,1)}, bf16[512,1920]{1,0:T(8,128)(2,1)}, u32[]{:S(2)}, u32[]{:S(2)}) collective-permute-start(bf16[512,1920]{1,0:T(8,128)(2,1)} %refs_0_.3), channel_id=1, source_target_pairs={{0,16},{4,20},{8,24},{12,28},{16,0},{20,4},{24,8},{28,12},{1,17},{... | collective-permute-start | bytes 5898248 | tf_op jit(solution)/shard_map/ppermute | solution.py:19
  5.2 41.5 %collective-permute-done.2.refs_2_ = bf16[512,1920]{1,0:T(8,128)(2,1)S(1)} collective-permute-done((bf16[512,1920]{1,0:T(8,128)(2,1)}, bf16[512,1920]{1,0:T(8,128)(2,1)S(1)}, u32[]{:S(2)}, u32[]{:S(2)}) %collective-permute-start.2) | collective-permute-done | bytes 1966112 | tf_op jit(solution)/shard_map/ppermute | solution.py:19
  47.2 1.1 collective-permute-done.7.refs_2_
  48.2 1.8 %reshape.61 = bf16[128,2,2,1024]{3,2,1,0:T(2,128)(2,1)S(1)} reshape(bf16[128,4096]{1,0:T(8,128)(2,1)} %own_tok.3) | data formatting | bytes 2097152 | tf_op jit(solution)/shard_map/reshape | solution.py:124
  50.1 1.0 copy-done.6
  51.5 0.9 copy.37
  52.4 1.5 %collective-permute-start = (bf16[128,2048]{1,0:T(8,128)(2,1)}, bf16[128,2048]{1,0:T(8,128)(2,1)S(1)}, u32[]{:S(2)}, u32[]{:S(2)}) collective-permute-start(bf16[128,2048]{1,0:T(8,128)(2,1)} %bitcast.9), channel_id=1, source_target_pairs={{0,16},{4,20},{8,24},{12,28},{16,0},{20,4},{24,8},{28,12},{1,17},{... | collective-permute-start | bytes 1572872 | tf_op jit(solution)/shard_map/ppermute | solution.py:19
  53.9 5.0 %dynamic-slice_reduce_fusion = bf16[128,2,1024]{2,1,0:T(2,128)(2,1)S(1)} fusion(bf16[128,2,2,1024]{3,2,1,0:T(2,128)(2,1)} %copy-done.6, s32[]{:T(128)S(6)} %select_n.38), kind=kLoop, calls=%fused_computation.3 | loop fusion | bytes 1048580 | tf_op jit(solution)/shard_map/jit(dynamic_index_in_dim)/dynamic_slice | solution.py:127
  59.2 7.8 %collective-permute-done.near_tok = bf16[128,2048]{1,0:T(8,128)(2,1)S(1)} collective-permute-done((bf16[128,2048]{1,0:T(8,128)(2,1)}, bf16[128,2048]{1,0:T(8,128)(2,1)S(1)}, u32[]{:S(2)}, u32[]{:S(2)}) %collective-permute-start) | collective-permute-done | bytes 524320 | tf_op jit(solution)/shard_map/ppermute | solution.py:19
  66.9 0.7 collective-permute-start.5
  67.7 1.5 %copy-done.2 = bf16[512,1920]{1,0:T(8,128)(2,1)S(1)} copy-done((bf16[512,1920]{1,0:T(8,128)(2,1)S(1)}, bf16[512,1920]{1,0:T(8,128)(2,1)}, u32[]{:S(2)}) %copy-start.2) | copy-done | bytes 1966104
  69.2 11.2 %shard_map.131 = (f32[128,3840]{1,0:T(8,128)S(1)}, f32[128,3840]{1,0:T(8,128)S(1)}) custom-call(s32[4]{0:T(128)S(1)} %get-tuple-element.12.chunks_ref, s32[4]{0:T(128)S(1)} %get-tuple-element.13.near_ref, s32[32,30]{1,0:T(8,128)S(1)} %broadcast_add_fusion.slots_ref, bf16[128,4096]{1,0:T(8,128)(2,1)S(1)} %copy-done.1, ...), custom_call_target="tpu_custom_call" | custom-call | flops 4026531840 | bytes 11796480 | tf_op jit(solution)/shard_map/pallas_call | solution.py:65
  80.4 1.1 convert_element_type.18
  81.5 1.5 %collective-permute-start.4 = (f16[128,3840]{1,0:T(8,128)(2,1)}, f16[128,3840]{1,0:T(8,128)(2,1)}, u32[]{:S(2)}, u32[]{:S(2)}) collective-permute-start(f16[128,3840]{1,0:T(8,128)(2,1)} %convert_element_type.18), channel_id=1, source_target_pairs={{0,16},{4,20},{8,24},{12,28},{16,0},{20,4},{24,8},{28,12},{1,17},{... | collective-permute-start | bytes 2949128 | tf_op jit(solution)/shard_map/ppermute | solution.py:19
  83.0 11.6 %shard_map.132 = (f32[128,3840]{1,0:T(8,128)S(1)}, f32[128,3840]{1,0:T(8,128)S(1)}) custom-call(s32[4]{0:T(128)S(1)} %get-tuple-element.11.chunks_ref, s32[4]{0:T(128)S(1)} %get-tuple-element.10.near_ref, s32[32,30]{1,0:T(8,128)S(1)} %broadcast_add_fusion.slots_ref, bf16[128,4096]{1,0:T(8,128)(2,1)S(1)} %copy-done.1, ...), custom_call_target="tpu_custom_call" | custom-call | flops 4026531840 | bytes 11796480 | tf_op jit(solution)/shard_map/pallas_call | solution.py:65
  94.7 1.2 convert_element_type.20
  96.3 1.4 collective-permute-start.9
  97.8 6.9 %collective-permute-done.4 = f16[128,3840]{1,0:T(8,128)(2,1)} collective-permute-done((f16[128,3840]{1,0:T(8,128)(2,1)}, f16[128,3840]{1,0:T(8,128)(2,1)}, u32[]{:S(2)}, u32[]{:S(2)}) %collective-permute-start.4) | collective-permute-done | bytes 983072 | tf_op jit(solution)/shard_map/ppermute | solution.py:19
  104.7 14.4 %collective-permute-done.9 = f16[128,3840]{1,0:T(8,128)(2,1)S(1)} collective-permute-done((f16[128,3840]{1,0:T(8,128)(2,1)}, f16[128,3840]{1,0:T(8,128)(2,1)S(1)}, u32[]{:S(2)}, u32[]{:S(2)}) %collective-permute-start.9) | collective-permute-done | bytes 983072 | tf_op jit(solution)/shard_map/ppermute | solution.py:19
  119.1 0.9 copy-done.8
  120.1 2.8 %multiply_convert_fusion = bf16[128,3840]{1,0:T(8,128)(2,1)S(1)} fusion(f32[128,3840]{1,0:T(8,128)} %copy-done, f16[128,3840]{1,0:T(8,128)(2,1)} %copy-done.8, f32[128,3840]{1,0:T(8,128)S(1)} %get-tuple-element.6, f16[128,3840]{1,0:T(8,128)(2,1)} %collective-permute-done.4), kind=kLoop, calls=%fused_computation | loop fusion | flops 4915200 | bytes 6881280 | tf_op jit(solution)/shard_map/convert_element_type | solution.py:159
  123.5 12.4 %all_to_all.6 = f32[32,1,4]{2,1,0:T(1,128)S(1)} all-to-all(f32[32,1,4]{2,1,0:T(1,128)S(1)} %broadcast_in_dim.54), channel_id=1, replica_groups=mesh['fsdp'=8,'tp'=4] {'fsdp','tp'}, dimensions={0} | all-to-all | bytes 1024 | tf_op jit(solution)/shard_map/all_to_all | solution.py:92
  136.4 0.5 multiply_subtract_fusion
  (57 shorter events, 2.8 us)
Async XLA Ops:
  0.6 46.0 %collective-permute-start.2 = (bf16[512,1920]{1,0:T(8,128)(2,1)}, bf16[512,1920]{1,0:T(8,128)(2,1)S(1)}, u32[]{:S(2)}, u32[]{:S(2)}) collective-permute-start(bf16[512,1920]{1,0:T(8,128)(2,1)} %refs_0_.2), channel_id=1, source_target_pairs={{0,8},{4,12},{8,0},{12,4},{16,24},{20,28},{24,16},{28,20},{1,9},{5... | collective-permute-start | bytes 5898248 | tf_op jit(solution)/shard_map/ppermute | solution.py:19
  3.6 44.6 %collective-permute-start.7 = (bf16[512,1920]{1,0:T(8,128)(2,1)}, bf16[512,1920]{1,0:T(8,128)(2,1)}, u32[]{:S(2)}, u32[]{:S(2)}) collective-permute-start(bf16[512,1920]{1,0:T(8,128)(2,1)} %refs_0_.3), channel_id=1, source_target_pairs={{0,16},{4,20},{8,24},{12,28},{16,0},{20,4},{24,8},{28,12},{1,17},{... | collective-permute-start | bytes 5898248 | tf_op jit(solution)/shard_map/ppermute | solution.py:19
  5.2 62.5 %collective-permute-start.1 = (bf16[512,1920]{1,0:T(8,128)(2,1)}, bf16[512,1920]{1,0:T(8,128)(2,1)}, u32[]{:S(2)}, u32[]{:S(2)}) collective-permute-start(bf16[512,1920]{1,0:T(8,128)(2,1)} %refs_0_.2), channel_id=1, source_target_pairs={{0,4},{4,0},{8,12},{12,8},{16,20},{20,16},{24,28},{28,24},{1,5},{5... | collective-permute-start | bytes 5898248 | tf_op jit(solution)/shard_map/ppermute | solution.py:19
  46.7 5.7 %copy-start.4 = (bf16[512,1920]{1,0:T(8,128)(2,1)}, bf16[512,1920]{1,0:T(8,128)(2,1)S(1)}, u32[]{:S(2)}) copy-start(bf16[512,1920]{1,0:T(8,128)(2,1)S(1)} %collective-permute-done.2.refs_2_) | copy-start | bytes 5898244
  46.7 21.0 %collective-permute-start.3 = (bf16[512,1920]{1,0:T(8,128)(2,1)S(1)}, bf16[512,1920]{1,0:T(8,128)(2,1)}, u32[]{:S(2)}, u32[]{:S(2)}) collective-permute-start(bf16[512,1920]{1,0:T(8,128)(2,1)S(1)} %collective-permute-done.2.refs_2_), channel_id=1, source_target_pairs={{0,4},{4,0},{8,12},{12,8},{16,20},{20,16},{24,28},{28,24},{1,5},{5... | collective-permute-start | bytes 5898248 | tf_op jit(solution)/shard_map/ppermute | solution.py:19
  46.7 36.3 %collective-permute-start.6 = (bf16[512,1920]{1,0:T(8,128)(2,1)}, bf16[512,1920]{1,0:T(8,128)(2,1)}, u32[]{:S(2)}, u32[]{:S(2)}) collective-permute-start(bf16[512,1920]{1,0:T(8,128)(2,1)} %refs_0_.3), channel_id=1, source_target_pairs={{0,4},{4,0},{8,12},{12,8},{16,20},{20,16},{24,28},{28,24},{1,5},{5... | collective-permute-start | bytes 5898248 | tf_op jit(solution)/shard_map/ppermute | solution.py:19
  48.2 34.8 %collective-permute-start.8 = (bf16[512,1920]{1,0:T(8,128)(2,1)}, bf16[512,1920]{1,0:T(8,128)(2,1)}, u32[]{:S(2)}, u32[]{:S(2)}) collective-permute-start(bf16[512,1920]{1,0:T(8,128)(2,1)} %collective-permute-done.7.refs_2_), channel_id=1, source_target_pairs={{0,4},{4,0},{8,12},{12,8},{16,20},{20,16},{24,28},{28,24},{1,5},{5... | collective-permute-start | bytes 5898248 | tf_op jit(solution)/shard_map/ppermute | solution.py:19
  51.4 7.6 %copy-start.9 = (s32[32,15]{0,1:T(8,128)S(1)}, s32[32,15]{0,1:T(8,128)}, u32[]{:S(2)}) copy-start(s32[32,15]{0,1:T(8,128)} %param.15) | copy-start | bytes 5764
  51.4 16.2 %copy-start.14 = (s32[4]{0:T(128)S(1)}, s32[4]{0:T(128)}, u32[]{:S(2)}) copy-start(s32[4]{0:T(128)} %constant.56.clone) | copy-start | bytes 52
  51.5 16.2 %copy-start.1 = (bf16[128,4096]{1,0:T(8,128)(2,1)S(1)}, bf16[128,4096]{1,0:T(8,128)(2,1)}, u32[]{:S(2)}) copy-start(bf16[128,4096]{1,0:T(8,128)(2,1)} %own_tok.3) | copy-start | bytes 3145732
  52.4 14.5 %collective-permute-start = (bf16[128,2048]{1,0:T(8,128)(2,1)}, bf16[128,2048]{1,0:T(8,128)(2,1)S(1)}, u32[]{:S(2)}, u32[]{:S(2)}) collective-permute-start(bf16[128,2048]{1,0:T(8,128)(2,1)} %bitcast.9), channel_id=1, source_target_pairs={{0,16},{4,20},{8,24},{12,28},{16,0},{20,4},{24,8},{28,12},{1,17},{... | collective-permute-start | bytes 1572872 | tf_op jit(solution)/shard_map/ppermute | solution.py:19
  53.9 13.8 %copy-start.5 = (bf16[512,1920]{1,0:T(8,128)(2,1)S(1)}, bf16[512,1920]{1,0:T(8,128)(2,1)}, u32[]{:S(2)}) copy-start(bf16[512,1920]{1,0:T(8,128)(2,1)} %copy-done.4) | copy-start | bytes 5898244
  66.9 16.1 %collective-permute-start.5 = (bf16[128,2048]{1,0:T(8,128)(2,1)S(1)}, bf16[128,2048]{1,0:T(8,128)(2,1)S(1)}, u32[]{:S(2)}, u32[]{:S(2)}) collective-permute-start(bf16[128,2048]{1,0:T(8,128)(2,1)S(1)} %bitcast.21), channel_id=1, source_target_pairs={{0,8},{4,12},{8,0},{12,4},{16,24},{20,28},{24,16},{28,20},{1,9},{5... | collective-permute-start | bytes 1572872 | tf_op jit(solution)/shard_map/ppermute | solution.py:19
  80.4 2.6 %copy-start.3 = (bf16[512,1920]{1,0:T(8,128)(2,1)S(1)}, bf16[512,1920]{1,0:T(8,128)(2,1)}, u32[]{:S(2)}) copy-start(bf16[512,1920]{1,0:T(8,128)(2,1)} %refs_0_.3) | copy-start | bytes 5898244
  81.5 23.2 %collective-permute-start.4 = (f16[128,3840]{1,0:T(8,128)(2,1)}, f16[128,3840]{1,0:T(8,128)(2,1)}, u32[]{:S(2)}, u32[]{:S(2)}) collective-permute-start(f16[128,3840]{1,0:T(8,128)(2,1)} %convert_element_type.18), channel_id=1, source_target_pairs={{0,16},{4,20},{8,24},{12,28},{16,0},{20,4},{24,8},{28,12},{1,17},{... | collective-permute-start | bytes 2949128 | tf_op jit(solution)/shard_map/ppermute | solution.py:19
  94.6 1.6 %copy-start = (f32[128,3840]{1,0:T(8,128)}, f32[128,3840]{1,0:T(8,128)S(1)}, u32[]{:S(2)}) copy-start(f32[128,3840]{1,0:T(8,128)S(1)} %get-tuple-element.8) | copy-start | bytes 5898244
  94.7 3.0 %copy-start.10 = (bf16[3840]{0:T(1024)(128)(2,1)S(1)}, bf16[3840]{0:T(1024)(128)(2,1)}, u32[]{:S(2)}) copy-start(bf16[3840]{0:T(1024)(128)(2,1)} %param.16) | copy-start | bytes 23044
  94.7 3.0 %copy-start.15 = (s32[1,4]{1,0:T(1,128)S(1)}, s32[1,4]{1,0:T(1,128)}, u32[]{:S(2)}) copy-start(s32[1,4]{1,0:T(1,128)} %param.19) | copy-start | bytes 52
  96.3 22.8 %collective-permute-start.9 = (f16[128,3840]{1,0:T(8,128)(2,1)}, f16[128,3840]{1,0:T(8,128)(2,1)S(1)}, u32[]{:S(2)}, u32[]{:S(2)}) collective-permute-start(f16[128,3840]{1,0:T(8,128)(2,1)} %convert_element_type.20), channel_id=1, source_target_pairs={{0,8},{4,12},{8,0},{12,4},{16,24},{20,28},{24,16},{28,20},{1,9},{5... | collective-permute-start | bytes 2949128 | tf_op jit(solution)/shard_map/ppermute | solution.py:19
  120.0 2.8 %copy-start.12 = (f32[128]{0:T(128)S(1)}, f32[128]{0:T(128)}, u32[]{:S(2)}) copy-start(f32[128]{0:T(128)} %param.17) | copy-start | bytes 1540
  120.0 2.8 %copy-start.13 = (f32[128]{0:T(128)S(1)}, f32[128]{0:T(128)}, u32[]{:S(2)}) copy-start(f32[128]{0:T(128)} %param.18) | copy-start | bytes 1540
  120.0 16.0 %copy-start.11 = (s32[2,2]{1,0:T(2,128)S(1)}, s32[2,2]{1,0:T(2,128)}, u32[]{:S(2)}) copy-start(s32[2,2]{1,0:T(2,128)} %param.20) | copy-start | bytes 52
  120.1 16.3 %copy-start.16 = (s32[2]{0:T(128)S(1)}, s32[2]{0:T(128)}, u32[]{:S(2)}) copy-start(s32[2]{0:T(128)} %param.21) | copy-start | bytes 28
  122.9 14.0 %copy-start.7 = (bf16[128,3840]{1,0:T(8,128)(2,1)}, bf16[128,3840]{1,0:T(8,128)(2,1)S(1)}, u32[]{:S(2)}) copy-start(bf16[128,3840]{1,0:T(8,128)(2,1)S(1)} %multiply_convert_fusion) | copy-start | bytes 2949124
  (3 other events, 3.5 us)

commit v2 on v1

v2 whole, which is shorter than its diff:
```python
import functools

import jax
import jax.numpy as jnp
from jax import lax
from jax.experimental import pallas as pl
from jax.experimental.pallas import tpu as pltpu
from jax.sharding import PartitionSpec as P

BLK = 128
EARLY_VMEM, LATE_VMEM = 24 << 20, 12 << 20
CORE, X, Y = 1, 2, 4


beta_scale = 0.1
smooth_rate = 0.1


def swap(value, core0, core1):
    return lax.ppermute(
        value, "fsdp", [(i, i ^ (core1 if i & CORE else core0)) for i in range(8)]
    )


SMEM, VMEM, ANY = (
    pl.BlockSpec(memory_space=pltpu.SMEM),
    pl.BlockSpec(memory_space=pltpu.VMEM),
    pl.BlockSpec(memory_space=pl.ANY),
)


def places():
    me, plane = lax.axis_index("fsdp"), lax.axis_index("tp") & 1
    core, x_at, y_at = me & 1, (me >> 1) & 1, (me >> 2) & 1
    on_gate = core == 0
    far = me ^ jnp.where(on_gate, X, Y)
    straight = jnp.where(on_gate, x_at, y_at) == plane
    return [me, me ^ CORE, far, far ^ CORE], [straight, straight, ~straight, ~straight]


def find_slots(slot_at, col_slots, block_row, count, at_row):
    for r in range(count):
        for column in range(2 * col_slots.shape[1]):
            slot_at[at_row + r, column] = -1
        for slot in range(col_slots.shape[1]):
            slot_at[at_row + r, col_slots[block_row + r, slot]] = slot


def fill_dense(dense, weights, slot_at, at_row, column):
    for r in range(weights.shape[0] // BLK):
        for h in range(dense.shape[1] // BLK):
            slot = slot_at[at_row + r, column + h]
            at = pl.multiple_of(jnp.maximum(slot, 0) * BLK, BLK)
            block = weights[r * BLK : (r + 1) * BLK, pl.ds(at, BLK)]
            rows = slice((at_row + r) * BLK, (at_row + r + 1) * BLK)
            dense[rows, h * BLK : (h + 1) * BLK] = jnp.where(slot >= 0, block, jnp.zeros_like(block))


def early_kernel(
    col_slots, own, beside, direct, passed, mine, low, high, first,
    total, later, panel, weights, dense, slot_at, sems,
):
    depth, split = mine.shape[0], low.shape[1]
    rows = depth // BLK

    @pl.when(pl.program_id(0) == 0)
    def _():
        copies = [
            pltpu.make_async_copy(mine, weights.at[0], sems.at[0]),
            pltpu.make_async_copy(low, weights.at[1, :, :split], sems.at[1]),
            pltpu.make_async_copy(high, weights.at[1, :, split:], sems.at[2]),
            pltpu.make_async_copy(first, weights.at[2], sems.at[3]),
        ]
        for copy in copies:
            copy.start()
        count = own.shape[0]
        chunks, straight = places()
        for s in range(4):
            wide = pl.ds(pl.multiple_of(chunks[s] * depth, depth), depth)
            near = pl.ds(pl.multiple_of((chunks[s] & 1) * depth, depth), depth)
            groups = [
                own[:, wide],
                beside[:, wide],
                jnp.where(straight[s], direct[:, near], passed[:, near]),
            ]
            for group, start in zip(groups, (0, count, 2 * count)):
                at = slice(start, start + group.shape[0])
                if s < 3:
                    panel[at, s * depth : (s + 1) * depth] = group
                else:
                    later[at, :] = group
        for s in range(3):
            find_slots(slot_at, col_slots, chunks[s] * rows, rows, s * rows)
        for copy in copies:
            copy.wait()

    column = dense.shape[1] // BLK * pl.program_id(0)
    for s in range(3):
        fill_dense(dense, weights.at[s], slot_at, s * rows, column)
    total[...] = jnp.dot(panel[...], dense[...], preferred_element_type=jnp.float32)


def early_sums(col_slots, tokens, weights):
    count, (depth, width) = 4 * tokens[0].shape[0], weights[0].shape
    columns = 2 * col_slots.shape[1]
    step = 3 * 2 * BLK if columns % 6 == 0 else 2 * BLK
    return pl.pallas_call(
        early_kernel,
        grid=(columns * BLK // step,),
        out_shape=(
            jax.ShapeDtypeStruct((count, columns * BLK), jnp.float32),
            jax.ShapeDtypeStruct((count, depth), jnp.bfloat16),
        ),
        in_specs=[SMEM] + [VMEM] * 4 + [ANY] * 4,
        out_specs=(pl.BlockSpec((count, step), lambda n: (0, n)), VMEM),
        scratch_shapes=[
            pltpu.VMEM((count, 3 * depth), jnp.bfloat16),
            pltpu.VMEM((3, depth, width), jnp.bfloat16),
            pltpu.VMEM((3 * depth, step), jnp.bfloat16),
            pltpu.SMEM((3 * depth // BLK, columns), jnp.int32),
            pltpu.SemaphoreType.DMA((4,)),
        ],
        compiler_params=pltpu.CompilerParams(vmem_limit_bytes=EARLY_VMEM),
        cost_estimate=pl.CostEstimate(
            flops=2 * count * 3 * depth * columns * BLK,
            bytes_accessed=3 * depth * width * 2 + count * columns * BLK * 4,
            transcendentals=0,
        ),
    )(col_slots, *tokens, *weights)


def late_kernel(first_pair, col_slots, panel, early, *refs):
    parts, (mine, beside, near, weights, dense, slot_at, sems) = refs[:-7], refs[-7:]
    depth = weights.shape[0]
    rows = depth // BLK

    @pl.when(pl.program_id(0) == 0)
    def _():
        copies, start = [], 0
        for i, part in enumerate(parts):
            stop = start + part.shape[1]
            copies.append(pltpu.make_async_copy(part, weights.at[:, start:stop], sems.at[i]))
            start = stop
        for copy in copies:
            copy.start()
        find_slots(slot_at, col_slots, places()[0][3] * rows, rows, 0)
        for copy in copies:
            copy.wait()

    fill_dense(dense, weights, slot_at, 0, 2 * (first_pair + pl.program_id(0)))
    total = early[...] + jnp.dot(panel[...], dense[...], preferred_element_type=jnp.float32)
    count = mine.shape[0]
    mine[...] = total[:count]
    beside[...] = total[count : 2 * count]
    near[...] = total[2 * count :]


def late_sums(first_pair, pairs, col_slots, panel, early, parts):
    count, depth = panel.shape
    width = sum(part.shape[1] for part in parts)
    out_rows = (count // 4, count // 4, count // 2)
    return pl.pallas_call(
        functools.partial(late_kernel, first_pair),
        grid=(pairs,),
        out_shape=[
            jax.ShapeDtypeStruct((rows, pairs * 2 * BLK), jnp.float32) for rows in out_rows
        ],
        in_specs=[SMEM, VMEM, pl.BlockSpec((count, 2 * BLK), lambda n: (0, first_pair + n))]
        + [ANY] * len(parts),
        out_specs=[pl.BlockSpec((rows, 2 * BLK), lambda n: (0, n)) for rows in out_rows],
        scratch_shapes=[
            pltpu.VMEM((depth, width), jnp.bfloat16),
            pltpu.VMEM((depth, 2 * BLK), jnp.bfloat16),
            pltpu.SMEM((depth // BLK, 2 * col_slots.shape[1]), jnp.int32),
            pltpu.SemaphoreType.DMA((len(parts),)),
        ],
        compiler_params=pltpu.CompilerParams(vmem_limit_bytes=LATE_VMEM),
        cost_estimate=pl.CostEstimate(
            flops=2 * count * depth * pairs * 2 * BLK,
            bytes_accessed=depth * width * 2 + 2 * count * pairs * 2 * BLK * 4,
            transcendentals=0,
        ),
    )(col_slots, panel, early, *parts)


def pair_losses(token_terms, seq_lengths, pair_index, noise_flags):
    lengths = seq_lengths[0]
    seq_ends = jnp.cumsum(lengths)
    seq_starts = seq_ends - lengths
    positions = jnp.arange(token_terms.shape[0], dtype=jnp.int32)
    member = (positions[None, :] >= seq_starts[:, None]) & (positions[None, :] < seq_ends[:, None])
    share = jnp.sum(jnp.where(member, token_terms[None, :], jnp.float32(0.0)), axis=1)
    n_fsdp, n_tp = lax.axis_size("fsdp"), lax.axis_size("tp")
    spread = jnp.broadcast_to(share, (n_fsdp * n_tp, share.shape[0]))
    shares = lax.all_to_all(spread, ("fsdp", "tp"), 0, 0, tiled=True)
    ratios = jnp.sum(shares.reshape(n_fsdp, n_tp, share.shape[0]), axis=1).reshape(-1)
    seq_ids = jnp.arange(ratios.shape[0], dtype=jnp.int32)
    picked = jnp.sum(
        jnp.where(pair_index[:, :, None] == seq_ids, ratios, jnp.float32(0.0)), axis=2
    )
    sign_flip = 1.0 - 2.0 * noise_flags.astype(jnp.float32)
    margin = beta_scale * sign_flip * (picked[:, 0] - picked[:, 1])
    return -(1.0 - smooth_rate) * jax.nn.log_sigmoid(margin) - smooth_rate * jax.nn.log_sigmoid(
        -margin
    )


def gathered_parts(tokens, gate_packed, up_packed, col_slots):
    slot_count, row_count = col_slots.shape[1], col_slots.shape[0]
    column_ids = jnp.arange(2 * slot_count, dtype=jnp.int32)
    place = (col_slots[:, :, None] == column_ids[None, None, :]).astype(jnp.bfloat16)

    def product(packed):
        whole = lax.all_gather(packed, "fsdp", axis=0, tiled=True)
        blocks = whole.reshape(row_count, BLK, slot_count, BLK)
        dense = jnp.einsum("rnjc,rjm->rnmc", blocks, place, preferred_element_type=jnp.bfloat16)
        dense = dense.reshape(row_count * BLK, 2 * slot_count * BLK)
        return jnp.dot(tokens, dense, preferred_element_type=jnp.float32)

    return [(product(gate_packed), product(up_packed))]


def exchanged_parts(tokens, gate_packed, up_packed, col_slots):
    me, plane = lax.axis_index("fsdp"), lax.axis_index("tp") & 1
    core, x_at, y_at = me & 1, (me >> 1) & 1, (me >> 2) & 1
    on_gate = core == 0
    slot_count = col_slots.shape[1]
    third = 2 * slot_count // 3
    quarter = tokens.shape[1] // 4

    for_gate = lax.dynamic_slice_in_dim(tokens, (2 * (1 - y_at) + plane) * quarter, quarter, 1)
    for_up = lax.dynamic_slice_in_dim(tokens, (2 * plane + 1 - x_at) * quarter, quarter, 1)
    same = swap(jnp.where(on_gate, for_gate, for_up), Y, X)
    cross = swap(jnp.where(on_gate, for_up, for_gate), X | CORE, Y | CORE)
    gate_after, up_after, same, cross = lax.optimization_barrier(
        (gate_packed, up_packed, same, cross)
    )
    direct = jnp.concatenate([same, cross])
    passed = lax.ppermute(direct, "tp", [(i, i ^ 1) for i in range(lax.axis_size("tp"))])
    beside = swap(tokens, CORE, CORE)

    split = third * BLK
    low = swap(jnp.where(on_gate, up_packed[:, :split], gate_packed[:, :split]), CORE, CORE)
    high = swap(jnp.where(on_gate, up_packed[:, split:], gate_packed[:, split:]), CORE, CORE)
    mine = jnp.where(on_gate, gate_after, up_after)
    first = swap(mine, X, Y)
    far_low, far_high = swap(low, X, Y), swap(high, X, Y)

    early, panel = early_sums(col_slots, (tokens, beside, direct, passed), (mine, low, high, first))
    parts = []
    for n in range(3):
        sources = (far_low,) if n == 0 else (far_low, far_high)
        own, other, near = late_sums(
            n * third // 2, third // 2, col_slots, panel, early, sources
        )
        count = own.shape[0]
        near = near.astype(jnp.float16)
        own = own + swap(near[:count], Y, X).astype(jnp.float32)
        other = swap(other, CORE, CORE) + swap(near[count:], Y | CORE, X | CORE).astype(jnp.float32)
        parts.append((jnp.where(on_gate, own, other), jnp.where(on_gate, other, own)))
    return parts


def shards(
    tokens,
    gate_packed,
    up_packed,
    col_slots,
    readout,
    base_logp,
    ref_logp,
    seq_lengths,
    pair_index,
    noise_flags,
):
    whole = gate_packed.shape[0] % BLK == 0 and col_slots.shape[1] % 3 == 0
    by_core = lax.axis_size("fsdp") == 8 and lax.axis_size("tp") % 2 == 0 and whole
    sums = exchanged_parts if by_core else gathered_parts
    hiddens, contrib, done = [], 0.0, 0
    for gate_sum, up_sum in sums(tokens, gate_packed, up_packed, col_slots):
        hidden = (jax.nn.silu(gate_sum) * up_sum).astype(jnp.bfloat16)
        columns = slice(done, done + hidden.shape[1])
        contrib += jnp.dot(hidden, readout[columns], preferred_element_type=jnp.float32)
        hiddens.append(hidden)
        done = columns.stop
    hidden = jnp.concatenate(hiddens, axis=1)
    local_term = jnp.where(lax.axis_index("tp") == 0, base_logp - ref_logp, jnp.float32(0.0))
    return hidden, pair_losses(local_term + contrib, seq_lengths, pair_index, noise_flags)


def solution(mesh):
    in_specs = (
        P("fsdp", None),
        P("fsdp", "tp"),
        P("fsdp", "tp"),
        P(None, "tp"),
        P("tp"),
        P("fsdp"),
        P("fsdp"),
        P("fsdp", None),
        P("fsdp", None),
        P("fsdp"),
    )
    out_specs = (P("fsdp", "tp"), P("fsdp"))
    return jax.shard_map(shards, mesh=mesh, in_specs=in_specs, out_specs=out_specs, check_vma=False)
```

time: 137 us -> 96 us (0.70)
  waiting for transfers between devices: 71.6 us -> 37.8 us
  starting transfers between devices: 10.1 us -> 22.9 us
  blocking collectives: 12.4 us -> 0 us
  local copies, waits for them, and re-layouts: 12.2 us -> 2.61 us
    ppermute x10 -> x18, waiting for transfers between devices: 71.6 us -> 31.6 us  [the longest x17 20.5 us: swap(): lax.ppermute(value, 'fsdp', [(i, i ^ (core1 if i & CORE else core0)) for...]
    all_to_all x1 -> x0, blocking collectives: 12.4 us -> none  [pair_losses(): shares = lax.all_to_all(spread, ('fsdp', 'tp'), 0, 0, tiled=True)]
    ppermute x10 -> x18, starting transfers between devices: 10.1 us -> 17.8 us  [the longest x17 15.7 us: swap(): lax.ppermute(value, 'fsdp', [(i, i ^ (core1 if i & CORE else core0)) for...]
    all_to_all x0 -> x1, waiting for transfers between devices: none -> 6.15 us  [pair_losses(): shares = lax.all_to_all(spread, ('fsdp', 'tp'), 0, 0, tiled=True)]
    dynamic_slice x2 -> x0, local copies, waits for them, and re-layouts: 5.32 us -> none  [the longest x1 4.96 us: exchanged_sums(): lax.dynamic_index_in_dim(quarters, 1 - x_at, 2, keepdims=False)]
    all_to_all x0 -> x1, starting transfers between devices: none -> 5.14 us  [pair_losses(): shares = lax.all_to_all(spread, ('fsdp', 'tp'), 0, 0, tiled=True)]
    select_n x0 -> x4, other arithmetic: none -> 4.26 us  [the longest x1 2 us: exchanged_parts(): jnp.where(on_gate, up_packed[:, :split], gate_packed[:, :split])]
    unnamed x37 -> x20, local copies, waits for them, and re-layouts: 4.95 us -> 0.84 us
  transfers between devices with their start and end apart: 10 -> 19, of which waited for: 5 -> 10; matrix products, arithmetic and copies ran while one was open for 8% -> 8% of each run, Pallas kernels for 17% -> 24%
where the time goes in v2:
time: 96 us; the launch traced here: 95.8 us
  waiting for transfers between devices  37.8 us (39%)
  Pallas kernels  23.4 us (24%)
  starting transfers between devices  22.9 us (24%)
  other arithmetic  7.6 us (8%)
  local copies, waits for them, and re-layouts  2.61 us (3%)
    ppermute x17, waiting for transfers between devices, swap(): lax.ppermute(value, 'fsdp', [(i, i ^ (core1 if i & CORE else core0)) for...  20.5 us
    ppermute x17, starting transfers between devices, swap(): lax.ppermute(value, 'fsdp', [(i, i ^ (core1 if i & CORE else core0)) for...  15.7 us
    pallas_call x1, Pallas kernels, early_sums(): pl.pallas_call(early_kernel, grid=(columns * BLK // step,), out_shape=(ja...  13.1 us
    ppermute x1, waiting for transfers between devices, exchanged_parts(): lax.ppermute(direct, 'tp', [(i, i ^ 1) for i in range(lax.axis_size('tp'))])  11.1 us
    pallas_call x3, Pallas kernels, late_sums(): pl.pallas_call(functools.partial(late_kernel, first_pair), grid=(pairs,),...  10.4 us
    all_to_all x1, waiting for transfers between devices, pair_losses(): shares = lax.all_to_all(spread, ('fsdp', 'tp'), 0, 0, tiled=True)  6.15 us
    all_to_all x1, starting transfers between devices, pair_losses(): shares = lax.all_to_all(spread, ('fsdp', 'tp'), 0, 0, tiled=True)  5.14 us
    ppermute x1, starting transfers between devices, exchanged_parts(): lax.ppermute(direct, 'tp', [(i, i ^ 1) for i in range(lax.axis_size('tp'))])  2.03 us
  transfers between devices with their start and end apart: 19, of which 10 were waited for; matrix products, arithmetic and copies ran while one was open for 8% of the time, Pallas kernels for 24%

profile of v2, /device:TPU:0, one launch (start us, length us, event | category | flops | bytes accessed | tf_op | source)
XLA Modules:
  0.0 95.8 jit_solution(1039708591640308764)
XLA Ops:
  0.6 1.1 %broadcast_select_fusion.1 = (bf16[128,1024]{1,0:T(8,128)(2,1)S(1)}, bf16[128,1024]{1,0:T(8,128)(2,1)S(1)}) fusion(pred[]{:T(512)S(6)} %eq.19, bf16[128,4096]{1,0:T(8,128)(2,1)} %own.1, s32[]{:T(128)S(6)} %select_n.97, s32[]{:T(128)S(6)} %select_n.96), kind=kLoop, calls=%fused_computation.13 | loop fusion | flops 262144 | bytes 1048585 | tf_op jit(solution)/shard_map/jit(_where)/select_n | solution.py:234
  1.8 3.0 %collective-permute-start.1 = (bf16[128,1024]{1,0:T(8,128)(2,1)S(1)}, bf16[128,1024]{1,0:T(8,128)(2,1)S(1)}, u32[]{:S(2)}, u32[]{:S(2)}) collective-permute-start(bf16[128,1024]{1,0:T(8,128)(2,1)S(1)} %get-tuple-element.33), channel_id=1, source_target_pairs={{0,16},{4,12},{8,24},{12,4},{16,0},{20,28},{24,8},{28,20},{1,17},{... | collective-permute-start | bytes 786440 | tf_op jit(solution)/shard_map/ppermute | solution.py:20
  4.8 2.0 %slice_select_fusion = bf16[512,1280]{1,0:T(8,128)(2,1)S(1)} fusion(bf16[512,1920]{1,0:T(8,128)(2,1)} %param.11, bf16[512,1920]{1,0:T(8,128)(2,1)} %param.12, pred[]{:T(512)S(6)} %eq.19), kind=kLoop, calls=%fused_computation.1 | loop fusion | flops 655360 | bytes 3932161 | tf_op jit(solution)/shard_map/jit(_where)/select_n | solution.py:243
  7.3 3.8 %collective-permute-done.1 = bf16[128,1024]{1,0:T(8,128)(2,1)S(1)} collective-permute-done((bf16[128,1024]{1,0:T(8,128)(2,1)S(1)}, bf16[128,1024]{1,0:T(8,128)(2,1)S(1)}, u32[]{:S(2)}, u32[]{:S(2)}) %collective-permute-start.1) | collective-permute-done | bytes 262176 | tf_op jit(solution)/shard_map/ppermute | solution.py:20
  12.2 2.1 %collective-permute-start.6 = (bf16[512,1920]{1,0:T(8,128)(2,1)S(1)}, bf16[512,1920]{1,0:T(8,128)(2,1)}, u32[]{:S(2)}, u32[]{:S(2)}) collective-permute-start(bf16[512,1920]{1,0:T(8,128)(2,1)S(1)} %broadcast_select_fusion.mine), channel_id=1, source_target_pairs={{0,8},{4,20},{8,0},{12,28},{16,24},{20,4},{24,16},{28,12},{1,9},{5... | collective-permute-start | bytes 5898248 | tf_op jit(solution)/shard_map/ppermute | solution.py:20
  17.2 2.0 %collective-permute-start.3 = (bf16[256,1024]{1,0:T(8,128)(2,1)}, bf16[256,1024]{1,0:T(8,128)(2,1)}, u32[]{:S(2)}, u32[]{:S(2)}) collective-permute-start(bf16[256,1024]{1,0:T(8,128)(2,1)} %constant_dynamic-update-slice_fusion.direct), channel_id=1, source_target_pairs={{0,1},{1,0},{2,3},{3,2},{4,5},{5,4},{6,7},{7,6},{8,9},{9,8},{10,11... | collective-permute-start | bytes 1572872 | tf_op jit(solution)/shard_map/ppermute | solution.py:239
  19.6 1.5 %collective-permute-start.11 = (bf16[512,640]{1,0:T(8,128)(2,1)}, bf16[512,640]{1,0:T(8,128)(2,1)S(1)}, u32[]{:S(2)}, u32[]{:S(2)}) collective-permute-start(bf16[512,640]{1,0:T(8,128)(2,1)} %collective-permute-done.5.high), channel_id=1, source_target_pairs={{0,8},{4,20},{8,0},{12,28},{16,24},{20,4},{24,16},{28,12},{1,9},{5... | collective-permute-start | bytes 1966088 | tf_op jit(solution)/shard_map/ppermute | solution.py:20
  21.1 11.1 %collective-permute-done.3.passed = bf16[256,1024]{1,0:T(8,128)(2,1)} collective-permute-done((bf16[256,1024]{1,0:T(8,128)(2,1)}, bf16[256,1024]{1,0:T(8,128)(2,1)}, u32[]{:S(2)}, u32[]{:S(2)}) %collective-permute-start.3) | collective-permute-done | bytes 524320 | tf_op jit(solution)/shard_map/ppermute | solution.py:239
  32.2 4.8 %collective-permute-done.6.first = bf16[512,1920]{1,0:T(8,128)(2,1)} collective-permute-done((bf16[512,1920]{1,0:T(8,128)(2,1)S(1)}, bf16[512,1920]{1,0:T(8,128)(2,1)}, u32[]{:S(2)}, u32[]{:S(2)}) %collective-permute-start.6) | collective-permute-done | bytes 1966112 | tf_op jit(solution)/shard_map/ppermute | solution.py:20
  37.0 13.1 %shard_map.113 = (f32[512,3840]{1,0:T(8,128)S(1)}, bf16[512,512]{1,0:T(8,128)(2,1)S(1)}) custom-call(s32[32,15]{1,0:T(8,128)S(1)} %copy.33.col_slots, bf16[128,4096]{1,0:T(8,128)(2,1)} %own.1, bf16[128,4096]{1,0:T(8,128)(2,1)} %collective-permute-done.beside, bf16[256,1024]{1,0:T(8,128)(2,1)} %constant_dynamic-update-slice_fusion.direct, ...), custom_call_target="tpu_custom_call" | custom-call | flops 6039797760 | bytes 13762560 | tf_op jit(solution)/shard_map/pallas_call | solution.py:107
  51.0 3.4 %shard_map.114 = (f32[128,1280]{1,0:T(8,128)S(1)}, f32[128,1280]{1,0:T(8,128)S(1)}, f32[256,1280]{1,0:T(8,128)S(1)}) custom-call(s32[32,15]{1,0:T(8,128)S(1)} %copy.33.col_slots, bf16[512,512]{1,0:T(8,128)(2,1)S(1)} %get-tuple-element.21.panel, f32[512,3840]{1,0:T(8,128)S(1)} %get-tuple-element.22.early, bf16[512,1280]{1,0:T(8,128)(2,1)S(1)} %collective-permute-done.7.refs_0_), custom_call_target="tpu_custom_call" | custom-call | flops 671088640 | bytes 6553600 | tf_op jit(solution)/shard_map/pallas_call | solution.py:162
  54.7 1.6 %collective-permute-start.8 = (f16[128,1280]{1,0:T(8,128)(2,1)S(1)}, f16[128,1280]{1,0:T(8,128)(2,1)S(1)}, u32[]{:S(2)}, u32[]{:S(2)}) collective-permute-start(f16[128,1280]{1,0:T(8,128)(2,1)S(1)} %get-tuple-element.34), channel_id=1, source_target_pairs={{0,16},{4,12},{8,24},{12,4},{16,0},{20,28},{24,8},{28,20},{1,17},{... | collective-permute-start | bytes 983048 | tf_op jit(solution)/shard_map/ppermute | solution.py:20
  56.8 1.6 %collective-permute-done.11.refs_1_ = bf16[512,640]{1,0:T(8,128)(2,1)S(1)} collective-permute-done((bf16[512,640]{1,0:T(8,128)(2,1)}, bf16[512,640]{1,0:T(8,128)(2,1)S(1)}, u32[]{:S(2)}, u32[]{:S(2)}) %collective-permute-start.11) | collective-permute-done | bytes 655392 | tf_op jit(solution)/shard_map/ppermute | solution.py:20
  58.3 3.5 %shard_map.115 = (f32[128,1280]{1,0:T(8,128)S(1)}, f32[128,1280]{1,0:T(8,128)S(1)}, f32[256,1280]{1,0:T(8,128)S(1)}) custom-call(s32[32,15]{1,0:T(8,128)S(1)} %copy.33.col_slots, bf16[512,512]{1,0:T(8,128)(2,1)S(1)} %get-tuple-element.21.panel, f32[512,3840]{1,0:T(8,128)S(1)} %get-tuple-element.22.early, ...), custom_call_target="tpu_custom_call" | custom-call | flops 671088640 | bytes 7208960 | tf_op jit(solution)/shard_map/pallas_call | solution.py:162
  62.0 1.6 %collective-permute-start.12 = (f16[128,1280]{1,0:T(8,128)(2,1)S(1)}, f16[128,1280]{1,0:T(8,128)(2,1)S(1)}, u32[]{:S(2)}, u32[]{:S(2)}) collective-permute-start(f16[128,1280]{1,0:T(8,128)(2,1)S(1)} %get-tuple-element.36), channel_id=1, source_target_pairs={{0,16},{4,12},{8,24},{12,4},{16,0},{20,28},{24,8},{28,20},{1,17},{... | collective-permute-start | bytes 983048 | tf_op jit(solution)/shard_map/ppermute | solution.py:20
  63.6 3.5 %shard_map.116 = (f32[128,1280]{1,0:T(8,128)S(1)}, f32[128,1280]{1,0:T(8,128)S(1)}, f32[256,1280]{1,0:T(8,128)S(1)}) custom-call(s32[32,15]{1,0:T(8,128)S(1)} %copy.33.col_slots, bf16[512,512]{1,0:T(8,128)(2,1)S(1)} %get-tuple-element.21.panel, f32[512,3840]{1,0:T(8,128)S(1)} %get-tuple-element.22.early, ...), custom_call_target="tpu_custom_call" | custom-call | flops 671088640 | bytes 7208960 | tf_op jit(solution)/shard_map/pallas_call | solution.py:162
  68.0 1.6 %collective-permute-start.15 = (f16[128,1280]{1,0:T(8,128)(2,1)S(1)}, f16[128,1280]{1,0:T(8,128)(2,1)S(1)}, u32[]{:S(2)}, u32[]{:S(2)}) collective-permute-start(f16[128,1280]{1,0:T(8,128)(2,1)S(1)} %get-tuple-element.38), channel_id=1, source_target_pairs={{0,16},{4,12},{8,24},{12,4},{16,0},{20,28},{24,8},{28,20},{1,17},{... | collective-permute-start | bytes 983048 | tf_op jit(solution)/shard_map/ppermute | solution.py:20
  70.1 1.8 %collective-permute-start.16 = (f32[128,1280]{1,0:T(8,128)S(1)}, f32[128,1280]{1,0:T(8,128)S(1)}, u32[]{:S(2)}, u32[]{:S(2)}) collective-permute-start(f32[128,1280]{1,0:T(8,128)S(1)} %get-tuple-element.31), channel_id=1, source_target_pairs={{0,4},{4,0},{8,12},{12,8},{16,20},{20,16},{24,28},{28,24},{1,5},{5... | collective-permute-start | bytes 1966088 | tf_op jit(solution)/shard_map/ppermute | solution.py:20
  71.9 2.3 %collective-permute-done.14 = f16[128,1280]{1,0:T(8,128)(2,1)S(1)} collective-permute-done((f16[128,1280]{1,0:T(8,128)(2,1)S(1)}, f16[128,1280]{1,0:T(8,128)(2,1)S(1)}, u32[]{:S(2)}, u32[]{:S(2)}) %collective-permute-start.14) | collective-permute-done | bytes 327712 | tf_op jit(solution)/shard_map/ppermute | solution.py:20
  74.9 3.2 %collective-permute-done.15 = f16[128,1280]{1,0:T(8,128)(2,1)S(1)} collective-permute-done((f16[128,1280]{1,0:T(8,128)(2,1)S(1)}, f16[128,1280]{1,0:T(8,128)(2,1)S(1)}, u32[]{:S(2)}, u32[]{:S(2)}) %collective-permute-start.15) | collective-permute-done | bytes 327712 | tf_op jit(solution)/shard_map/ppermute | solution.py:20
  78.1 3.1 %collective-permute-done.17 = f16[128,1280]{1,0:T(8,128)(2,1)S(1)} collective-permute-done((f16[128,1280]{1,0:T(8,128)(2,1)S(1)}, f16[128,1280]{1,0:T(8,128)(2,1)S(1)}, u32[]{:S(2)}, u32[]{:S(2)}) %collective-permute-start.17) | collective-permute-done | bytes 327712 | tf_op jit(solution)/shard_map/ppermute | solution.py:20
  82.5 5.1 %all-to-all-start = ((f32[32,1,4]{2,1,0:T(1,128)}), f32[32,1,4]{2,1,0:T(1,128)S(1)}, u32[]{:S(2)}, u32[]{:S(2)}) async-start(f32[32,1,4]{2,1,0:T(1,128)} %broadcast_in_dim.37), calls=%async_computation | async-start | bytes 32768 | tf_op jit(solution)/shard_map/all_to_all | solution.py:195
  87.7 1.0 %pad_maximum_fusion = bf16[128,3840]{1,0:T(8,128)(2,1)} fusion(bf16[128,1280]{1,0:T(8,128)(2,1)S(1)} %multiply_convert_fusion, bf16[128,1280]{1,0:T(8,128)(2,1)S(1)} %multiply_convert_fusion.1, bf16[128,1280]{1,0:T(8,128)(2,1)S(1)} %multiply_convert_fusion.2), kind=kLoop, calls=%fused_computation.8 | loop fusion | flops 2949120 | bytes 1966080 | tf_op jit(solution)/shard_map/concatenate | solution.py:286
  88.7 6.2 %all-to-all-done = f32[32,1,4]{2,1,0:T(1,128)S(1)} async-done(((f32[32,1,4]{2,1,0:T(1,128)}), f32[32,1,4]{2,1,0:T(1,128)S(1)}, u32[]{:S(2)}, u32[]{:S(2)}) %all-to-all-start) | async-done | bytes 544 | tf_op jit(solution)/shard_map/all_to_all | solution.py:195
  (69 shorter events, 10.9 us)
Async XLA Ops:
  1.8 9.2 %collective-permute-start.1 = (bf16[128,1024]{1,0:T(8,128)(2,1)S(1)}, bf16[128,1024]{1,0:T(8,128)(2,1)S(1)}, u32[]{:S(2)}, u32[]{:S(2)}) collective-permute-start(bf16[128,1024]{1,0:T(8,128)(2,1)S(1)} %get-tuple-element.33), channel_id=1, source_target_pairs={{0,16},{4,12},{8,24},{12,4},{16,0},{20,28},{24,8},{28,20},{1,17},{... | collective-permute-start | bytes 786440 | tf_op jit(solution)/shard_map/ppermute | solution.py:20
  4.8 7.2 %copy-start = (bf16[512,1920]{1,0:T(8,128)(2,1)S(1)}, bf16[512,1920]{1,0:T(8,128)(2,1)}, u32[]{:S(2)}) copy-start(bf16[512,1920]{1,0:T(8,128)(2,1)} %param.11) | copy-start | bytes 5898244
  4.8 7.2 %copy-start.1 = (bf16[512,1920]{1,0:T(8,128)(2,1)S(1)}, bf16[512,1920]{1,0:T(8,128)(2,1)}, u32[]{:S(2)}) copy-start(bf16[512,1920]{1,0:T(8,128)(2,1)} %param.12) | copy-start | bytes 5898244
  4.8 7.2 %collective-permute-start.2 = (bf16[128,1024]{1,0:T(8,128)(2,1)S(1)}, bf16[128,1024]{1,0:T(8,128)(2,1)S(1)}, u32[]{:S(2)}, u32[]{:S(2)}) collective-permute-start(bf16[128,1024]{1,0:T(8,128)(2,1)S(1)} %get-tuple-element.32), channel_id=1, source_target_pairs={{0,12},{4,16},{8,4},{12,24},{16,28},{20,0},{24,20},{28,8},{1,13},{... | collective-permute-start | bytes 786440 | tf_op jit(solution)/shard_map/ppermute | solution.py:20
  6.8 8.9 %collective-permute-start.4 = (bf16[512,1280]{1,0:T(8,128)(2,1)S(1)}, bf16[512,1280]{1,0:T(8,128)(2,1)}, u32[]{:S(2)}, u32[]{:S(2)}) collective-permute-start(bf16[512,1280]{1,0:T(8,128)(2,1)S(1)} %slice_select_fusion), channel_id=1, source_target_pairs={{0,4},{4,0},{8,12},{12,8},{16,20},{20,16},{24,28},{28,24},{1,5},{5... | collective-permute-start | bytes 3932168 | tf_op jit(solution)/shard_map/ppermute | solution.py:20
  12.2 7.2 %copy-start.5 = (s32[1,4]{1,0:T(1,128)S(1)}, s32[1,4]{1,0:T(1,128)}, u32[]{:S(2)}) copy-start(s32[1,4]{1,0:T(1,128)} %param.17) | copy-start | bytes 52
  12.2 24.8 %collective-permute-start.6 = (bf16[512,1920]{1,0:T(8,128)(2,1)S(1)}, bf16[512,1920]{1,0:T(8,128)(2,1)}, u32[]{:S(2)}, u32[]{:S(2)}) collective-permute-start(bf16[512,1920]{1,0:T(8,128)(2,1)S(1)} %broadcast_select_fusion.mine), channel_id=1, source_target_pairs={{0,8},{4,20},{8,0},{12,28},{16,24},{20,4},{24,16},{28,12},{1,9},{5... | collective-permute-start | bytes 5898248 | tf_op jit(solution)/shard_map/ppermute | solution.py:20
  14.3 17.9 %collective-permute-start = (bf16[128,4096]{1,0:T(8,128)(2,1)}, bf16[128,4096]{1,0:T(8,128)(2,1)}, u32[]{:S(2)}, u32[]{:S(2)}) collective-permute-start(bf16[128,4096]{1,0:T(8,128)(2,1)} %own.1), channel_id=1, source_target_pairs={{0,4},{4,0},{8,12},{12,8},{16,20},{20,16},{24,28},{28,24},{1,5},{5... | collective-permute-start | bytes 3145736 | tf_op jit(solution)/shard_map/ppermute | solution.py:20
  15.2 4.4 %collective-permute-start.5 = (bf16[512,640]{1,0:T(8,128)(2,1)}, bf16[512,640]{1,0:T(8,128)(2,1)}, u32[]{:S(2)}, u32[]{:S(2)}) collective-permute-start(bf16[512,640]{1,0:T(8,128)(2,1)} %slice_select_fusion.1), channel_id=1, source_target_pairs={{0,4},{4,0},{8,12},{12,8},{16,20},{20,16},{24,28},{28,24},{1,5},{5... | collective-permute-start | bytes 1966088 | tf_op jit(solution)/shard_map/ppermute | solution.py:20
  15.7 35.3 %collective-permute-start.7 = (bf16[512,1280]{1,0:T(8,128)(2,1)}, bf16[512,1280]{1,0:T(8,128)(2,1)S(1)}, u32[]{:S(2)}, u32[]{:S(2)}) collective-permute-start(bf16[512,1280]{1,0:T(8,128)(2,1)} %collective-permute-done.4.low), channel_id=1, source_target_pairs={{0,8},{4,20},{8,0},{12,28},{16,24},{20,4},{24,16},{28,12},{1,9},{5... | collective-permute-start | bytes 3932168 | tf_op jit(solution)/shard_map/ppermute | solution.py:20
  17.2 15.0 %collective-permute-start.3 = (bf16[256,1024]{1,0:T(8,128)(2,1)}, bf16[256,1024]{1,0:T(8,128)(2,1)}, u32[]{:S(2)}, u32[]{:S(2)}) collective-permute-start(bf16[256,1024]{1,0:T(8,128)(2,1)} %constant_dynamic-update-slice_fusion.direct), channel_id=1, source_target_pairs={{0,1},{1,0},{2,3},{3,2},{4,5},{5,4},{6,7},{7,6},{8,9},{9,8},{10,11... | collective-permute-start | bytes 1572872 | tf_op jit(solution)/shard_map/ppermute | solution.py:239
  19.6 38.7 %collective-permute-start.11 = (bf16[512,640]{1,0:T(8,128)(2,1)}, bf16[512,640]{1,0:T(8,128)(2,1)S(1)}, u32[]{:S(2)}, u32[]{:S(2)}) collective-permute-start(bf16[512,640]{1,0:T(8,128)(2,1)} %collective-permute-done.5.high), channel_id=1, source_target_pairs={{0,8},{4,20},{8,0},{12,28},{16,24},{20,4},{24,16},{28,12},{1,9},{5... | collective-permute-start | bytes 1966088 | tf_op jit(solution)/shard_map/ppermute | solution.py:20
  54.6 12.7 %collective-permute-start.10 = (f16[128,1280]{1,0:T(8,128)(2,1)S(1)}, f16[128,1280]{1,0:T(8,128)(2,1)S(1)}, u32[]{:S(2)}, u32[]{:S(2)}) collective-permute-start(f16[128,1280]{1,0:T(8,128)(2,1)S(1)} %get-tuple-element.35), channel_id=1, source_target_pairs={{0,20},{4,8},{8,28},{12,0},{16,4},{20,24},{24,12},{28,16},{1,21},{... | collective-permute-start | bytes 983048 | tf_op jit(solution)/shard_map/ppermute | solution.py:20
  54.7 13.3 %collective-permute-start.8 = (f16[128,1280]{1,0:T(8,128)(2,1)S(1)}, f16[128,1280]{1,0:T(8,128)(2,1)S(1)}, u32[]{:S(2)}, u32[]{:S(2)}) collective-permute-start(f16[128,1280]{1,0:T(8,128)(2,1)S(1)} %get-tuple-element.34), channel_id=1, source_target_pairs={{0,16},{4,12},{8,24},{12,4},{16,0},{20,28},{24,8},{28,20},{1,17},{... | collective-permute-start | bytes 983048 | tf_op jit(solution)/shard_map/ppermute | solution.py:20
  56.3 13.2 %collective-permute-start.9 = (f32[128,1280]{1,0:T(8,128)S(1)}, f32[128,1280]{1,0:T(8,128)S(1)}, u32[]{:S(2)}, u32[]{:S(2)}) collective-permute-start(f32[128,1280]{1,0:T(8,128)S(1)} %get-tuple-element.25), channel_id=1, source_target_pairs={{0,4},{4,0},{8,12},{12,8},{16,20},{20,16},{24,28},{28,24},{1,5},{5... | collective-permute-start | bytes 1966088 | tf_op jit(solution)/shard_map/ppermute | solution.py:20
  62.0 8.0 %collective-permute-start.12 = (f16[128,1280]{1,0:T(8,128)(2,1)S(1)}, f16[128,1280]{1,0:T(8,128)(2,1)S(1)}, u32[]{:S(2)}, u32[]{:S(2)}) collective-permute-start(f16[128,1280]{1,0:T(8,128)(2,1)S(1)} %get-tuple-element.36), channel_id=1, source_target_pairs={{0,16},{4,12},{8,24},{12,4},{16,0},{20,28},{24,8},{28,20},{1,17},{... | collective-permute-start | bytes 983048 | tf_op jit(solution)/shard_map/ppermute | solution.py:20
  63.6 10.5 %collective-permute-start.13 = (f32[128,1280]{1,0:T(8,128)S(1)}, f32[128,1280]{1,0:T(8,128)S(1)}, u32[]{:S(2)}, u32[]{:S(2)}) collective-permute-start(f32[128,1280]{1,0:T(8,128)S(1)} %get-tuple-element.28), channel_id=1, source_target_pairs={{0,4},{4,0},{8,12},{12,8},{16,20},{20,16},{24,28},{28,24},{1,5},{5... | collective-permute-start | bytes 1966088 | tf_op jit(solution)/shard_map/ppermute | solution.py:20
  67.3 6.8 %collective-permute-start.14 = (f16[128,1280]{1,0:T(8,128)(2,1)S(1)}, f16[128,1280]{1,0:T(8,128)(2,1)S(1)}, u32[]{:S(2)}, u32[]{:S(2)}) collective-permute-start(f16[128,1280]{1,0:T(8,128)(2,1)S(1)} %get-tuple-element.37), channel_id=1, source_target_pairs={{0,20},{4,8},{8,28},{12,0},{16,4},{20,24},{24,12},{28,16},{1,21},{... | collective-permute-start | bytes 983048 | tf_op jit(solution)/shard_map/ppermute | solution.py:20
  68.0 10.1 %collective-permute-start.15 = (f16[128,1280]{1,0:T(8,128)(2,1)S(1)}, f16[128,1280]{1,0:T(8,128)(2,1)S(1)}, u32[]{:S(2)}, u32[]{:S(2)}) collective-permute-start(f16[128,1280]{1,0:T(8,128)(2,1)S(1)} %get-tuple-element.38), channel_id=1, source_target_pairs={{0,16},{4,12},{8,24},{12,4},{16,0},{20,28},{24,8},{28,20},{1,17},{... | collective-permute-start | bytes 983048 | tf_op jit(solution)/shard_map/ppermute | solution.py:20
  69.5 11.7 %collective-permute-start.17 = (f16[128,1280]{1,0:T(8,128)(2,1)S(1)}, f16[128,1280]{1,0:T(8,128)(2,1)S(1)}, u32[]{:S(2)}, u32[]{:S(2)}) collective-permute-start(f16[128,1280]{1,0:T(8,128)(2,1)S(1)} %get-tuple-element.39), channel_id=1, source_target_pairs={{0,20},{4,8},{8,28},{12,0},{16,4},{20,24},{24,12},{28,16},{1,21},{... | collective-permute-start | bytes 983048 | tf_op jit(solution)/shard_map/ppermute | solution.py:20
  70.1 11.1 %collective-permute-start.16 = (f32[128,1280]{1,0:T(8,128)S(1)}, f32[128,1280]{1,0:T(8,128)S(1)}, u32[]{:S(2)}, u32[]{:S(2)}) collective-permute-start(f32[128,1280]{1,0:T(8,128)S(1)} %get-tuple-element.31), channel_id=1, source_target_pairs={{0,4},{4,0},{8,12},{12,8},{16,20},{20,16},{24,28},{28,24},{1,5},{5... | collective-permute-start | bytes 1966088 | tf_op jit(solution)/shard_map/ppermute | solution.py:20
  81.2 13.7 %copy-start.4 = (s32[2,2]{1,0:T(2,128)S(1)}, s32[2,2]{1,0:T(2,128)}, u32[]{:S(2)}) copy-start(s32[2,2]{1,0:T(2,128)} %param.18) | copy-start | bytes 52
  81.2 14.1 %copy-start.8 = (s32[2]{0:T(128)S(1)}, s32[2]{0:T(128)}, u32[]{:S(2)}) copy-start(s32[2]{0:T(128)} %param.19) | copy-start | bytes 28
  82.5 12.3 %all-to-all-start = ((f32[32,1,4]{2,1,0:T(1,128)}), f32[32,1,4]{2,1,0:T(1,128)S(1)}, u32[]{:S(2)}, u32[]{:S(2)}) async-start(f32[32,1,4]{2,1,0:T(1,128)} %broadcast_in_dim.37), calls=%async_computation | async-start | bytes 32768 | tf_op jit(solution)/shard_map/all_to_all | solution.py:195
  (4 other events, 28.2 us)

commit v3 on v2

--- a/solution.py
+++ b/solution.py
@@ -8,7 +8,7 @@
 from jax.sharding import PartitionSpec as P
 
 BLK = 128
-EARLY_VMEM, LATE_VMEM = 24 << 20, 12 << 20
+EARLY_VMEM, LATE_VMEM = 18 << 20, 12 << 20
 CORE, X, Y = 1, 2, 4
 
 
@@ -57,7 +57,7 @@
 
 
 def early_kernel(
-    col_slots, own, beside, direct, passed, mine, low, high, first,
+    col_slots, own, direct, passed, mine, low, high, first,
     total, later, panel, weights, dense, slot_at, sems,
 ):
     depth, split = mine.shape[0], low.shape[1]
@@ -65,30 +65,34 @@
 
     @pl.when(pl.program_id(0) == 0)
     def _():
-        copies = [
-            pltpu.make_async_copy(mine, weights.at[0], sems.at[0]),
-            pltpu.make_async_copy(low, weights.at[1, :, :split], sems.at[1]),
-            pltpu.make_async_copy(high, weights.at[1, :, split:], sems.at[2]),
-            pltpu.make_async_copy(first, weights.at[2], sems.at[3]),
+        sources = [
+            (mine, weights.at[0]),
+            (low, weights.at[1, :, :split]),
+            (high, weights.at[1, :, split:]),
+            (first, weights.at[2]),
         ]
+        chunks, straight = places()
+        count = own.shape[0]
+        targets = [panel.at[:, s * depth : (s + 1) * depth] for s in range(3)] + [later]
+        for s in range(4):
+            at = pl.multiple_of((s // 2 * 2 + (chunks[s] & 1)) * depth, depth)
+            sources.append((own.at[:, pl.ds(at, depth)], targets[s].at[:count]))
+        copies = [pltpu.make_async_copy(a, b, sems.at[n]) for n, (a, b) in enumerate(sources)]
         for copy in copies:
             copy.start()
-        count = own.shape[0]
-        chunks, straight = places()
         for s in range(4):
-            wide = pl.ds(pl.multiple_of(chunks[s] * depth, depth), depth)
             near = pl.ds(pl.multiple_of((chunks[s] & 1) * depth, depth), depth)
-            groups = [
-                own[:, wide],
-                beside[:, wide],
-                jnp.where(straight[s], direct[:, near], passed[:, near]),
-            ]
-            for group, start in zip(groups, (0, count, 2 * count)):
-                at = slice(start, start + group.shape[0])
-                if s < 3:
-                    panel[at, s * depth : (s + 1) * depth] = group
-                else:
-                    later[at, :] = group
+            target, sem = targets[s].at[count:], sems.at[len(copies)]
+
+            @pl.when(straight[s])
+            def _():
+                pltpu.make_async_copy(direct.at[:, near], target, sem).start()
+
+            @pl.when(~straight[s])
+            def _():
+                pltpu.make_async_copy(passed.at[:, near], target, sem).start()
+
+            copies.append(pltpu.make_async_copy(direct.at[:, near], target, sem))
         for s in range(3):
             find_slots(slot_at, col_slots, chunks[s] * rows, rows, s * rows)
         for copy in copies:
@@ -101,7 +105,7 @@
 
 
 def early_sums(col_slots, tokens, weights):
-    count, (depth, width) = 4 * tokens[0].shape[0], weights[0].shape
+    count, (depth, width) = 2 * tokens[0].shape[0], weights[0].shape
     columns = 2 * col_slots.shape[1]
     step = 3 * 2 * BLK if columns % 6 == 0 else 2 * BLK
     return pl.pallas_call(
@@ -111,14 +115,14 @@
             jax.ShapeDtypeStruct((count, columns * BLK), jnp.float32),
             jax.ShapeDtypeStruct((count, depth), jnp.bfloat16),
         ),
-        in_specs=[SMEM] + [VMEM] * 4 + [ANY] * 4,
+        in_specs=[SMEM] + [ANY] * 7,
         out_specs=(pl.BlockSpec((count, step), lambda n: (0, n)), VMEM),
         scratch_shapes=[
             pltpu.VMEM((count, 3 * depth), jnp.bfloat16),
             pltpu.VMEM((3, depth, width), jnp.bfloat16),
             pltpu.VMEM((3 * depth, step), jnp.bfloat16),
             pltpu.SMEM((3 * depth // BLK, columns), jnp.int32),
-            pltpu.SemaphoreType.DMA((4,)),
+            pltpu.SemaphoreType.DMA((12,)),
         ],
         compiler_params=pltpu.CompilerParams(vmem_limit_bytes=EARLY_VMEM),
         cost_estimate=pl.CostEstimate(
@@ -228,25 +232,28 @@
     third = 2 * slot_count // 3
     quarter = tokens.shape[1] // 4
 
-    for_gate = lax.dynamic_slice_in_dim(tokens, (2 * (1 - y_at) + plane) * quarter, quarter, 1)
-    for_up = lax.dynamic_slice_in_dim(tokens, (2 * plane + 1 - x_at) * quarter, quarter, 1)
-    same = swap(jnp.where(on_gate, for_gate, for_up), Y, X)
-    cross = swap(jnp.where(on_gate, for_up, for_gate), X | CORE, Y | CORE)
-    gate_after, up_after, same, cross = lax.optimization_barrier(
-        (gate_packed, up_packed, same, cross)
-    )
-    direct = jnp.concatenate([same, cross])
+    beside = swap(tokens, CORE, CORE)
+    mine = jnp.where(on_gate, gate_packed, up_packed)
+    first = swap(mine, X, Y)
+    start = quarter * jnp.where(on_gate, 2 * (1 - y_at) + plane, 2 * plane + 1 - x_at)
+    quarters = [lax.dynamic_slice_in_dim(rows, start, quarter, 1) for rows in (tokens, beside)]
+    direct = swap(jnp.concatenate(quarters), Y, X)
+    tokens_after, beside, direct = lax.optimization_barrier((tokens, beside, direct))
     passed = lax.ppermute(direct, "tp", [(i, i ^ 1) for i in range(lax.axis_size("tp"))])
-    beside = swap(tokens, CORE, CORE)
-
     split = third * BLK
     low = swap(jnp.where(on_gate, up_packed[:, :split], gate_packed[:, :split]), CORE, CORE)
     high = swap(jnp.where(on_gate, up_packed[:, split:], gate_packed[:, split:]), CORE, CORE)
-    mine = jnp.where(on_gate, gate_after, up_after)
-    first = swap(mine, X, Y)
-    far_low, far_high = swap(low, X, Y), swap(high, X, Y)
-
-    early, panel = early_sums(col_slots, (tokens, beside, direct, passed), (mine, low, high, first))
+    far_low = swap(low, X, Y)
+    high, passed = lax.optimization_barrier((high, passed))
+    far_high = swap(high, X, Y)
+    chip = me >> 1
+    far_chip = chip ^ jnp.where(on_gate, 1, 2)
+    both = jnp.concatenate([tokens_after, beside])
+    own = jnp.concatenate(
+        [lax.dynamic_slice_in_dim(both, at * quarter, quarter, 1) for at in (chip, far_chip)], axis=1
+    )
+
+    early, panel = early_sums(col_slots, (own, direct, passed), (mine, low, high, first))
     parts = []
     for n in range(3):
         sources = (far_low,) if n == 0 else (far_low, far_high)

time: 96 us -> 95.1 us (level)
  waiting for transfers between devices: 37.8 us -> 33.8 us
  local copies, waits for them, and re-layouts: 2.61 us -> 5.86 us
  other arithmetic: 7.6 us -> 9.71 us
  Pallas kernels: 23.4 us -> 22.2 us
  starting transfers between devices: 22.9 us -> 21.7 us
    ppermute x1, waiting for transfers between devices: 11.1 us -> 8.57 us  [exchanged_parts(): lax.ppermute(direct, 'tp', [(i, i ^ 1) for i in range(lax.axis_size('tp'))])]
    ppermute x17 -> x16, starting transfers between devices: 15.7 us -> 13.6 us  [swap(): lax.ppermute(value, 'fsdp', [(i, i ^ (core1 if i & CORE else core0)) for...]
    dynamic_slice x0 -> x3, local copies, waits for them, and re-layouts: none -> 2.07 us  [the longest x2 1.98 us: exchanged_parts(): lax.dynamic_slice_in_dim(rows, start, quarter, 1)]
    ppermute x17 -> x16, waiting for transfers between devices: 20.5 us -> 19.1 us  [swap(): lax.ppermute(value, 'fsdp', [(i, i ^ (core1 if i & CORE else core0)) for...]
    all_to_all x1, starting transfers between devices: 5.14 us -> 6.5 us  [pair_losses(): shares = lax.all_to_all(spread, ('fsdp', 'tp'), 0, 0, tiled=True)]
    select_n x1, other arithmetic: 0.91 us -> 2.2 us  [exchanged_parts(): jnp.where(on_gate, up_packed[:, split:], gate_packed[:, split:])]
    pallas_call x1, Pallas kernels: 13.1 us -> 11.8 us  [early_sums(): pl.pallas_call(early_kernel, grid=(columns * BLK // step,), out_shape=(ja...]
    select_n x2 -> x1, other arithmetic: 1.36 us -> 0.21 us  [exchanged_parts(): mine = jnp.where(on_gate, gate_packed, up_packed)]
  transfers between devices with their start and end apart: 19 -> 18, of which waited for: 10 -> 7; matrix products, arithmetic and copies ran while one was open for 8% -> 15% of each run, Pallas kernels for 24% -> 23%
where the time goes in v3:
time: 95.1 us; the launch traced here: 94.8 us
  waiting for transfers between devices  33.8 us (36%)
  Pallas kernels  22.2 us (23%)
  starting transfers between devices  21.7 us (23%)
  other arithmetic  9.71 us (10%)
  local copies, waits for them, and re-layouts  5.86 us (6%)
    ppermute x16, waiting for transfers between devices, swap(): lax.ppermute(value, 'fsdp', [(i, i ^ (core1 if i & CORE else core0)) for...  19.1 us
    ppermute x16, starting transfers between devices, swap(): lax.ppermute(value, 'fsdp', [(i, i ^ (core1 if i & CORE else core0)) for...  13.6 us
    pallas_call x1, Pallas kernels, early_sums(): pl.pallas_call(early_kernel, grid=(columns * BLK // step,), out_shape=(ja...  11.8 us
    pallas_call x3, Pallas kernels, late_sums(): pl.pallas_call(functools.partial(late_kernel, first_pair), grid=(pairs,),...  10.4 us
    ppermute x1, waiting for transfers between devices, exchanged_parts(): lax.ppermute(direct, 'tp', [(i, i ^ 1) for i in range(lax.axis_size('tp'))])  8.57 us
    all_to_all x1, starting transfers between devices, pair_losses(): shares = lax.all_to_all(spread, ('fsdp', 'tp'), 0, 0, tiled=True)  6.5 us
    all_to_all x1, waiting for transfers between devices, pair_losses(): shares = lax.all_to_all(spread, ('fsdp', 'tp'), 0, 0, tiled=True)  6.15 us
    select_n x1, other arithmetic, exchanged_parts(): jnp.where(on_gate, up_packed[:, :split], gate_packed[:, :split])  3.05 us
  transfers between devices with their start and end apart: 18, of which 7 were waited for; matrix products, arithmetic and copies ran while one was open for 15% of the time, Pallas kernels for 23%

profile of v3, /device:TPU:0, one launch (start us, length us, event | category | flops | bytes accessed | tf_op | source)
XLA Modules:
  0.0 94.8 jit_solution(930372988789790723)
XLA Ops:
  1.2 3.1 %slice_select_fusion = bf16[512,1280]{1,0:T(8,128)(2,1)} fusion(bf16[512,1920]{1,0:T(8,128)(2,1)} %param.11, bf16[512,1920]{1,0:T(8,128)(2,1)} %param.12, pred[]{:T(512)S(6)} %eq.19), kind=kLoop, calls=%fused_computation.1 | loop fusion | flops 655360 | bytes 3932161 | tf_op jit(solution)/shard_map/jit(_where)/select_n | solution.py:244
  4.5 3.0 %collective-permute-start.5 = (bf16[512,1920]{1,0:T(8,128)(2,1)S(1)}, bf16[512,1920]{1,0:T(8,128)(2,1)}, u32[]{:S(2)}, u32[]{:S(2)}) collective-permute-start(bf16[512,1920]{1,0:T(8,128)(2,1)S(1)} %broadcast_select_fusion.mine), channel_id=1, source_target_pairs={{0,8},{4,20},{8,0},{12,28},{16,24},{20,4},{24,16},{28,12},{1,9},{5... | collective-permute-start | bytes 5898248 | tf_op jit(solution)/shard_map/ppermute | solution.py:20
  7.5 1.0 %constant_dynamic-slice_fusion.3 = bf16[128,1024]{1,0:T(8,128)(2,1)S(1)} fusion(bf16[128,4096]{1,0:T(8,128)(2,1)} %param.10, s32[]{:T(128)S(6)} %select_n.96), kind=kLoop, calls=%fused_computation.29 | loop fusion | bytes 524292 | tf_op jit(solution)/shard_map/dynamic_slice | solution.py:239
  8.5 1.0 %constant_dynamic-slice_fusion.2 = bf16[128,1024]{1,0:T(8,128)(2,1)S(1)} fusion(bf16[128,4096]{1,0:T(8,128)(2,1)} %collective-permute-done, s32[]{:T(128)S(6)} %select_n.96), kind=kLoop, calls=%fused_computation.28 | loop fusion | bytes 524292 | tf_op jit(solution)/shard_map/dynamic_slice | solution.py:239
  10.3 1.5 %collective-permute-start.1 = (bf16[256,1024]{1,0:T(8,128)(2,1)}, bf16[256,1024]{1,0:T(8,128)(2,1)}, u32[]{:S(2)}, u32[]{:S(2)}) collective-permute-start(bf16[256,1024]{1,0:T(8,128)(2,1)} %pad_maximum_fusion.2), channel_id=1, source_target_pairs={{0,16},{4,12},{8,24},{12,4},{16,0},{20,28},{24,8},{28,20},{1,17},{... | collective-permute-start | bytes 1572872 | tf_op jit(solution)/shard_map/ppermute | solution.py:20
  11.8 2.2 %slice_select_fusion.1 = bf16[512,640]{1,0:T(8,128)(2,1)} fusion(bf16[512,1920]{1,0:T(8,128)(2,1)} %param.11, bf16[512,1920]{1,0:T(8,128)(2,1)} %param.12, pred[]{:T(512)S(6)} %eq.19), kind=kLoop, calls=%fused_computation.13 | loop fusion | flops 327680 | bytes 1966081 | tf_op jit(solution)/shard_map/jit(_where)/select_n | solution.py:245
  15.0 10.5 %collective-permute-done.1.direct = bf16[256,1024]{1,0:T(8,128)(2,1)} collective-permute-done((bf16[256,1024]{1,0:T(8,128)(2,1)}, bf16[256,1024]{1,0:T(8,128)(2,1)}, u32[]{:S(2)}, u32[]{:S(2)}) %collective-permute-start.1) | collective-permute-done | bytes 524320 | tf_op jit(solution)/shard_map/ppermute | solution.py:20
  25.5 1.6 %collective-permute-start.3 = (bf16[256,1024]{1,0:T(8,128)(2,1)}, bf16[256,1024]{1,0:T(8,128)(2,1)S(1)}, u32[]{:S(2)}, u32[]{:S(2)}) collective-permute-start(bf16[256,1024]{1,0:T(8,128)(2,1)} %collective-permute-done.1.direct), channel_id=1, source_target_pairs={{0,1},{1,0},{2,3},{3,2},{4,5},{5,4},{6,7},{7,6},{8,9},{9,8},{10,11... | collective-permute-start | bytes 1572872 | tf_op jit(solution)/shard_map/ppermute | solution.py:242
  27.1 1.3 %constant_dynamic-update-slice_fusion.1 = bf16[256,4096]{1,0:T(8,128)(2,1)S(1)} fusion(bf16[128,4096]{1,0:T(8,128)(2,1)} %param.10), kind=kLoop, calls=%fused_computation.16 | loop fusion | bytes 2097152
  28.4 1.3 %constant_dynamic-update-slice_fusion = bf16[256,4096]{1,0:T(8,128)(2,1)S(1)} fusion(bf16[256,4096]{1,0:T(8,128)(2,1)S(1)} %constant_dynamic-update-slice_fusion.1, bf16[128,4096]{1,0:T(8,128)(2,1)} %collective-permute-done), kind=kLoop, calls=%fused_computation.15 | loop fusion | bytes 2097152 | tf_op jit(solution)/shard_map/concatenate | solution.py:251
  29.9 8.6 %collective-permute-done.3.passed = bf16[256,1024]{1,0:T(8,128)(2,1)S(1)} collective-permute-done((bf16[256,1024]{1,0:T(8,128)(2,1)}, bf16[256,1024]{1,0:T(8,128)(2,1)S(1)}, u32[]{:S(2)}, u32[]{:S(2)}) %collective-permute-start.3) | collective-permute-done | bytes 524320 | tf_op jit(solution)/shard_map/ppermute | solution.py:242
  38.5 1.5 %collective-permute-start.10 = (bf16[512,640]{1,0:T(8,128)(2,1)}, bf16[512,640]{1,0:T(8,128)(2,1)S(1)}, u32[]{:S(2)}, u32[]{:S(2)}) collective-permute-start(bf16[512,640]{1,0:T(8,128)(2,1)} %collective-permute-done.2.high), channel_id=1, source_target_pairs={{0,8},{4,20},{8,0},{12,28},{16,24},{20,4},{24,16},{28,12},{1,9},{5... | collective-permute-start | bytes 1966088 | tf_op jit(solution)/shard_map/ppermute | solution.py:20
  40.0 11.8 %shard_map.113 = (f32[512,3840]{1,0:T(8,128)S(1)}, bf16[512,512]{1,0:T(8,128)(2,1)S(1)}) custom-call(s32[32,15]{1,0:T(8,128)S(1)} %copy.33.col_slots, bf16[256,2048]{1,0:T(8,128)(2,1)S(1)} %pad_maximum_fusion.own, bf16[256,1024]{1,0:T(8,128)(2,1)} %collective-permute-done.1.direct, bf16[256,1024]{1,0:T(8,128)(2,1)S(1)} %collective-permute-done.3.passed, ...), custom_call_target="tpu_custom_call" | custom-call | flops 6039797760 | bytes 13762560 | tf_op jit(solution)/shard_map/pallas_call | solution.py:111
  51.8 3.4 %shard_map.114 = (f32[128,1280]{1,0:T(8,128)S(1)}, f32[128,1280]{1,0:T(8,128)S(1)}, f32[256,1280]{1,0:T(8,128)S(1)}) custom-call(s32[32,15]{1,0:T(8,128)S(1)} %copy.33.col_slots, bf16[512,512]{1,0:T(8,128)(2,1)S(1)} %get-tuple-element.23.panel, f32[512,3840]{1,0:T(8,128)S(1)} %get-tuple-element.24.early, bf16[512,1280]{1,0:T(8,128)(2,1)S(1)} %collective-permute-done.6.refs_0_), custom_call_target="tpu_custom_call" | custom-call | flops 671088640 | bytes 6553600 | tf_op jit(solution)/shard_map/pallas_call | solution.py:166
  57.6 3.5 %shard_map.115 = (f32[128,1280]{1,0:T(8,128)S(1)}, f32[128,1280]{1,0:T(8,128)S(1)}, f32[256,1280]{1,0:T(8,128)S(1)}) custom-call(s32[32,15]{1,0:T(8,128)S(1)} %copy.33.col_slots, bf16[512,512]{1,0:T(8,128)(2,1)S(1)} %get-tuple-element.23.panel, f32[512,3840]{1,0:T(8,128)S(1)} %get-tuple-element.24.early, ...), custom_call_target="tpu_custom_call" | custom-call | flops 671088640 | bytes 7208960 | tf_op jit(solution)/shard_map/pallas_call | solution.py:166
  61.2 2.4 %collective-permute-start.11 = (f16[128,1280]{1,0:T(8,128)(2,1)S(1)}, f16[128,1280]{1,0:T(8,128)(2,1)S(1)}, u32[]{:S(2)}, u32[]{:S(2)}) collective-permute-start(f16[128,1280]{1,0:T(8,128)(2,1)S(1)} %get-tuple-element.38), channel_id=1, source_target_pairs={{0,16},{4,12},{8,24},{12,4},{16,0},{20,28},{24,8},{28,20},{1,17},{... | collective-permute-start | bytes 983048 | tf_op jit(solution)/shard_map/ppermute | solution.py:20
  63.7 3.5 %shard_map.116 = (f32[128,1280]{1,0:T(8,128)S(1)}, f32[128,1280]{1,0:T(8,128)S(1)}, f32[256,1280]{1,0:T(8,128)S(1)}) custom-call(s32[32,15]{1,0:T(8,128)S(1)} %copy.33.col_slots, bf16[512,512]{1,0:T(8,128)(2,1)S(1)} %get-tuple-element.23.panel, f32[512,3840]{1,0:T(8,128)S(1)} %get-tuple-element.24.early, ...), custom_call_target="tpu_custom_call" | custom-call | flops 671088640 | bytes 7208960 | tf_op jit(solution)/shard_map/pallas_call | solution.py:166
  67.3 1.4 %collective-permute-start.12 = (f32[128,1280]{1,0:T(8,128)S(1)}, f32[128,1280]{1,0:T(8,128)S(1)}, u32[]{:S(2)}, u32[]{:S(2)}) collective-permute-start(f32[128,1280]{1,0:T(8,128)S(1)} %get-tuple-element.30), channel_id=1, source_target_pairs={{0,4},{4,0},{8,12},{12,8},{16,20},{20,16},{24,28},{28,24},{1,5},{5... | collective-permute-start | bytes 1966088 | tf_op jit(solution)/shard_map/ppermute | solution.py:20
  70.2 1.5 %collective-permute-done.13 = f16[128,1280]{1,0:T(8,128)(2,1)S(1)} collective-permute-done((f16[128,1280]{1,0:T(8,128)(2,1)S(1)}, f16[128,1280]{1,0:T(8,128)(2,1)S(1)}, u32[]{:S(2)}, u32[]{:S(2)}) %collective-permute-start.13) | collective-permute-done | bytes 327712 | tf_op jit(solution)/shard_map/ppermute | solution.py:20
  72.2 4.4 %collective-permute-done.14 = f16[128,1280]{1,0:T(8,128)(2,1)S(1)} collective-permute-done((f16[128,1280]{1,0:T(8,128)(2,1)S(1)}, f16[128,1280]{1,0:T(8,128)(2,1)S(1)}, u32[]{:S(2)}, u32[]{:S(2)}) %collective-permute-start.14) | collective-permute-done | bytes 327712 | tf_op jit(solution)/shard_map/ppermute | solution.py:20
  76.7 2.1 %collective-permute-done.16 = f16[128,1280]{1,0:T(8,128)(2,1)S(1)} collective-permute-done((f16[128,1280]{1,0:T(8,128)(2,1)S(1)}, f16[128,1280]{1,0:T(8,128)(2,1)S(1)}, u32[]{:S(2)}, u32[]{:S(2)}) %collective-permute-start.16) | collective-permute-done | bytes 327712 | tf_op jit(solution)/shard_map/ppermute | solution.py:20
  80.1 6.5 %all-to-all-start = ((f32[32,1,4]{2,1,0:T(1,128)}), f32[32,1,4]{2,1,0:T(1,128)S(1)}, u32[]{:S(2)}, u32[]{:S(2)}) async-start(f32[32,1,4]{2,1,0:T(1,128)} %broadcast_in_dim.37), calls=%async_computation | async-start | bytes 32768 | tf_op jit(solution)/shard_map/all_to_all | solution.py:199
  86.6 1.0 %pad_maximum_fusion.1 = bf16[128,3840]{1,0:T(8,128)(2,1)} fusion(bf16[128,1280]{1,0:T(8,128)(2,1)S(1)} %multiply_convert_fusion, bf16[128,1280]{1,0:T(8,128)(2,1)S(1)} %multiply_convert_fusion.1, bf16[128,1280]{1,0:T(8,128)(2,1)S(1)} %multiply_convert_fusion.2), kind=kLoop, calls=%fused_computation.9 | loop fusion | flops 2949120 | bytes 1966080 | tf_op jit(solution)/shard_map/concatenate | solution.py:293
  87.6 6.2 %all-to-all-done = f32[32,1,4]{2,1,0:T(1,128)S(1)} async-done(((f32[32,1,4]{2,1,0:T(1,128)}), f32[32,1,4]{2,1,0:T(1,128)S(1)}, u32[]{:S(2)}, u32[]{:S(2)}) %all-to-all-start) | async-done | bytes 544 | tf_op jit(solution)/shard_map/all_to_all | solution.py:199
  (71 shorter events, 9.5 us)
Async XLA Ops:
  0.6 7.9 %collective-permute-start = (bf16[128,4096]{1,0:T(8,128)(2,1)}, bf16[128,4096]{1,0:T(8,128)(2,1)}, u32[]{:S(2)}, u32[]{:S(2)}) collective-permute-start(bf16[128,4096]{1,0:T(8,128)(2,1)} %param.10), channel_id=1, source_target_pairs={{0,4},{4,0},{8,12},{12,8},{16,20},{20,16},{24,28},{28,24},{1,5},{5... | collective-permute-start | bytes 3145736 | tf_op jit(solution)/shard_map/ppermute | solution.py:20
  4.2 10.2 %collective-permute-start.4 = (bf16[512,1280]{1,0:T(8,128)(2,1)}, bf16[512,1280]{1,0:T(8,128)(2,1)S(1)}, u32[]{:S(2)}, u32[]{:S(2)}) collective-permute-start(bf16[512,1280]{1,0:T(8,128)(2,1)} %slice_select_fusion), channel_id=1, source_target_pairs={{0,4},{4,0},{8,12},{12,8},{16,20},{20,16},{24,28},{28,24},{1,5},{5... | collective-permute-start | bytes 3932168 | tf_op jit(solution)/shard_map/ppermute | solution.py:20
  4.5 35.5 %collective-permute-start.5 = (bf16[512,1920]{1,0:T(8,128)(2,1)S(1)}, bf16[512,1920]{1,0:T(8,128)(2,1)}, u32[]{:S(2)}, u32[]{:S(2)}) collective-permute-start(bf16[512,1920]{1,0:T(8,128)(2,1)S(1)} %broadcast_select_fusion.mine), channel_id=1, source_target_pairs={{0,8},{4,20},{8,0},{12,28},{16,24},{20,4},{24,16},{28,12},{1,9},{5... | collective-permute-start | bytes 5898248 | tf_op jit(solution)/shard_map/ppermute | solution.py:20
  7.5 6.6 %copy-start.2 = (bf16[3840]{0:T(1024)(128)(2,1)S(1)}, bf16[3840]{0:T(1024)(128)(2,1)}, u32[]{:S(2)}) copy-start(bf16[3840]{0:T(1024)(128)(2,1)} %param.14) | copy-start | bytes 23044
  7.5 6.7 %copy-start.5 = (s32[1,4]{1,0:T(1,128)S(1)}, s32[1,4]{1,0:T(1,128)}, u32[]{:S(2)}) copy-start(s32[1,4]{1,0:T(1,128)} %param.17) | copy-start | bytes 52
  10.3 15.2 %collective-permute-start.1 = (bf16[256,1024]{1,0:T(8,128)(2,1)}, bf16[256,1024]{1,0:T(8,128)(2,1)}, u32[]{:S(2)}, u32[]{:S(2)}) collective-permute-start(bf16[256,1024]{1,0:T(8,128)(2,1)} %pad_maximum_fusion.2), channel_id=1, source_target_pairs={{0,16},{4,12},{8,24},{12,4},{16,0},{20,28},{24,8},{28,20},{1,17},{... | collective-permute-start | bytes 1572872 | tf_op jit(solution)/shard_map/ppermute | solution.py:20
  14.0 15.9 %collective-permute-start.2 = (bf16[512,640]{1,0:T(8,128)(2,1)}, bf16[512,640]{1,0:T(8,128)(2,1)}, u32[]{:S(2)}, u32[]{:S(2)}) collective-permute-start(bf16[512,640]{1,0:T(8,128)(2,1)} %slice_select_fusion.1), channel_id=1, source_target_pairs={{0,4},{4,0},{8,12},{12,8},{16,20},{20,16},{24,28},{28,24},{1,5},{5... | collective-permute-start | bytes 1966088 | tf_op jit(solution)/shard_map/ppermute | solution.py:20
  14.4 37.5 %collective-permute-start.6 = (bf16[512,1280]{1,0:T(8,128)(2,1)S(1)}, bf16[512,1280]{1,0:T(8,128)(2,1)S(1)}, u32[]{:S(2)}, u32[]{:S(2)}) collective-permute-start(bf16[512,1280]{1,0:T(8,128)(2,1)S(1)} %collective-permute-done.4.low), channel_id=1, source_target_pairs={{0,8},{4,20},{8,0},{12,28},{16,24},{20,4},{24,16},{28,12},{1,9},{5... | collective-permute-start | bytes 3932168 | tf_op jit(solution)/shard_map/ppermute | solution.py:20
  25.5 13.0 %collective-permute-start.3 = (bf16[256,1024]{1,0:T(8,128)(2,1)}, bf16[256,1024]{1,0:T(8,128)(2,1)S(1)}, u32[]{:S(2)}, u32[]{:S(2)}) collective-permute-start(bf16[256,1024]{1,0:T(8,128)(2,1)} %collective-permute-done.1.direct), channel_id=1, source_target_pairs={{0,1},{1,0},{2,3},{3,2},{4,5},{5,4},{6,7},{7,6},{8,9},{9,8},{10,11... | collective-permute-start | bytes 1572872 | tf_op jit(solution)/shard_map/ppermute | solution.py:242
  38.5 19.1 %collective-permute-start.10 = (bf16[512,640]{1,0:T(8,128)(2,1)}, bf16[512,640]{1,0:T(8,128)(2,1)S(1)}, u32[]{:S(2)}, u32[]{:S(2)}) collective-permute-start(bf16[512,640]{1,0:T(8,128)(2,1)} %collective-permute-done.2.high), channel_id=1, source_target_pairs={{0,8},{4,20},{8,0},{12,28},{16,24},{20,4},{24,16},{28,12},{1,9},{5... | collective-permute-start | bytes 1966088 | tf_op jit(solution)/shard_map/ppermute | solution.py:20
  55.5 11.9 %collective-permute-start.7 = (f16[128,1280]{1,0:T(8,128)(2,1)S(1)}, f16[128,1280]{1,0:T(8,128)(2,1)S(1)}, u32[]{:S(2)}, u32[]{:S(2)}) collective-permute-start(f16[128,1280]{1,0:T(8,128)(2,1)S(1)} %get-tuple-element.36), channel_id=1, source_target_pairs={{0,16},{4,12},{8,24},{12,4},{16,0},{20,28},{24,8},{28,20},{1,17},{... | collective-permute-start | bytes 983048 | tf_op jit(solution)/shard_map/ppermute | solution.py:20
  56.1 12.7 %collective-permute-start.9 = (f16[128,1280]{1,0:T(8,128)(2,1)S(1)}, f16[128,1280]{1,0:T(8,128)(2,1)S(1)}, u32[]{:S(2)}, u32[]{:S(2)}) collective-permute-start(f16[128,1280]{1,0:T(8,128)(2,1)S(1)} %get-tuple-element.37), channel_id=1, source_target_pairs={{0,20},{4,8},{8,28},{12,0},{16,4},{20,24},{24,12},{28,16},{1,21},{... | collective-permute-start | bytes 983048 | tf_op jit(solution)/shard_map/ppermute | solution.py:20
  56.2 13.4 %collective-permute-start.8 = (f32[128,1280]{1,0:T(8,128)S(1)}, f32[128,1280]{1,0:T(8,128)S(1)}, u32[]{:S(2)}, u32[]{:S(2)}) collective-permute-start(f32[128,1280]{1,0:T(8,128)S(1)} %get-tuple-element.27), channel_id=1, source_target_pairs={{0,4},{4,0},{8,12},{12,8},{16,20},{20,16},{24,28},{28,24},{1,5},{5... | collective-permute-start | bytes 1966088 | tf_op jit(solution)/shard_map/ppermute | solution.py:20
  61.2 8.7 %collective-permute-start.11 = (f16[128,1280]{1,0:T(8,128)(2,1)S(1)}, f16[128,1280]{1,0:T(8,128)(2,1)S(1)}, u32[]{:S(2)}, u32[]{:S(2)}) collective-permute-start(f16[128,1280]{1,0:T(8,128)(2,1)S(1)} %get-tuple-element.38), channel_id=1, source_target_pairs={{0,16},{4,12},{8,24},{12,4},{16,0},{20,28},{24,8},{28,20},{1,17},{... | collective-permute-start | bytes 983048 | tf_op jit(solution)/shard_map/ppermute | solution.py:20
  63.6 8.1 %collective-permute-start.13 = (f16[128,1280]{1,0:T(8,128)(2,1)S(1)}, f16[128,1280]{1,0:T(8,128)(2,1)S(1)}, u32[]{:S(2)}, u32[]{:S(2)}) collective-permute-start(f16[128,1280]{1,0:T(8,128)(2,1)S(1)} %get-tuple-element.39), channel_id=1, source_target_pairs={{0,20},{4,8},{8,28},{12,0},{16,4},{20,24},{24,12},{28,16},{1,21},{... | collective-permute-start | bytes 983048 | tf_op jit(solution)/shard_map/ppermute | solution.py:20
  67.3 4.4 %collective-permute-start.12 = (f32[128,1280]{1,0:T(8,128)S(1)}, f32[128,1280]{1,0:T(8,128)S(1)}, u32[]{:S(2)}, u32[]{:S(2)}) collective-permute-start(f32[128,1280]{1,0:T(8,128)S(1)} %get-tuple-element.30), channel_id=1, source_target_pairs={{0,4},{4,0},{8,12},{12,8},{16,20},{20,16},{24,28},{28,24},{1,5},{5... | collective-permute-start | bytes 1966088 | tf_op jit(solution)/shard_map/ppermute | solution.py:20
  68.8 7.9 %collective-permute-start.14 = (f16[128,1280]{1,0:T(8,128)(2,1)S(1)}, f16[128,1280]{1,0:T(8,128)(2,1)S(1)}, u32[]{:S(2)}, u32[]{:S(2)}) collective-permute-start(f16[128,1280]{1,0:T(8,128)(2,1)S(1)} %get-tuple-element.40), channel_id=1, source_target_pairs={{0,16},{4,12},{8,24},{12,4},{16,0},{20,28},{24,8},{28,20},{1,17},{... | collective-permute-start | bytes 983048 | tf_op jit(solution)/shard_map/ppermute | solution.py:20
  69.5 9.3 %collective-permute-start.16 = (f16[128,1280]{1,0:T(8,128)(2,1)S(1)}, f16[128,1280]{1,0:T(8,128)(2,1)S(1)}, u32[]{:S(2)}, u32[]{:S(2)}) collective-permute-start(f16[128,1280]{1,0:T(8,128)(2,1)S(1)} %get-tuple-element.41), channel_id=1, source_target_pairs={{0,20},{4,8},{8,28},{12,0},{16,4},{20,24},{24,12},{28,16},{1,21},{... | collective-permute-start | bytes 983048 | tf_op jit(solution)/shard_map/ppermute | solution.py:20
  70.0 8.8 %collective-permute-start.15 = (f32[128,1280]{1,0:T(8,128)S(1)}, f32[128,1280]{1,0:T(8,128)S(1)}, u32[]{:S(2)}, u32[]{:S(2)}) collective-permute-start(f32[128,1280]{1,0:T(8,128)S(1)} %get-tuple-element.33), channel_id=1, source_target_pairs={{0,4},{4,0},{8,12},{12,8},{16,20},{20,16},{24,28},{28,24},{1,5},{5... | collective-permute-start | bytes 1966088 | tf_op jit(solution)/shard_map/ppermute | solution.py:20
  71.8 7.3 %copy-start.6 = (f32[128]{0:T(128)S(1)}, f32[128]{0:T(128)}, u32[]{:S(2)}) copy-start(f32[128]{0:T(128)} %param.15) | copy-start | bytes 1540
  71.8 7.3 %copy-start.7 = (f32[128]{0:T(128)S(1)}, f32[128]{0:T(128)}, u32[]{:S(2)}) copy-start(f32[128]{0:T(128)} %param.16) | copy-start | bytes 1540
  78.8 15.1 %copy-start.4 = (s32[2,2]{1,0:T(2,128)S(1)}, s32[2,2]{1,0:T(2,128)}, u32[]{:S(2)}) copy-start(s32[2,2]{1,0:T(2,128)} %param.18) | copy-start | bytes 52
  78.8 15.4 %copy-start.8 = (s32[2]{0:T(128)S(1)}, s32[2]{0:T(128)}, u32[]{:S(2)}) copy-start(s32[2]{0:T(128)} %param.19) | copy-start | bytes 28
  80.1 13.7 %all-to-all-start = ((f32[32,1,4]{2,1,0:T(1,128)}), f32[32,1,4]{2,1,0:T(1,128)S(1)}, u32[]{:S(2)}, u32[]{:S(2)}) async-start(f32[32,1,4]{2,1,0:T(1,128)} %broadcast_in_dim.37), calls=%async_computation | async-start | bytes 32768 | tf_op jit(solution)/shard_map/all_to_all | solution.py:199
  (3 other events, 12.8 us)

commit v4 on v3

--- a/solution.py
+++ b/solution.py
@@ -9,6 +9,7 @@
 
 BLK = 128
 EARLY_VMEM, LATE_VMEM = 18 << 20, 12 << 20
+HEAD = 3 * BLK // 2
 CORE, X, Y = 1, 2, 4
 
 
@@ -57,19 +58,21 @@
 
 
 def early_kernel(
-    col_slots, own, direct, passed, mine, low, high, first,
+    col_slots, own, direct, passed, mine1, mine2, low, high, first1, first2,
     total, later, panel, weights, dense, slot_at, sems,
 ):
-    depth, split = mine.shape[0], low.shape[1]
+    (depth, split), head = low.shape, mine1.shape[0]
     rows = depth // BLK
 
     @pl.when(pl.program_id(0) == 0)
     def _():
         sources = [
-            (mine, weights.at[0]),
+            (mine1, weights.at[0, :head]),
+            (mine2, weights.at[0, head:]),
             (low, weights.at[1, :, :split]),
             (high, weights.at[1, :, split:]),
-            (first, weights.at[2]),
+            (first1, weights.at[2, :head]),
+            (first2, weights.at[2, head:]),
         ]
         chunks, straight = places()
         count = own.shape[0]
@@ -105,7 +108,7 @@
 
 
 def early_sums(col_slots, tokens, weights):
-    count, (depth, width) = 2 * tokens[0].shape[0], weights[0].shape
+    count, depth, width = 2 * tokens[0].shape[0], weights[2].shape[0], weights[0].shape[1]
     columns = 2 * col_slots.shape[1]
     step = 3 * 2 * BLK if columns % 6 == 0 else 2 * BLK
     return pl.pallas_call(
@@ -115,14 +118,14 @@
             jax.ShapeDtypeStruct((count, columns * BLK), jnp.float32),
             jax.ShapeDtypeStruct((count, depth), jnp.bfloat16),
         ),
-        in_specs=[SMEM] + [ANY] * 7,
+        in_specs=[SMEM] + [ANY] * 9,
         out_specs=(pl.BlockSpec((count, step), lambda n: (0, n)), VMEM),
         scratch_shapes=[
             pltpu.VMEM((count, 3 * depth), jnp.bfloat16),
             pltpu.VMEM((3, depth, width), jnp.bfloat16),
             pltpu.VMEM((3 * depth, step), jnp.bfloat16),
             pltpu.SMEM((3 * depth // BLK, columns), jnp.int32),
-            pltpu.SemaphoreType.DMA((12,)),
+            pltpu.SemaphoreType.DMA((14,)),
         ],
         compiler_params=pltpu.CompilerParams(vmem_limit_bytes=EARLY_VMEM),
         cost_estimate=pl.CostEstimate(
@@ -233,8 +236,15 @@
     quarter = tokens.shape[1] // 4
 
     beside = swap(tokens, CORE, CORE)
-    mine = jnp.where(on_gate, gate_packed, up_packed)
-    first = swap(mine, X, Y)
+    mine = [
+        jnp.where(on_gate, gate_packed[:HEAD], up_packed[:HEAD]),
+        jnp.where(on_gate, gate_packed[HEAD:], up_packed[HEAD:]),
+    ]
+    first = [swap(mine[0], X, Y)]
+    gate_after, up_after, mine[1], first[0] = lax.optimization_barrier(
+        (gate_packed, up_packed, mine[1], first[0])
+    )
+    first.append(swap(mine[1], X, Y))
     start = quarter * jnp.where(on_gate, 2 * (1 - y_at) + plane, 2 * plane + 1 - x_at)
     quarters = [lax.dynamic_slice_in_dim(rows, start, quarter, 1) for rows in (tokens, beside)]
     direct = swap(jnp.concatenate(quarters), Y, X)
@@ -242,7 +252,7 @@
     passed = lax.ppermute(direct, "tp", [(i, i ^ 1) for i in range(lax.axis_size("tp"))])
     split = third * BLK
     low = swap(jnp.where(on_gate, up_packed[:, :split], gate_packed[:, :split]), CORE, CORE)
-    high = swap(jnp.where(on_gate, up_packed[:, split:], gate_packed[:, split:]), CORE, CORE)
+    high = swap(jnp.where(on_gate, up_after[:, split:], gate_after[:, split:]), CORE, CORE)
     far_low = swap(low, X, Y)
     high, passed = lax.optimization_barrier((high, passed))
     far_high = swap(high, X, Y)
@@ -253,7 +263,7 @@
         [lax.dynamic_slice_in_dim(both, at * quarter, quarter, 1) for at in (chip, far_chip)], axis=1
     )
 
-    early, panel = early_sums(col_slots, (own, direct, passed), (mine, low, high, first))
+    early, panel = early_sums(col_slots, (own, direct, passed), (*mine, low, high, *first))
     parts = []
     for n in range(3):
         sources = (far_low,) if n == 0 else (far_low, far_high)

time: 95.1 us -> 93.2 us (0.980)
  waiting for transfers between devices: 33.8 us -> 30.9 us
  starting transfers between devices: 21.7 us -> 23.7 us
  local copies, waits for them, and re-layouts: 5.86 us -> 4.61 us
    ppermute x16 -> x17, waiting for transfers between devices: 19.1 us -> 13.6 us  [swap(): lax.ppermute(value, 'fsdp', [(i, i ^ (core1 if i & CORE else core0)) for...]
    ppermute x1, waiting for transfers between devices: 8.57 us -> 11.1 us  [exchanged_parts(): lax.ppermute(direct, 'tp', [(i, i ^ 1) for i in range(lax.axis_size('tp'))])]
    ppermute x16 -> x17, starting transfers between devices: 13.6 us -> 15.8 us  [swap(): lax.ppermute(value, 'fsdp', [(i, i ^ (core1 if i & CORE else core0)) for...]
    unnamed x20 -> x24, local copies, waits for them, and re-layouts: 1.43 us -> 0.21 us
    select_n x2 -> x3, other arithmetic: 2.4 us -> 2.97 us  [the longest x1 1.48 us: exchanged_parts(): jnp.where(on_gate, gate_packed[:HEAD], up_packed[:HEAD])]
  transfers between devices with their start and end apart: 18 -> 19, of which waited for: 7 -> 9; matrix products, arithmetic and copies ran while one was open for 15% -> 13% of each run, Pallas kernels for 23% -> 24%
where the time goes in v4:
time: 93.2 us; the launch traced here: 92.9 us
  waiting for transfers between devices  30.9 us (33%)
  starting transfers between devices  23.7 us (25%)
  Pallas kernels  22.4 us (24%)
  other arithmetic  9.73 us (10%)
  local copies, waits for them, and re-layouts  4.61 us (5%)
  between operations  0.98 us (1%)
    ppermute x17, starting transfers between devices, swap(): lax.ppermute(value, 'fsdp', [(i, i ^ (core1 if i & CORE else core0)) for...  15.8 us
    ppermute x17, waiting for transfers between devices, swap(): lax.ppermute(value, 'fsdp', [(i, i ^ (core1 if i & CORE else core0)) for...  13.6 us
    pallas_call x1, Pallas kernels, early_sums(): pl.pallas_call(early_kernel, grid=(columns * BLK // step,), out_shape=(ja...  12 us
    ppermute x1, waiting for transfers between devices, exchanged_parts(): lax.ppermute(direct, 'tp', [(i, i ^ 1) for i in range(lax.axis_size('tp'))])  11.1 us
    pallas_call x3, Pallas kernels, late_sums(): pl.pallas_call(functools.partial(late_kernel, first_pair), grid=(pairs,),...  10.4 us
    all_to_all x1, starting transfers between devices, pair_losses(): shares = lax.all_to_all(spread, ('fsdp', 'tp'), 0, 0, tiled=True)  6.31 us
    all_to_all x1, waiting for transfers between devices, pair_losses(): shares = lax.all_to_all(spread, ('fsdp', 'tp'), 0, 0, tiled=True)  6.15 us
    select_n x1, other arithmetic, exchanged_parts(): jnp.where(on_gate, up_packed[:, :split], gate_packed[:, :split])  2.51 us
  transfers between devices with their start and end apart: 19, of which 9 were waited for; matrix products, arithmetic and copies ran while one was open for 13% of the time, Pallas kernels for 24%

profile of v4, /device:TPU:0, one launch (start us, length us, event | category | flops | bytes accessed | tf_op | source)
XLA Modules:
  0.0 92.9 jit_solution(1955609382054438912)
XLA Ops:
  1.2 1.5 %slice_select_fusion.2.mine1 = bf16[192,1920]{1,0:T(8,128)(2,1)S(1)} fusion(bf16[512,1920]{1,0:T(8,128)(2,1)} %param.12, bf16[512,1920]{1,0:T(8,128)(2,1)} %param.11, pred[]{:T(512)S(6)} %eq.19), kind=kLoop, calls=%fused_computation.10 | loop fusion | flops 368640 | bytes 2211841 | tf_op jit(solution)/shard_map/jit(_where)/select_n | solution.py:240
  2.7 2.6 %collective-permute-start.2 = (bf16[192,1920]{1,0:T(8,128)(2,1)S(1)}, bf16[192,1920]{1,0:T(8,128)(2,1)}, u32[]{:S(2)}, u32[]{:S(2)}) collective-permute-start(bf16[192,1920]{1,0:T(8,128)(2,1)S(1)} %slice_select_fusion.2.mine1), channel_id=1, source_target_pairs={{0,8},{4,20},{8,0},{12,28},{16,24},{20,4},{24,16},{28,12},{1,9},{5... | collective-permute-start | bytes 2211848 | tf_op jit(solution)/shard_map/ppermute | solution.py:21
  5.3 2.5 %slice_select_fusion = bf16[512,1280]{1,0:T(8,128)(2,1)} fusion(bf16[512,1920]{1,0:T(8,128)(2,1)} %param.11, bf16[512,1920]{1,0:T(8,128)(2,1)S(1)} %copy-done, pred[]{:T(512)S(6)} %eq.19), kind=kLoop, calls=%fused_computation | loop fusion | flops 655360 | bytes 3932161 | tf_op jit(solution)/shard_map/jit(_where)/select_n | solution.py:254
  10.9 1.4 %collective-permute-start.1 = (bf16[256,1024]{1,0:T(8,128)(2,1)}, bf16[256,1024]{1,0:T(8,128)(2,1)}, u32[]{:S(2)}, u32[]{:S(2)}) collective-permute-start(bf16[256,1024]{1,0:T(8,128)(2,1)} %pad_maximum_fusion.2), channel_id=1, source_target_pairs={{0,16},{4,12},{8,24},{12,4},{16,0},{20,28},{24,8},{28,20},{1,17},{... | collective-permute-start | bytes 1572872 | tf_op jit(solution)/shard_map/ppermute | solution.py:21
  12.7 3.1 %collective-permute-done.2.first1 = bf16[192,1920]{1,0:T(8,128)(2,1)} collective-permute-done((bf16[192,1920]{1,0:T(8,128)(2,1)S(1)}, bf16[192,1920]{1,0:T(8,128)(2,1)}, u32[]{:S(2)}, u32[]{:S(2)}) %collective-permute-start.2) | collective-permute-done | bytes 737312 | tf_op jit(solution)/shard_map/ppermute | solution.py:21
  15.8 1.4 %slice_select_fusion.3 = bf16[512,640]{1,0:T(8,128)(2,1)S(1)} fusion(bf16[512,1920]{1,0:T(8,128)(2,1)} %param.11, bf16[512,1920]{1,0:T(8,128)(2,1)} %param.12, pred[]{:T(512)S(6)} %eq.19), kind=kLoop, calls=%fused_computation.14 | loop fusion | flops 327680 | bytes 1966081 | tf_op jit(solution)/shard_map/jit(_where)/select_n | solution.py:255
  17.2 2.7 %collective-permute-start.6 = (bf16[320,1920]{1,0:T(8,128)(2,1)S(1)}, bf16[320,1920]{1,0:T(8,128)(2,1)S(1)}, u32[]{:S(2)}, u32[]{:S(2)}) collective-permute-start(bf16[320,1920]{1,0:T(8,128)(2,1)S(1)} %slice_select_fusion.1.mine2), channel_id=1, source_target_pairs={{0,8},{4,20},{8,0},{12,28},{16,24},{20,4},{24,16},{28,12},{1,9},{5... | collective-permute-start | bytes 3686408 | tf_op jit(solution)/shard_map/ppermute | solution.py:21
  20.4 1.6 %collective-permute-start.4 = (bf16[256,1024]{1,0:T(8,128)(2,1)}, bf16[256,1024]{1,0:T(8,128)(2,1)S(1)}, u32[]{:S(2)}, u32[]{:S(2)}) collective-permute-start(bf16[256,1024]{1,0:T(8,128)(2,1)} %collective-permute-done.1.direct), channel_id=1, source_target_pairs={{0,1},{1,0},{2,3},{3,2},{4,5},{5,4},{6,7},{7,6},{8,9},{9,8},{10,11... | collective-permute-start | bytes 1572872 | tf_op jit(solution)/shard_map/ppermute | solution.py:252
  22.1 1.3 %constant_dynamic-update-slice_fusion = bf16[256,4096]{1,0:T(8,128)(2,1)S(1)} fusion(bf16[256,4096]{1,0:T(8,128)(2,1)S(1)} %constant_dynamic-update-slice_fusion.1, bf16[128,4096]{1,0:T(8,128)(2,1)} %collective-permute-done), kind=kLoop, calls=%fused_computation.16 | loop fusion | bytes 2097152 | tf_op jit(solution)/shard_map/concatenate | solution.py:261
  23.6 11.1 %collective-permute-done.4.passed = bf16[256,1024]{1,0:T(8,128)(2,1)S(1)} collective-permute-done((bf16[256,1024]{1,0:T(8,128)(2,1)}, bf16[256,1024]{1,0:T(8,128)(2,1)S(1)}, u32[]{:S(2)}, u32[]{:S(2)}) %collective-permute-start.4) | collective-permute-done | bytes 524320 | tf_op jit(solution)/shard_map/ppermute | solution.py:252
  34.7 1.7 %collective-permute-start.11 = (bf16[512,640]{1,0:T(8,128)(2,1)S(1)}, bf16[512,640]{1,0:T(8,128)(2,1)S(1)}, u32[]{:S(2)}, u32[]{:S(2)}) collective-permute-start(bf16[512,640]{1,0:T(8,128)(2,1)S(1)} %collective-permute-done.3.high), channel_id=1, source_target_pairs={{0,8},{4,20},{8,0},{12,28},{16,24},{20,4},{24,16},{28,12},{1,9},{5... | collective-permute-start | bytes 1966088 | tf_op jit(solution)/shard_map/ppermute | solution.py:21
  36.4 12.0 %shard_map.113 = (f32[512,3840]{1,0:T(8,128)S(1)}, bf16[512,512]{1,0:T(8,128)(2,1)S(1)}) custom-call(s32[32,15]{1,0:T(8,128)S(1)} %copy.33.col_slots, bf16[256,2048]{1,0:T(8,128)(2,1)S(1)} %pad_maximum_fusion.own, bf16[256,1024]{1,0:T(8,128)(2,1)} %collective-permute-done.1.direct, bf16[256,1024]{1,0:T(8,128)(2,1)S(1)} %collective-permute-done.4.passed, ...), custom_call_target="tpu_custom_call" | custom-call | flops 6039797760 | bytes 13762560 | tf_op jit(solution)/shard_map/pallas_call | solution.py:114
  48.6 3.4 %shard_map.114 = (f32[128,1280]{1,0:T(8,128)S(1)}, f32[128,1280]{1,0:T(8,128)S(1)}, f32[256,1280]{1,0:T(8,128)S(1)}) custom-call(s32[32,15]{1,0:T(8,128)S(1)} %copy.33.col_slots, bf16[512,512]{1,0:T(8,128)(2,1)S(1)} %get-tuple-element.31.panel, f32[512,3840]{1,0:T(8,128)S(1)} %get-tuple-element.32.early, bf16[512,1280]{1,0:T(8,128)(2,1)S(1)} %collective-permute-done.7.refs_0_), custom_call_target="tpu_custom_call" | custom-call | flops 671088640 | bytes 6553600 | tf_op jit(solution)/shard_map/pallas_call | solution.py:169
  53.1 1.0 %collective-permute-start.8 = (f16[128,1280]{1,0:T(8,128)(2,1)S(1)}, f16[128,1280]{1,0:T(8,128)(2,1)S(1)}, u32[]{:S(2)}, u32[]{:S(2)}) collective-permute-start(f16[128,1280]{1,0:T(8,128)(2,1)S(1)} %get-tuple-element.44), channel_id=1, source_target_pairs={{0,16},{4,12},{8,24},{12,4},{16,0},{20,28},{24,8},{28,20},{1,17},{... | collective-permute-start | bytes 983048 | tf_op jit(solution)/shard_map/ppermute | solution.py:21
  54.4 1.5 %collective-permute-done.11.refs_1_ = bf16[512,640]{1,0:T(8,128)(2,1)S(1)} collective-permute-done((bf16[512,640]{1,0:T(8,128)(2,1)S(1)}, bf16[512,640]{1,0:T(8,128)(2,1)S(1)}, u32[]{:S(2)}, u32[]{:S(2)}) %collective-permute-start.11) | collective-permute-done | bytes 655392 | tf_op jit(solution)/shard_map/ppermute | solution.py:21
  55.9 3.5 %shard_map.115 = (f32[128,1280]{1,0:T(8,128)S(1)}, f32[128,1280]{1,0:T(8,128)S(1)}, f32[256,1280]{1,0:T(8,128)S(1)}) custom-call(s32[32,15]{1,0:T(8,128)S(1)} %copy.33.col_slots, bf16[512,512]{1,0:T(8,128)(2,1)S(1)} %get-tuple-element.31.panel, f32[512,3840]{1,0:T(8,128)S(1)} %get-tuple-element.32.early, ...), custom_call_target="tpu_custom_call" | custom-call | flops 671088640 | bytes 7208960 | tf_op jit(solution)/shard_map/pallas_call | solution.py:169
  59.6 1.9 %collective-permute-start.12 = (f16[128,1280]{1,0:T(8,128)(2,1)S(1)}, f16[128,1280]{1,0:T(8,128)(2,1)S(1)}, u32[]{:S(2)}, u32[]{:S(2)}) collective-permute-start(f16[128,1280]{1,0:T(8,128)(2,1)S(1)} %get-tuple-element.46), channel_id=1, source_target_pairs={{0,16},{4,12},{8,24},{12,4},{16,0},{20,28},{24,8},{28,20},{1,17},{... | collective-permute-start | bytes 983048 | tf_op jit(solution)/shard_map/ppermute | solution.py:21
  62.1 3.5 %shard_map.116 = (f32[128,1280]{1,0:T(8,128)S(1)}, f32[128,1280]{1,0:T(8,128)S(1)}, f32[256,1280]{1,0:T(8,128)S(1)}) custom-call(s32[32,15]{1,0:T(8,128)S(1)} %copy.33.col_slots, bf16[512,512]{1,0:T(8,128)(2,1)S(1)} %get-tuple-element.31.panel, f32[512,3840]{1,0:T(8,128)S(1)} %get-tuple-element.32.early, ...), custom_call_target="tpu_custom_call" | custom-call | flops 671088640 | bytes 7208960 | tf_op jit(solution)/shard_map/pallas_call | solution.py:169
  65.8 1.6 %collective-permute-start.13 = (f32[128,1280]{1,0:T(8,128)S(1)}, f32[128,1280]{1,0:T(8,128)S(1)}, u32[]{:S(2)}, u32[]{:S(2)}) collective-permute-start(f32[128,1280]{1,0:T(8,128)S(1)} %get-tuple-element.38), channel_id=1, source_target_pairs={{0,4},{4,0},{8,12},{12,8},{16,20},{20,16},{24,28},{28,24},{1,5},{5... | collective-permute-start | bytes 1966088 | tf_op jit(solution)/shard_map/ppermute | solution.py:21
  68.2 1.4 %collective-permute-done.14 = f16[128,1280]{1,0:T(8,128)(2,1)S(1)} collective-permute-done((f16[128,1280]{1,0:T(8,128)(2,1)S(1)}, f16[128,1280]{1,0:T(8,128)(2,1)S(1)}, u32[]{:S(2)}, u32[]{:S(2)}) %collective-permute-start.14) | collective-permute-done | bytes 327712 | tf_op jit(solution)/shard_map/ppermute | solution.py:21
  70.2 4.3 %collective-permute-done.15 = f16[128,1280]{1,0:T(8,128)(2,1)S(1)} collective-permute-done((f16[128,1280]{1,0:T(8,128)(2,1)S(1)}, f16[128,1280]{1,0:T(8,128)(2,1)S(1)}, u32[]{:S(2)}, u32[]{:S(2)}) %collective-permute-start.15) | collective-permute-done | bytes 327712 | tf_op jit(solution)/shard_map/ppermute | solution.py:21
  74.4 2.6 %collective-permute-done.17 = f16[128,1280]{1,0:T(8,128)(2,1)S(1)} collective-permute-done((f16[128,1280]{1,0:T(8,128)(2,1)S(1)}, f16[128,1280]{1,0:T(8,128)(2,1)S(1)}, u32[]{:S(2)}, u32[]{:S(2)}) %collective-permute-start.17) | collective-permute-done | bytes 327712 | tf_op jit(solution)/shard_map/ppermute | solution.py:21
  78.4 6.3 %all-to-all-start = ((f32[32,1,4]{2,1,0:T(1,128)}), f32[32,1,4]{2,1,0:T(1,128)S(1)}, u32[]{:S(2)}, u32[]{:S(2)}) async-start(f32[32,1,4]{2,1,0:T(1,128)} %broadcast_in_dim.37), calls=%async_computation | async-start | bytes 32768 | tf_op jit(solution)/shard_map/all_to_all | solution.py:202
  85.7 6.2 %all-to-all-done = f32[32,1,4]{2,1,0:T(1,128)S(1)} async-done(((f32[32,1,4]{2,1,0:T(1,128)}), f32[32,1,4]{2,1,0:T(1,128)S(1)}, u32[]{:S(2)}, u32[]{:S(2)}) %all-to-all-start) | async-done | bytes 544 | tf_op jit(solution)/shard_map/all_to_all | solution.py:202
  (78 shorter events, 11.9 us)
Async XLA Ops:
  0.6 8.5 %collective-permute-start = (bf16[128,4096]{1,0:T(8,128)(2,1)}, bf16[128,4096]{1,0:T(8,128)(2,1)}, u32[]{:S(2)}, u32[]{:S(2)}) collective-permute-start(bf16[128,4096]{1,0:T(8,128)(2,1)} %param.10), channel_id=1, source_target_pairs={{0,4},{4,0},{8,12},{12,8},{16,20},{20,16},{24,28},{28,24},{1,5},{5... | collective-permute-start | bytes 3145736 | tf_op jit(solution)/shard_map/ppermute | solution.py:21
  2.7 13.1 %collective-permute-start.2 = (bf16[192,1920]{1,0:T(8,128)(2,1)S(1)}, bf16[192,1920]{1,0:T(8,128)(2,1)}, u32[]{:S(2)}, u32[]{:S(2)}) collective-permute-start(bf16[192,1920]{1,0:T(8,128)(2,1)S(1)} %slice_select_fusion.2.mine1), channel_id=1, source_target_pairs={{0,8},{4,20},{8,0},{12,28},{16,24},{20,4},{24,16},{28,12},{1,9},{5... | collective-permute-start | bytes 2211848 | tf_op jit(solution)/shard_map/ppermute | solution.py:21
  7.8 12.0 %collective-permute-start.5 = (bf16[512,1280]{1,0:T(8,128)(2,1)}, bf16[512,1280]{1,0:T(8,128)(2,1)S(1)}, u32[]{:S(2)}, u32[]{:S(2)}) collective-permute-start(bf16[512,1280]{1,0:T(8,128)(2,1)} %slice_select_fusion), channel_id=1, source_target_pairs={{0,4},{4,0},{8,12},{12,8},{16,20},{20,16},{24,28},{28,24},{1,5},{5... | collective-permute-start | bytes 3932168 | tf_op jit(solution)/shard_map/ppermute | solution.py:21
  10.9 9.5 %collective-permute-start.1 = (bf16[256,1024]{1,0:T(8,128)(2,1)}, bf16[256,1024]{1,0:T(8,128)(2,1)}, u32[]{:S(2)}, u32[]{:S(2)}) collective-permute-start(bf16[256,1024]{1,0:T(8,128)(2,1)} %pad_maximum_fusion.2), channel_id=1, source_target_pairs={{0,16},{4,12},{8,24},{12,4},{16,0},{20,28},{24,8},{28,20},{1,17},{... | collective-permute-start | bytes 1572872 | tf_op jit(solution)/shard_map/ppermute | solution.py:21
  12.7 9.3 %copy-start.3 = (bf16[128,4096]{1,0:T(8,128)(2,1)S(1)}, bf16[128,4096]{1,0:T(8,128)(2,1)}, u32[]{:S(2)}) copy-start(bf16[128,4096]{1,0:T(8,128)(2,1)} %param.10) | copy-start | bytes 3145732
  17.1 6.5 %collective-permute-start.3 = (bf16[512,640]{1,0:T(8,128)(2,1)S(1)}, bf16[512,640]{1,0:T(8,128)(2,1)S(1)}, u32[]{:S(2)}, u32[]{:S(2)}) collective-permute-start(bf16[512,640]{1,0:T(8,128)(2,1)S(1)} %slice_select_fusion.3), channel_id=1, source_target_pairs={{0,4},{4,0},{8,12},{12,8},{16,20},{20,16},{24,28},{28,24},{1,5},{5... | collective-permute-start | bytes 1966088 | tf_op jit(solution)/shard_map/ppermute | solution.py:21
  17.2 19.2 %collective-permute-start.6 = (bf16[320,1920]{1,0:T(8,128)(2,1)S(1)}, bf16[320,1920]{1,0:T(8,128)(2,1)S(1)}, u32[]{:S(2)}, u32[]{:S(2)}) collective-permute-start(bf16[320,1920]{1,0:T(8,128)(2,1)S(1)} %slice_select_fusion.1.mine2), channel_id=1, source_target_pairs={{0,8},{4,20},{8,0},{12,28},{16,24},{20,4},{24,16},{28,12},{1,9},{5... | collective-permute-start | bytes 3686408 | tf_op jit(solution)/shard_map/ppermute | solution.py:21
  19.9 28.8 %collective-permute-start.7 = (bf16[512,1280]{1,0:T(8,128)(2,1)S(1)}, bf16[512,1280]{1,0:T(8,128)(2,1)S(1)}, u32[]{:S(2)}, u32[]{:S(2)}) collective-permute-start(bf16[512,1280]{1,0:T(8,128)(2,1)S(1)} %collective-permute-done.5.low), channel_id=1, source_target_pairs={{0,8},{4,20},{8,0},{12,28},{16,24},{20,4},{24,16},{28,12},{1,9},{5... | collective-permute-start | bytes 3932168 | tf_op jit(solution)/shard_map/ppermute | solution.py:21
  20.4 14.3 %collective-permute-start.4 = (bf16[256,1024]{1,0:T(8,128)(2,1)}, bf16[256,1024]{1,0:T(8,128)(2,1)S(1)}, u32[]{:S(2)}, u32[]{:S(2)}) collective-permute-start(bf16[256,1024]{1,0:T(8,128)(2,1)} %collective-permute-done.1.direct), channel_id=1, source_target_pairs={{0,1},{1,0},{2,3},{3,2},{4,5},{5,4},{6,7},{7,6},{8,9},{9,8},{10,11... | collective-permute-start | bytes 1572872 | tf_op jit(solution)/shard_map/ppermute | solution.py:252
  34.7 21.2 %collective-permute-start.11 = (bf16[512,640]{1,0:T(8,128)(2,1)S(1)}, bf16[512,640]{1,0:T(8,128)(2,1)S(1)}, u32[]{:S(2)}, u32[]{:S(2)}) collective-permute-start(bf16[512,640]{1,0:T(8,128)(2,1)S(1)} %collective-permute-done.3.high), channel_id=1, source_target_pairs={{0,8},{4,20},{8,0},{12,28},{16,24},{20,4},{24,16},{28,12},{1,9},{5... | collective-permute-start | bytes 1966088 | tf_op jit(solution)/shard_map/ppermute | solution.py:21
  52.2 13.6 %collective-permute-start.10 = (f16[128,1280]{1,0:T(8,128)(2,1)S(1)}, f16[128,1280]{1,0:T(8,128)(2,1)S(1)}, u32[]{:S(2)}, u32[]{:S(2)}) collective-permute-start(f16[128,1280]{1,0:T(8,128)(2,1)S(1)} %get-tuple-element.45), channel_id=1, source_target_pairs={{0,20},{4,8},{8,28},{12,0},{16,4},{20,24},{24,12},{28,16},{1,21},{... | collective-permute-start | bytes 983048 | tf_op jit(solution)/shard_map/ppermute | solution.py:21
  53.1 14.3 %collective-permute-start.8 = (f16[128,1280]{1,0:T(8,128)(2,1)S(1)}, f16[128,1280]{1,0:T(8,128)(2,1)S(1)}, u32[]{:S(2)}, u32[]{:S(2)}) collective-permute-start(f16[128,1280]{1,0:T(8,128)(2,1)S(1)} %get-tuple-element.44), channel_id=1, source_target_pairs={{0,16},{4,12},{8,24},{12,4},{16,0},{20,28},{24,8},{28,20},{1,17},{... | collective-permute-start | bytes 983048 | tf_op jit(solution)/shard_map/ppermute | solution.py:21
  54.1 13.5 %collective-permute-start.9 = (f32[128,1280]{1,0:T(8,128)S(1)}, f32[128,1280]{1,0:T(8,128)S(1)}, u32[]{:S(2)}, u32[]{:S(2)}) collective-permute-start(f32[128,1280]{1,0:T(8,128)S(1)} %get-tuple-element.35), channel_id=1, source_target_pairs={{0,4},{4,0},{8,12},{12,8},{16,20},{20,16},{24,28},{28,24},{1,5},{5... | collective-permute-start | bytes 1966088 | tf_op jit(solution)/shard_map/ppermute | solution.py:21
  59.6 8.4 %collective-permute-start.12 = (f16[128,1280]{1,0:T(8,128)(2,1)S(1)}, f16[128,1280]{1,0:T(8,128)(2,1)S(1)}, u32[]{:S(2)}, u32[]{:S(2)}) collective-permute-start(f16[128,1280]{1,0:T(8,128)(2,1)S(1)} %get-tuple-element.46), channel_id=1, source_target_pairs={{0,16},{4,12},{8,24},{12,4},{16,0},{20,28},{24,8},{28,20},{1,17},{... | collective-permute-start | bytes 983048 | tf_op jit(solution)/shard_map/ppermute | solution.py:21
  61.5 8.2 %collective-permute-start.14 = (f16[128,1280]{1,0:T(8,128)(2,1)S(1)}, f16[128,1280]{1,0:T(8,128)(2,1)S(1)}, u32[]{:S(2)}, u32[]{:S(2)}) collective-permute-start(f16[128,1280]{1,0:T(8,128)(2,1)S(1)} %get-tuple-element.47), channel_id=1, source_target_pairs={{0,20},{4,8},{8,28},{12,0},{16,4},{20,24},{24,12},{28,16},{1,21},{... | collective-permute-start | bytes 983048 | tf_op jit(solution)/shard_map/ppermute | solution.py:21
  65.8 3.9 %collective-permute-start.13 = (f32[128,1280]{1,0:T(8,128)S(1)}, f32[128,1280]{1,0:T(8,128)S(1)}, u32[]{:S(2)}, u32[]{:S(2)}) collective-permute-start(f32[128,1280]{1,0:T(8,128)S(1)} %get-tuple-element.38), channel_id=1, source_target_pairs={{0,4},{4,0},{8,12},{12,8},{16,20},{20,16},{24,28},{28,24},{1,5},{5... | collective-permute-start | bytes 1966088 | tf_op jit(solution)/shard_map/ppermute | solution.py:21
  67.4 7.1 %collective-permute-start.15 = (f16[128,1280]{1,0:T(8,128)(2,1)S(1)}, f16[128,1280]{1,0:T(8,128)(2,1)S(1)}, u32[]{:S(2)}, u32[]{:S(2)}) collective-permute-start(f16[128,1280]{1,0:T(8,128)(2,1)S(1)} %get-tuple-element.48), channel_id=1, source_target_pairs={{0,16},{4,12},{8,24},{12,4},{16,0},{20,28},{24,8},{28,20},{1,17},{... | collective-permute-start | bytes 983048 | tf_op jit(solution)/shard_map/ppermute | solution.py:21
  67.6 9.5 %collective-permute-start.17 = (f16[128,1280]{1,0:T(8,128)(2,1)S(1)}, f16[128,1280]{1,0:T(8,128)(2,1)S(1)}, u32[]{:S(2)}, u32[]{:S(2)}) collective-permute-start(f16[128,1280]{1,0:T(8,128)(2,1)S(1)} %get-tuple-element.49), channel_id=1, source_target_pairs={{0,20},{4,8},{8,28},{12,0},{16,4},{20,24},{24,12},{28,16},{1,21},{... | collective-permute-start | bytes 983048 | tf_op jit(solution)/shard_map/ppermute | solution.py:21
  68.1 9.0 %collective-permute-start.16 = (f32[128,1280]{1,0:T(8,128)S(1)}, f32[128,1280]{1,0:T(8,128)S(1)}, u32[]{:S(2)}, u32[]{:S(2)}) collective-permute-start(f32[128,1280]{1,0:T(8,128)S(1)} %get-tuple-element.41), channel_id=1, source_target_pairs={{0,4},{4,0},{8,12},{12,8},{16,20},{20,16},{24,28},{28,24},{1,5},{5... | collective-permute-start | bytes 1966088 | tf_op jit(solution)/shard_map/ppermute | solution.py:21
  69.7 7.7 %copy-start.8 = (f32[128]{0:T(128)S(1)}, f32[128]{0:T(128)}, u32[]{:S(2)}) copy-start(f32[128]{0:T(128)} %param.15) | copy-start | bytes 1540
  69.7 7.7 %copy-start.9 = (f32[128]{0:T(128)S(1)}, f32[128]{0:T(128)}, u32[]{:S(2)}) copy-start(f32[128]{0:T(128)} %param.16) | copy-start | bytes 1540
  77.1 14.9 %copy-start.6 = (s32[2,2]{1,0:T(2,128)S(1)}, s32[2,2]{1,0:T(2,128)}, u32[]{:S(2)}) copy-start(s32[2,2]{1,0:T(2,128)} %param.18) | copy-start | bytes 52
  77.1 15.3 %copy-start.10 = (s32[2]{0:T(128)S(1)}, s32[2]{0:T(128)}, u32[]{:S(2)}) copy-start(s32[2]{0:T(128)} %param.19) | copy-start | bytes 28
  78.4 13.5 %all-to-all-start = ((f32[32,1,4]{2,1,0:T(1,128)}), f32[32,1,4]{2,1,0:T(1,128)S(1)}, u32[]{:S(2)}, u32[]{:S(2)}) async-start(f32[32,1,4]{2,1,0:T(1,128)} %broadcast_in_dim.37), calls=%async_computation | async-start | bytes 32768 | tf_op jit(solution)/shard_map/all_to_all | solution.py:202
  (6 other events, 28.2 us)

commit v5 on v4

--- a/solution.py
+++ b/solution.py
@@ -136,25 +136,25 @@
     )(col_slots, *tokens, *weights)
 
 
-def late_kernel(first_pair, col_slots, panel, early, *refs):
-    parts, (mine, beside, near, weights, dense, slot_at, sems) = refs[:-7], refs[-7:]
-    depth = weights.shape[0]
-    rows = depth // BLK
+def late_kernel(first_column, col_slots, panel, early, *refs):
+    parts, (mine, beside, near, dense, slot_at) = refs[:-5], refs[-5:]
+    rows, lasts = panel.shape[1] // BLK, [part.shape[1] // BLK for part in parts]
 
     @pl.when(pl.program_id(0) == 0)
     def _():
-        copies, start = [], 0
-        for i, part in enumerate(parts):
-            stop = start + part.shape[1]
-            copies.append(pltpu.make_async_copy(part, weights.at[:, start:stop], sems.at[i]))
-            start = stop
-        for copy in copies:
-            copy.start()
         find_slots(slot_at, col_slots, places()[0][3] * rows, rows, 0)
-        for copy in copies:
-            copy.wait()
-
-    fill_dense(dense, weights, slot_at, 0, 2 * (first_pair + pl.program_id(0)))
+
+    column = first_column + dense.shape[1] // BLK * pl.program_id(0)
+    for r in range(rows):
+        at_rows = slice(r * BLK, (r + 1) * BLK)
+        for h in range(dense.shape[1] // BLK):
+            slot = slot_at[r, column + h]
+            block, before = jnp.zeros((BLK, BLK), dense.dtype), 0
+            for part, count in zip(parts, lasts):
+                at = pl.multiple_of(jnp.clip(slot - before, 0, count - 1) * BLK, BLK)
+                block = jnp.where(slot >= before, part[at_rows, pl.ds(at, BLK)], block)
+                before += count
+            dense[at_rows, h * BLK : (h + 1) * BLK] = block
     total = early[...] + jnp.dot(panel[...], dense[...], preferred_element_type=jnp.float32)
     count = mine.shape[0]
     mine[...] = total[:count]
@@ -166,20 +166,20 @@
     count, depth = panel.shape
     width = sum(part.shape[1] for part in parts)
     out_rows = (count // 4, count // 4, count // 2)
+    step = pairs * BLK
+    first = 2 * first_pair * BLK // step
     return pl.pallas_call(
-        functools.partial(late_kernel, first_pair),
-        grid=(pairs,),
+        functools.partial(late_kernel, 2 * first_pair),
+        grid=(pairs * 2 * BLK // step,),
         out_shape=[
             jax.ShapeDtypeStruct((rows, pairs * 2 * BLK), jnp.float32) for rows in out_rows
         ],
-        in_specs=[SMEM, VMEM, pl.BlockSpec((count, 2 * BLK), lambda n: (0, first_pair + n))]
-        + [ANY] * len(parts),
-        out_specs=[pl.BlockSpec((rows, 2 * BLK), lambda n: (0, n)) for rows in out_rows],
+        in_specs=[SMEM, VMEM, pl.BlockSpec((count, step), lambda n: (0, first + n))]
+        + [VMEM] * len(parts),
+        out_specs=[pl.BlockSpec((rows, step), lambda n: (0, n)) for rows in out_rows],
         scratch_shapes=[
-            pltpu.VMEM((depth, width), jnp.bfloat16),
-            pltpu.VMEM((depth, 2 * BLK), jnp.bfloat16),
+            pltpu.VMEM((depth, step), jnp.bfloat16),
             pltpu.SMEM((depth // BLK, 2 * col_slots.shape[1]), jnp.int32),
-            pltpu.SemaphoreType.DMA((len(parts),)),
         ],
         compiler_params=pltpu.CompilerParams(vmem_limit_bytes=LATE_VMEM),
         cost_estimate=pl.CostEstimate(
@@ -235,19 +235,21 @@
     third = 2 * slot_count // 3
     quarter = tokens.shape[1] // 4
 
-    beside = swap(tokens, CORE, CORE)
     mine = [
         jnp.where(on_gate, gate_packed[:HEAD], up_packed[:HEAD]),
         jnp.where(on_gate, gate_packed[HEAD:], up_packed[HEAD:]),
     ]
+    tokens, mine[0] = lax.optimization_barrier((tokens, mine[0]))
+    beside = swap(tokens, CORE, CORE)
     first = [swap(mine[0], X, Y)]
-    gate_after, up_after, mine[1], first[0] = lax.optimization_barrier(
-        (gate_packed, up_packed, mine[1], first[0])
-    )
+    mine[1], first[0] = lax.optimization_barrier((mine[1], first[0]))
     first.append(swap(mine[1], X, Y))
     start = quarter * jnp.where(on_gate, 2 * (1 - y_at) + plane, 2 * plane + 1 - x_at)
     quarters = [lax.dynamic_slice_in_dim(rows, start, quarter, 1) for rows in (tokens, beside)]
-    direct = swap(jnp.concatenate(quarters), Y, X)
+    gate_after, up_after, quarters = lax.optimization_barrier(
+        (gate_packed, up_packed, jnp.concatenate(quarters))
+    )
+    direct = swap(quarters, Y, X)
     tokens_after, beside, direct = lax.optimization_barrier((tokens, beside, direct))
     passed = lax.ppermute(direct, "tp", [(i, i ^ 1) for i in range(lax.axis_size("tp"))])
     split = third * BLK

time: 93.2 us -> 91.9 us (0.986)
  Pallas kernels: 22.4 us -> 20.2 us
  waiting for transfers between devices: 30.9 us -> 32.5 us
    ppermute x17, waiting for transfers between devices: 13.6 us -> 17 us  [swap(): lax.ppermute(value, 'fsdp', [(i, i ^ (core1 if i & CORE else core0)) for...]
    pallas_call x3, Pallas kernels: 10.4 us -> 8.25 us  [late_sums(): pl.pallas_call(functools.partial(late_kernel, 2 * first_pair), grid=(pair...]
    ppermute x1, waiting for transfers between devices: 11.1 us -> 9.39 us  [exchanged_parts(): lax.ppermute(direct, 'tp', [(i, i ^ 1) for i in range(lax.axis_size('tp'))])]
  transfers between devices with their start and end apart: 19 -> 19, of which waited for: 9 -> 8; matrix products, arithmetic and copies ran while one was open for 13% -> 12% of each run, Pallas kernels for 24% -> 22%
where the time goes in v5:
time: 91.9 us; the launch traced here: 91.6 us
  waiting for transfers between devices  32.5 us (35%)
  starting transfers between devices  22.8 us (25%)
  Pallas kernels  20.2 us (22%)
  other arithmetic  9.81 us (11%)
  local copies, waits for them, and re-layouts  4.61 us (5%)
  between operations  1.01 us (1%)
    ppermute x17, waiting for transfers between devices, swap(): lax.ppermute(value, 'fsdp', [(i, i ^ (core1 if i & CORE else core0)) for...  17 us
    ppermute x17, starting transfers between devices, swap(): lax.ppermute(value, 'fsdp', [(i, i ^ (core1 if i & CORE else core0)) for...  15.5 us
    pallas_call x1, Pallas kernels, early_sums(): pl.pallas_call(early_kernel, grid=(columns * BLK // step,), out_shape=(ja...  12 us
    ppermute x1, waiting for transfers between devices, exchanged_parts(): lax.ppermute(direct, 'tp', [(i, i ^ 1) for i in range(lax.axis_size('tp'))])  9.39 us
    pallas_call x3, Pallas kernels, late_sums(): pl.pallas_call(functools.partial(late_kernel, 2 * first_pair), grid=(pair...  8.25 us
    all_to_all x1, waiting for transfers between devices, pair_losses(): shares = lax.all_to_all(spread, ('fsdp', 'tp'), 0, 0, tiled=True)  6.15 us
    all_to_all x1, starting transfers between devices, pair_losses(): shares = lax.all_to_all(spread, ('fsdp', 'tp'), 0, 0, tiled=True)  5.89 us
    select_n x1, other arithmetic, exchanged_parts(): jnp.where(on_gate, up_packed[:, :split], gate_packed[:, :split])  2.51 us
  transfers between devices with their start and end apart: 19, of which 8 were waited for; matrix products, arithmetic and copies ran while one was open for 12% of the time, Pallas kernels for 22%

profile of v5, /device:TPU:0, one launch (start us, length us, event | category | flops | bytes accessed | tf_op | source)
XLA Modules:
  0.0 91.6 jit_solution(17257220209343054844)
XLA Ops:
  0.6 1.6 %slice_select_fusion.2.mine1 = bf16[192,1920]{1,0:T(8,128)(2,1)S(1)} fusion(bf16[512,1920]{1,0:T(8,128)(2,1)} %param.12, bf16[512,1920]{1,0:T(8,128)(2,1)} %param.11, pred[]{:T(512)S(6)} %eq.19), kind=kLoop, calls=%fused_computation.10 | loop fusion | flops 368640 | bytes 2211841 | tf_op jit(solution)/shard_map/jit(_where)/select_n | solution.py:239
  2.8 2.6 %collective-permute-start.4 = (bf16[192,1920]{1,0:T(8,128)(2,1)S(1)}, bf16[192,1920]{1,0:T(8,128)(2,1)}, u32[]{:S(2)}, u32[]{:S(2)}) collective-permute-start(bf16[192,1920]{1,0:T(8,128)(2,1)S(1)} %slice_select_fusion.2.mine1), channel_id=1, source_target_pairs={{0,8},{4,20},{8,0},{12,28},{16,24},{20,4},{24,16},{28,12},{1,9},{5... | collective-permute-start | bytes 2211848 | tf_op jit(solution)/shard_map/ppermute | solution.py:21
  5.3 2.5 %slice_select_fusion = bf16[512,1280]{1,0:T(8,128)(2,1)} fusion(bf16[512,1920]{1,0:T(8,128)(2,1)} %param.11, bf16[512,1920]{1,0:T(8,128)(2,1)S(1)} %copy-done, pred[]{:T(512)S(6)} %eq.19), kind=kLoop, calls=%fused_computation | loop fusion | flops 655360 | bytes 3932161 | tf_op jit(solution)/shard_map/jit(_where)/select_n | solution.py:256
  11.0 1.4 %collective-permute-start.1 = (bf16[256,1024]{1,0:T(8,128)(2,1)}, bf16[256,1024]{1,0:T(8,128)(2,1)}, u32[]{:S(2)}, u32[]{:S(2)}) collective-permute-start(bf16[256,1024]{1,0:T(8,128)(2,1)} %pad_maximum_fusion.2), channel_id=1, source_target_pairs={{0,16},{4,12},{8,24},{12,4},{16,0},{20,28},{24,8},{28,20},{1,17},{... | collective-permute-start | bytes 1572872 | tf_op jit(solution)/shard_map/ppermute | solution.py:21
  12.7 3.0 %collective-permute-done.4.first1 = bf16[192,1920]{1,0:T(8,128)(2,1)} collective-permute-done((bf16[192,1920]{1,0:T(8,128)(2,1)S(1)}, bf16[192,1920]{1,0:T(8,128)(2,1)}, u32[]{:S(2)}, u32[]{:S(2)}) %collective-permute-start.4) | collective-permute-done | bytes 737312 | tf_op jit(solution)/shard_map/ppermute | solution.py:21
  15.7 2.6 %collective-permute-start.6 = (bf16[320,1920]{1,0:T(8,128)(2,1)S(1)}, bf16[320,1920]{1,0:T(8,128)(2,1)S(1)}, u32[]{:S(2)}, u32[]{:S(2)}) collective-permute-start(bf16[320,1920]{1,0:T(8,128)(2,1)S(1)} %slice_select_fusion.1.mine2), channel_id=1, source_target_pairs={{0,8},{4,20},{8,0},{12,28},{16,24},{20,4},{24,16},{28,12},{1,9},{5... | collective-permute-start | bytes 3686408 | tf_op jit(solution)/shard_map/ppermute | solution.py:21
  18.3 1.4 %slice_select_fusion.3 = bf16[512,640]{1,0:T(8,128)(2,1)S(1)} fusion(bf16[512,1920]{1,0:T(8,128)(2,1)} %param.11, bf16[512,1920]{1,0:T(8,128)(2,1)} %param.12, pred[]{:T(512)S(6)} %eq.19), kind=kLoop, calls=%fused_computation.14 | loop fusion | flops 327680 | bytes 1966081 | tf_op jit(solution)/shard_map/jit(_where)/select_n | solution.py:257
  19.8 3.6 %collective-permute-done.1.direct = bf16[256,1024]{1,0:T(8,128)(2,1)} collective-permute-done((bf16[256,1024]{1,0:T(8,128)(2,1)}, bf16[256,1024]{1,0:T(8,128)(2,1)}, u32[]{:S(2)}, u32[]{:S(2)}) %collective-permute-start.1) | collective-permute-done | bytes 524320 | tf_op jit(solution)/shard_map/ppermute | solution.py:21
  23.4 1.4 %collective-permute-start.3 = (bf16[256,1024]{1,0:T(8,128)(2,1)}, bf16[256,1024]{1,0:T(8,128)(2,1)S(1)}, u32[]{:S(2)}, u32[]{:S(2)}) collective-permute-start(bf16[256,1024]{1,0:T(8,128)(2,1)} %collective-permute-done.1.direct), channel_id=1, source_target_pairs={{0,1},{1,0},{2,3},{3,2},{4,5},{5,4},{6,7},{7,6},{8,9},{9,8},{10,11... | collective-permute-start | bytes 1572872 | tf_op jit(solution)/shard_map/ppermute | solution.py:254
  24.9 1.3 %constant_dynamic-update-slice_fusion = bf16[256,4096]{1,0:T(8,128)(2,1)S(1)} fusion(bf16[256,4096]{1,0:T(8,128)(2,1)S(1)} %constant_dynamic-update-slice_fusion.1, bf16[128,4096]{1,0:T(8,128)(2,1)} %collective-permute-done), kind=kLoop, calls=%fused_computation.16 | loop fusion | bytes 2097152 | tf_op jit(solution)/shard_map/concatenate | solution.py:263
  26.4 9.4 %collective-permute-done.3.passed = bf16[256,1024]{1,0:T(8,128)(2,1)S(1)} collective-permute-done((bf16[256,1024]{1,0:T(8,128)(2,1)}, bf16[256,1024]{1,0:T(8,128)(2,1)S(1)}, u32[]{:S(2)}, u32[]{:S(2)}) %collective-permute-start.3) | collective-permute-done | bytes 524320 | tf_op jit(solution)/shard_map/ppermute | solution.py:254
  35.8 1.3 %collective-permute-start.11 = (bf16[512,640]{1,0:T(8,128)(2,1)S(1)}, bf16[512,640]{1,0:T(8,128)(2,1)S(1)}, u32[]{:S(2)}, u32[]{:S(2)}) collective-permute-start(bf16[512,640]{1,0:T(8,128)(2,1)S(1)} %collective-permute-done.2.high), channel_id=1, source_target_pairs={{0,8},{4,20},{8,0},{12,28},{16,24},{20,4},{24,16},{28,12},{1,9},{5... | collective-permute-start | bytes 1966088 | tf_op jit(solution)/shard_map/ppermute | solution.py:21
  37.1 12.0 %shard_map.113 = (f32[512,3840]{1,0:T(8,128)S(1)}, bf16[512,512]{1,0:T(8,128)(2,1)S(1)}) custom-call(s32[32,15]{1,0:T(8,128)S(1)} %copy.33.col_slots, bf16[256,2048]{1,0:T(8,128)(2,1)S(1)} %pad_maximum_fusion.own, bf16[256,1024]{1,0:T(8,128)(2,1)} %collective-permute-done.1.direct, bf16[256,1024]{1,0:T(8,128)(2,1)S(1)} %collective-permute-done.3.passed, ...), custom_call_target="tpu_custom_call" | custom-call | flops 6039797760 | bytes 13762560 | tf_op jit(solution)/shard_map/pallas_call | solution.py:114
  49.2 2.7 %shard_map.114 = (f32[128,1280]{1,0:T(8,128)S(1)}, f32[128,1280]{1,0:T(8,128)S(1)}, f32[256,1280]{1,0:T(8,128)S(1)}) custom-call(s32[32,15]{1,0:T(8,128)S(1)} %copy.33.col_slots, bf16[512,512]{1,0:T(8,128)(2,1)S(1)} %get-tuple-element.37.panel, f32[512,3840]{1,0:T(8,128)S(1)} %get-tuple-element.38.early, bf16[512,1280]{1,0:T(8,128)(2,1)S(1)} %collective-permute-done.7.refs_0_), custom_call_target="tpu_custom_call" | custom-call | flops 671088640 | bytes 6553600 | tf_op jit(solution)/shard_map/pallas_call | solution.py:171
  52.1 1.3 %collective-permute-start.8 = (f16[128,1280]{1,0:T(8,128)(2,1)S(1)}, f16[128,1280]{1,0:T(8,128)(2,1)S(1)}, u32[]{:S(2)}, u32[]{:S(2)}) collective-permute-start(f16[128,1280]{1,0:T(8,128)(2,1)S(1)} %get-tuple-element.50), channel_id=1, source_target_pairs={{0,16},{4,12},{8,24},{12,4},{16,0},{20,28},{24,8},{28,20},{1,17},{... | collective-permute-start | bytes 983048 | tf_op jit(solution)/shard_map/ppermute | solution.py:21
  54.8 2.8 %shard_map.115 = (f32[128,1280]{1,0:T(8,128)S(1)}, f32[128,1280]{1,0:T(8,128)S(1)}, f32[256,1280]{1,0:T(8,128)S(1)}) custom-call(s32[32,15]{1,0:T(8,128)S(1)} %copy.33.col_slots, bf16[512,512]{1,0:T(8,128)(2,1)S(1)} %get-tuple-element.37.panel, f32[512,3840]{1,0:T(8,128)S(1)} %get-tuple-element.38.early, ...), custom_call_target="tpu_custom_call" | custom-call | flops 671088640 | bytes 7208960 | tf_op jit(solution)/shard_map/pallas_call | solution.py:171
  57.8 2.1 %collective-permute-start.12 = (f16[128,1280]{1,0:T(8,128)(2,1)S(1)}, f16[128,1280]{1,0:T(8,128)(2,1)S(1)}, u32[]{:S(2)}, u32[]{:S(2)}) collective-permute-start(f16[128,1280]{1,0:T(8,128)(2,1)S(1)} %get-tuple-element.52), channel_id=1, source_target_pairs={{0,16},{4,12},{8,24},{12,4},{16,0},{20,28},{24,8},{28,20},{1,17},{... | collective-permute-start | bytes 983048 | tf_op jit(solution)/shard_map/ppermute | solution.py:21
  60.8 2.8 %shard_map.116 = (f32[128,1280]{1,0:T(8,128)S(1)}, f32[128,1280]{1,0:T(8,128)S(1)}, f32[256,1280]{1,0:T(8,128)S(1)}) custom-call(s32[32,15]{1,0:T(8,128)S(1)} %copy.33.col_slots, bf16[512,512]{1,0:T(8,128)(2,1)S(1)} %get-tuple-element.37.panel, f32[512,3840]{1,0:T(8,128)S(1)} %get-tuple-element.38.early, ...), custom_call_target="tpu_custom_call" | custom-call | flops 671088640 | bytes 7208960 | tf_op jit(solution)/shard_map/pallas_call | solution.py:171
  63.8 1.2 %collective-permute-start.13 = (f32[128,1280]{1,0:T(8,128)S(1)}, f32[128,1280]{1,0:T(8,128)S(1)}, u32[]{:S(2)}, u32[]{:S(2)}) collective-permute-start(f32[128,1280]{1,0:T(8,128)S(1)} %get-tuple-element.44), channel_id=1, source_target_pairs={{0,4},{4,0},{8,12},{12,8},{16,20},{20,16},{24,28},{28,24},{1,5},{5... | collective-permute-start | bytes 1966088 | tf_op jit(solution)/shard_map/ppermute | solution.py:21
  66.2 3.0 %collective-permute-done.14 = f16[128,1280]{1,0:T(8,128)(2,1)S(1)} collective-permute-done((f16[128,1280]{1,0:T(8,128)(2,1)S(1)}, f16[128,1280]{1,0:T(8,128)(2,1)S(1)}, u32[]{:S(2)}, u32[]{:S(2)}) %collective-permute-start.14) | collective-permute-done | bytes 327712 | tf_op jit(solution)/shard_map/ppermute | solution.py:21
  69.6 2.8 %collective-permute-done.15 = f16[128,1280]{1,0:T(8,128)(2,1)S(1)} collective-permute-done((f16[128,1280]{1,0:T(8,128)(2,1)S(1)}, f16[128,1280]{1,0:T(8,128)(2,1)S(1)}, u32[]{:S(2)}, u32[]{:S(2)}) %collective-permute-start.15) | collective-permute-done | bytes 327712 | tf_op jit(solution)/shard_map/ppermute | solution.py:21
  72.5 3.7 %collective-permute-done.17 = f16[128,1280]{1,0:T(8,128)(2,1)S(1)} collective-permute-done((f16[128,1280]{1,0:T(8,128)(2,1)S(1)}, f16[128,1280]{1,0:T(8,128)(2,1)S(1)}, u32[]{:S(2)}, u32[]{:S(2)}) %collective-permute-start.17) | collective-permute-done | bytes 327712 | tf_op jit(solution)/shard_map/ppermute | solution.py:21
  77.5 5.9 %all-to-all-start = ((f32[32,1,4]{2,1,0:T(1,128)}), f32[32,1,4]{2,1,0:T(1,128)S(1)}, u32[]{:S(2)}, u32[]{:S(2)}) async-start(f32[32,1,4]{2,1,0:T(1,128)} %broadcast_in_dim.37), calls=%async_computation | async-start | bytes 32768 | tf_op jit(solution)/shard_map/all_to_all | solution.py:202
  84.4 6.2 %all-to-all-done = f32[32,1,4]{2,1,0:T(1,128)S(1)} async-done(((f32[32,1,4]{2,1,0:T(1,128)}), f32[32,1,4]{2,1,0:T(1,128)S(1)}, u32[]{:S(2)}, u32[]{:S(2)}) %all-to-all-start) | async-done | bytes 544 | tf_op jit(solution)/shard_map/all_to_all | solution.py:202
  (78 shorter events, 12.2 us)
Async XLA Ops:
  2.2 7.0 %collective-permute-start = (bf16[128,4096]{1,0:T(8,128)(2,1)}, bf16[128,4096]{1,0:T(8,128)(2,1)}, u32[]{:S(2)}, u32[]{:S(2)}) collective-permute-start(bf16[128,4096]{1,0:T(8,128)(2,1)} %param.10), channel_id=1, source_target_pairs={{0,4},{4,0},{8,12},{12,8},{16,20},{20,16},{24,28},{28,24},{1,5},{5... | collective-permute-start | bytes 3145736 | tf_op jit(solution)/shard_map/ppermute | solution.py:21
  2.8 13.0 %collective-permute-start.4 = (bf16[192,1920]{1,0:T(8,128)(2,1)S(1)}, bf16[192,1920]{1,0:T(8,128)(2,1)}, u32[]{:S(2)}, u32[]{:S(2)}) collective-permute-start(bf16[192,1920]{1,0:T(8,128)(2,1)S(1)} %slice_select_fusion.2.mine1), channel_id=1, source_target_pairs={{0,8},{4,20},{8,0},{12,28},{16,24},{20,4},{24,16},{28,12},{1,9},{5... | collective-permute-start | bytes 2211848 | tf_op jit(solution)/shard_map/ppermute | solution.py:21
  7.8 11.9 %collective-permute-start.5 = (bf16[512,1280]{1,0:T(8,128)(2,1)}, bf16[512,1280]{1,0:T(8,128)(2,1)S(1)}, u32[]{:S(2)}, u32[]{:S(2)}) collective-permute-start(bf16[512,1280]{1,0:T(8,128)(2,1)} %slice_select_fusion), channel_id=1, source_target_pairs={{0,4},{4,0},{8,12},{12,8},{16,20},{20,16},{24,28},{28,24},{1,5},{5... | collective-permute-start | bytes 3932168 | tf_op jit(solution)/shard_map/ppermute | solution.py:21
  11.0 12.4 %collective-permute-start.1 = (bf16[256,1024]{1,0:T(8,128)(2,1)}, bf16[256,1024]{1,0:T(8,128)(2,1)}, u32[]{:S(2)}, u32[]{:S(2)}) collective-permute-start(bf16[256,1024]{1,0:T(8,128)(2,1)} %pad_maximum_fusion.2), channel_id=1, source_target_pairs={{0,16},{4,12},{8,24},{12,4},{16,0},{20,28},{24,8},{28,20},{1,17},{... | collective-permute-start | bytes 1572872 | tf_op jit(solution)/shard_map/ppermute | solution.py:21
  12.7 12.1 %copy-start.3 = (bf16[128,4096]{1,0:T(8,128)(2,1)S(1)}, bf16[128,4096]{1,0:T(8,128)(2,1)}, u32[]{:S(2)}) copy-start(bf16[128,4096]{1,0:T(8,128)(2,1)} %param.10) | copy-start | bytes 3145732
  15.7 21.4 %collective-permute-start.6 = (bf16[320,1920]{1,0:T(8,128)(2,1)S(1)}, bf16[320,1920]{1,0:T(8,128)(2,1)S(1)}, u32[]{:S(2)}, u32[]{:S(2)}) collective-permute-start(bf16[320,1920]{1,0:T(8,128)(2,1)S(1)} %slice_select_fusion.1.mine2), channel_id=1, source_target_pairs={{0,8},{4,20},{8,0},{12,28},{16,24},{20,4},{24,16},{28,12},{1,9},{5... | collective-permute-start | bytes 3686408 | tf_op jit(solution)/shard_map/ppermute | solution.py:21
  19.7 6.8 %collective-permute-start.2 = (bf16[512,640]{1,0:T(8,128)(2,1)S(1)}, bf16[512,640]{1,0:T(8,128)(2,1)S(1)}, u32[]{:S(2)}, u32[]{:S(2)}) collective-permute-start(bf16[512,640]{1,0:T(8,128)(2,1)S(1)} %slice_select_fusion.3), channel_id=1, source_target_pairs={{0,4},{4,0},{8,12},{12,8},{16,20},{20,16},{24,28},{28,24},{1,5},{5... | collective-permute-start | bytes 1966088 | tf_op jit(solution)/shard_map/ppermute | solution.py:21
  19.8 29.4 %collective-permute-start.7 = (bf16[512,1280]{1,0:T(8,128)(2,1)S(1)}, bf16[512,1280]{1,0:T(8,128)(2,1)S(1)}, u32[]{:S(2)}, u32[]{:S(2)}) collective-permute-start(bf16[512,1280]{1,0:T(8,128)(2,1)S(1)} %collective-permute-done.5.low), channel_id=1, source_target_pairs={{0,8},{4,20},{8,0},{12,28},{16,24},{20,4},{24,16},{28,12},{1,9},{5... | collective-permute-start | bytes 3932168 | tf_op jit(solution)/shard_map/ppermute | solution.py:21
  23.4 12.4 %collective-permute-start.3 = (bf16[256,1024]{1,0:T(8,128)(2,1)}, bf16[256,1024]{1,0:T(8,128)(2,1)S(1)}, u32[]{:S(2)}, u32[]{:S(2)}) collective-permute-start(bf16[256,1024]{1,0:T(8,128)(2,1)} %collective-permute-done.1.direct), channel_id=1, source_target_pairs={{0,1},{1,0},{2,3},{3,2},{4,5},{5,4},{6,7},{7,6},{8,9},{9,8},{10,11... | collective-permute-start | bytes 1572872 | tf_op jit(solution)/shard_map/ppermute | solution.py:254
  35.8 19.0 %collective-permute-start.11 = (bf16[512,640]{1,0:T(8,128)(2,1)S(1)}, bf16[512,640]{1,0:T(8,128)(2,1)S(1)}, u32[]{:S(2)}, u32[]{:S(2)}) collective-permute-start(bf16[512,640]{1,0:T(8,128)(2,1)S(1)} %collective-permute-done.2.high), channel_id=1, source_target_pairs={{0,8},{4,20},{8,0},{12,28},{16,24},{20,4},{24,16},{28,12},{1,9},{5... | collective-permute-start | bytes 1966088 | tf_op jit(solution)/shard_map/ppermute | solution.py:21
  52.1 11.8 %collective-permute-start.10 = (f16[128,1280]{1,0:T(8,128)(2,1)S(1)}, f16[128,1280]{1,0:T(8,128)(2,1)S(1)}, u32[]{:S(2)}, u32[]{:S(2)}) collective-permute-start(f16[128,1280]{1,0:T(8,128)(2,1)S(1)} %get-tuple-element.51), channel_id=1, source_target_pairs={{0,20},{4,8},{8,28},{12,0},{16,4},{20,24},{24,12},{28,16},{1,21},{... | collective-permute-start | bytes 983048 | tf_op jit(solution)/shard_map/ppermute | solution.py:21
  52.1 12.9 %collective-permute-start.8 = (f16[128,1280]{1,0:T(8,128)(2,1)S(1)}, f16[128,1280]{1,0:T(8,128)(2,1)S(1)}, u32[]{:S(2)}, u32[]{:S(2)}) collective-permute-start(f16[128,1280]{1,0:T(8,128)(2,1)S(1)} %get-tuple-element.50), channel_id=1, source_target_pairs={{0,16},{4,12},{8,24},{12,4},{16,0},{20,28},{24,8},{28,20},{1,17},{... | collective-permute-start | bytes 983048 | tf_op jit(solution)/shard_map/ppermute | solution.py:21
  53.4 12.1 %collective-permute-start.9 = (f32[128,1280]{1,0:T(8,128)S(1)}, f32[128,1280]{1,0:T(8,128)S(1)}, u32[]{:S(2)}, u32[]{:S(2)}) collective-permute-start(f32[128,1280]{1,0:T(8,128)S(1)} %get-tuple-element.41), channel_id=1, source_target_pairs={{0,4},{4,0},{8,12},{12,8},{16,20},{20,16},{24,28},{28,24},{1,5},{5... | collective-permute-start | bytes 1966088 | tf_op jit(solution)/shard_map/ppermute | solution.py:21
  57.8 8.2 %collective-permute-start.12 = (f16[128,1280]{1,0:T(8,128)(2,1)S(1)}, f16[128,1280]{1,0:T(8,128)(2,1)S(1)}, u32[]{:S(2)}, u32[]{:S(2)}) collective-permute-start(f16[128,1280]{1,0:T(8,128)(2,1)S(1)} %get-tuple-element.52), channel_id=1, source_target_pairs={{0,16},{4,12},{8,24},{12,4},{16,0},{20,28},{24,8},{28,20},{1,17},{... | collective-permute-start | bytes 983048 | tf_op jit(solution)/shard_map/ppermute | solution.py:21
  59.9 9.2 %collective-permute-start.14 = (f16[128,1280]{1,0:T(8,128)(2,1)S(1)}, f16[128,1280]{1,0:T(8,128)(2,1)S(1)}, u32[]{:S(2)}, u32[]{:S(2)}) collective-permute-start(f16[128,1280]{1,0:T(8,128)(2,1)S(1)} %get-tuple-element.53), channel_id=1, source_target_pairs={{0,20},{4,8},{8,28},{12,0},{16,4},{20,24},{24,12},{28,16},{1,21},{... | collective-permute-start | bytes 983048 | tf_op jit(solution)/shard_map/ppermute | solution.py:21
  63.8 5.3 %collective-permute-start.13 = (f32[128,1280]{1,0:T(8,128)S(1)}, f32[128,1280]{1,0:T(8,128)S(1)}, u32[]{:S(2)}, u32[]{:S(2)}) collective-permute-start(f32[128,1280]{1,0:T(8,128)S(1)} %get-tuple-element.44), channel_id=1, source_target_pairs={{0,4},{4,0},{8,12},{12,8},{16,20},{20,16},{24,28},{28,24},{1,5},{5... | collective-permute-start | bytes 1966088 | tf_op jit(solution)/shard_map/ppermute | solution.py:21
  65.0 7.5 %collective-permute-start.15 = (f16[128,1280]{1,0:T(8,128)(2,1)S(1)}, f16[128,1280]{1,0:T(8,128)(2,1)S(1)}, u32[]{:S(2)}, u32[]{:S(2)}) collective-permute-start(f16[128,1280]{1,0:T(8,128)(2,1)S(1)} %get-tuple-element.54), channel_id=1, source_target_pairs={{0,16},{4,12},{8,24},{12,4},{16,0},{20,28},{24,8},{28,20},{1,17},{... | collective-permute-start | bytes 983048 | tf_op jit(solution)/shard_map/ppermute | solution.py:21
  65.6 10.6 %collective-permute-start.17 = (f16[128,1280]{1,0:T(8,128)(2,1)S(1)}, f16[128,1280]{1,0:T(8,128)(2,1)S(1)}, u32[]{:S(2)}, u32[]{:S(2)}) collective-permute-start(f16[128,1280]{1,0:T(8,128)(2,1)S(1)} %get-tuple-element.55), channel_id=1, source_target_pairs={{0,20},{4,8},{8,28},{12,0},{16,4},{20,24},{24,12},{28,16},{1,21},{... | collective-permute-start | bytes 983048 | tf_op jit(solution)/shard_map/ppermute | solution.py:21
  66.0 10.2 %collective-permute-start.16 = (f32[128,1280]{1,0:T(8,128)S(1)}, f32[128,1280]{1,0:T(8,128)S(1)}, u32[]{:S(2)}, u32[]{:S(2)}) collective-permute-start(f32[128,1280]{1,0:T(8,128)S(1)} %get-tuple-element.47), channel_id=1, source_target_pairs={{0,4},{4,0},{8,12},{12,8},{16,20},{20,16},{24,28},{28,24},{1,5},{5... | collective-permute-start | bytes 1966088 | tf_op jit(solution)/shard_map/ppermute | solution.py:21
  69.1 7.3 %copy-start.8 = (f32[128]{0:T(128)S(1)}, f32[128]{0:T(128)}, u32[]{:S(2)}) copy-start(f32[128]{0:T(128)} %param.15) | copy-start | bytes 1540
  69.2 7.3 %copy-start.9 = (f32[128]{0:T(128)S(1)}, f32[128]{0:T(128)}, u32[]{:S(2)}) copy-start(f32[128]{0:T(128)} %param.16) | copy-start | bytes 1540
  76.2 14.5 %copy-start.6 = (s32[2,2]{1,0:T(2,128)S(1)}, s32[2,2]{1,0:T(2,128)}, u32[]{:S(2)}) copy-start(s32[2,2]{1,0:T(2,128)} %param.18) | copy-start | bytes 52
  76.2 14.8 %copy-start.10 = (s32[2]{0:T(128)S(1)}, s32[2]{0:T(128)}, u32[]{:S(2)}) copy-start(s32[2]{0:T(128)} %param.19) | copy-start | bytes 28
  77.5 13.1 %all-to-all-start = ((f32[32,1,4]{2,1,0:T(1,128)}), f32[32,1,4]{2,1,0:T(1,128)S(1)}, u32[]{:S(2)}, u32[]{:S(2)}) async-start(f32[32,1,4]{2,1,0:T(1,128)} %broadcast_in_dim.37), calls=%async_computation | async-start | bytes 32768 | tf_op jit(solution)/shard_map/all_to_all | solution.py:202
  (6 other events, 29.1 us)

commit v6 on v5

--- a/solution.py
+++ b/solution.py
@@ -1,4 +1,5 @@
 import functools
+import math
 
 import jax
 import jax.numpy as jnp
@@ -266,6 +267,7 @@
     )
 
     early, panel = early_sums(col_slots, (own, direct, passed), (*mine, low, high, *first))
+    scale = 2.0 ** math.floor(math.log2(65504 / (6 * 0.125 * tokens.shape[1] / 2)))
     parts = []
     for n in range(3):
         sources = (far_low,) if n == 0 else (far_low, far_high)
@@ -273,9 +275,10 @@
             n * third // 2, third // 2, col_slots, panel, early, sources
         )
         count = own.shape[0]
-        near = near.astype(jnp.float16)
-        own = own + swap(near[:count], Y, X).astype(jnp.float32)
-        other = swap(other, CORE, CORE) + swap(near[count:], Y | CORE, X | CORE).astype(jnp.float32)
+        near = (near * scale).astype(jnp.float16)
+        same, cross = swap(near[:count], Y, X), swap(near[count:], Y | CORE, X | CORE)
+        own = own + same.astype(jnp.float32) * (1 / scale)
+        other = swap(other, CORE, CORE) + cross.astype(jnp.float32) * (1 / scale)
         parts.append((jnp.where(on_gate, own, other), jnp.where(on_gate, other, own)))
     return parts
 

time: 91.9 us -> 91.9 us (level)
  no operation moved by 1% of the time
where the time goes in v6:
time: 91.9 us; the launch traced here: 91.6 us
  waiting for transfers between devices  32.4 us (35%)
  starting transfers between devices  22.8 us (25%)
  Pallas kernels  20.2 us (22%)
  other arithmetic  10.1 us (11%)
  local copies, waits for them, and re-layouts  4.61 us (5%)
  between operations  1.01 us (1%)
    ppermute x17, waiting for transfers between devices, swap(): lax.ppermute(value, 'fsdp', [(i, i ^ (core1 if i & CORE else core0)) for...  16.8 us
    ppermute x17, starting transfers between devices, swap(): lax.ppermute(value, 'fsdp', [(i, i ^ (core1 if i & CORE else core0)) for...  15.5 us
    pallas_call x1, Pallas kernels, early_sums(): pl.pallas_call(early_kernel, grid=(columns * BLK // step,), out_shape=(ja...  12 us
    ppermute x1, waiting for transfers between devices, exchanged_parts(): lax.ppermute(direct, 'tp', [(i, i ^ 1) for i in range(lax.axis_size('tp'))])  9.39 us
    pallas_call x3, Pallas kernels, late_sums(): pl.pallas_call(functools.partial(late_kernel, 2 * first_pair), grid=(pair...  8.23 us
    all_to_all x1, waiting for transfers between devices, pair_losses(): shares = lax.all_to_all(spread, ('fsdp', 'tp'), 0, 0, tiled=True)  6.15 us
    all_to_all x1, starting transfers between devices, pair_losses(): shares = lax.all_to_all(spread, ('fsdp', 'tp'), 0, 0, tiled=True)  5.85 us
    select_n x1, other arithmetic, exchanged_parts(): jnp.where(on_gate, up_packed[:, :split], gate_packed[:, :split])  2.51 us
  transfers between devices with their start and end apart: 19, of which 8 were waited for; matrix products, arithmetic and copies ran while one was open for 12% of the time, Pallas kernels for 22%

profile of v6, /device:TPU:0, one launch (start us, length us, event | category | flops | bytes accessed | tf_op | source)
XLA Modules:
  0.0 91.6 jit_solution(16369536721076200614)
XLA Ops:
  0.6 1.6 %slice_select_fusion.2.mine1 = bf16[192,1920]{1,0:T(8,128)(2,1)S(1)} fusion(bf16[512,1920]{1,0:T(8,128)(2,1)} %param.12, bf16[512,1920]{1,0:T(8,128)(2,1)} %param.11, pred[]{:T(512)S(6)} %eq.19), kind=kLoop, calls=%fused_computation.13 | loop fusion | flops 368640 | bytes 2211841 | tf_op jit(solution)/shard_map/jit(_where)/select_n | solution.py:240
  2.8 2.6 %collective-permute-start.4 = (bf16[192,1920]{1,0:T(8,128)(2,1)S(1)}, bf16[192,1920]{1,0:T(8,128)(2,1)}, u32[]{:S(2)}, u32[]{:S(2)}) collective-permute-start(bf16[192,1920]{1,0:T(8,128)(2,1)S(1)} %slice_select_fusion.2.mine1), channel_id=1, source_target_pairs={{0,8},{4,20},{8,0},{12,28},{16,24},{20,4},{24,16},{28,12},{1,9},{5... | collective-permute-start | bytes 2211848 | tf_op jit(solution)/shard_map/ppermute | solution.py:22
  5.3 2.5 %slice_select_fusion = bf16[512,1280]{1,0:T(8,128)(2,1)} fusion(bf16[512,1920]{1,0:T(8,128)(2,1)} %param.11, bf16[512,1920]{1,0:T(8,128)(2,1)S(1)} %copy-done, pred[]{:T(512)S(6)} %eq.19), kind=kLoop, calls=%fused_computation.3 | loop fusion | flops 655360 | bytes 3932161 | tf_op jit(solution)/shard_map/jit(_where)/select_n | solution.py:257
  11.0 1.4 %collective-permute-start.1 = (bf16[256,1024]{1,0:T(8,128)(2,1)}, bf16[256,1024]{1,0:T(8,128)(2,1)}, u32[]{:S(2)}, u32[]{:S(2)}) collective-permute-start(bf16[256,1024]{1,0:T(8,128)(2,1)} %pad_maximum_fusion.2), channel_id=1, source_target_pairs={{0,16},{4,12},{8,24},{12,4},{16,0},{20,28},{24,8},{28,20},{1,17},{... | collective-permute-start | bytes 1572872 | tf_op jit(solution)/shard_map/ppermute | solution.py:22
  12.7 3.0 %collective-permute-done.4.first1 = bf16[192,1920]{1,0:T(8,128)(2,1)} collective-permute-done((bf16[192,1920]{1,0:T(8,128)(2,1)S(1)}, bf16[192,1920]{1,0:T(8,128)(2,1)}, u32[]{:S(2)}, u32[]{:S(2)}) %collective-permute-start.4) | collective-permute-done | bytes 737312 | tf_op jit(solution)/shard_map/ppermute | solution.py:22
  15.7 2.6 %collective-permute-start.6 = (bf16[320,1920]{1,0:T(8,128)(2,1)S(1)}, bf16[320,1920]{1,0:T(8,128)(2,1)S(1)}, u32[]{:S(2)}, u32[]{:S(2)}) collective-permute-start(bf16[320,1920]{1,0:T(8,128)(2,1)S(1)} %slice_select_fusion.1.mine2), channel_id=1, source_target_pairs={{0,8},{4,20},{8,0},{12,28},{16,24},{20,4},{24,16},{28,12},{1,9},{5... | collective-permute-start | bytes 3686408 | tf_op jit(solution)/shard_map/ppermute | solution.py:22
  18.3 1.4 %slice_select_fusion.3 = bf16[512,640]{1,0:T(8,128)(2,1)S(1)} fusion(bf16[512,1920]{1,0:T(8,128)(2,1)} %param.11, bf16[512,1920]{1,0:T(8,128)(2,1)} %param.12, pred[]{:T(512)S(6)} %eq.19), kind=kLoop, calls=%fused_computation.17 | loop fusion | flops 327680 | bytes 1966081 | tf_op jit(solution)/shard_map/jit(_where)/select_n | solution.py:258
  19.8 3.6 %collective-permute-done.1.direct = bf16[256,1024]{1,0:T(8,128)(2,1)} collective-permute-done((bf16[256,1024]{1,0:T(8,128)(2,1)}, bf16[256,1024]{1,0:T(8,128)(2,1)}, u32[]{:S(2)}, u32[]{:S(2)}) %collective-permute-start.1) | collective-permute-done | bytes 524320 | tf_op jit(solution)/shard_map/ppermute | solution.py:22
  23.4 1.4 %collective-permute-start.3 = (bf16[256,1024]{1,0:T(8,128)(2,1)}, bf16[256,1024]{1,0:T(8,128)(2,1)S(1)}, u32[]{:S(2)}, u32[]{:S(2)}) collective-permute-start(bf16[256,1024]{1,0:T(8,128)(2,1)} %collective-permute-done.1.direct), channel_id=1, source_target_pairs={{0,1},{1,0},{2,3},{3,2},{4,5},{5,4},{6,7},{7,6},{8,9},{9,8},{10,11... | collective-permute-start | bytes 1572872 | tf_op jit(solution)/shard_map/ppermute | solution.py:255
  24.9 1.3 %constant_dynamic-update-slice_fusion = bf16[256,4096]{1,0:T(8,128)(2,1)S(1)} fusion(bf16[256,4096]{1,0:T(8,128)(2,1)S(1)} %constant_dynamic-update-slice_fusion.1, bf16[128,4096]{1,0:T(8,128)(2,1)} %collective-permute-done), kind=kLoop, calls=%fused_computation.19 | loop fusion | bytes 2097152 | tf_op jit(solution)/shard_map/concatenate | solution.py:264
  26.4 9.4 %collective-permute-done.3.passed = bf16[256,1024]{1,0:T(8,128)(2,1)S(1)} collective-permute-done((bf16[256,1024]{1,0:T(8,128)(2,1)}, bf16[256,1024]{1,0:T(8,128)(2,1)S(1)}, u32[]{:S(2)}, u32[]{:S(2)}) %collective-permute-start.3) | collective-permute-done | bytes 524320 | tf_op jit(solution)/shard_map/ppermute | solution.py:255
  35.8 1.3 %collective-permute-start.11 = (bf16[512,640]{1,0:T(8,128)(2,1)S(1)}, bf16[512,640]{1,0:T(8,128)(2,1)S(1)}, u32[]{:S(2)}, u32[]{:S(2)}) collective-permute-start(bf16[512,640]{1,0:T(8,128)(2,1)S(1)} %collective-permute-done.2.high), channel_id=1, source_target_pairs={{0,8},{4,20},{8,0},{12,28},{16,24},{20,4},{24,16},{28,12},{1,9},{5... | collective-permute-start | bytes 1966088 | tf_op jit(solution)/shard_map/ppermute | solution.py:22
  37.1 12.0 %shard_map.113 = (f32[512,3840]{1,0:T(8,128)S(1)}, bf16[512,512]{1,0:T(8,128)(2,1)S(1)}) custom-call(s32[32,15]{1,0:T(8,128)S(1)} %copy.33.col_slots, bf16[256,2048]{1,0:T(8,128)(2,1)S(1)} %pad_maximum_fusion.own, bf16[256,1024]{1,0:T(8,128)(2,1)} %collective-permute-done.1.direct, bf16[256,1024]{1,0:T(8,128)(2,1)S(1)} %collective-permute-done.3.passed, ...), custom_call_target="tpu_custom_call" | custom-call | flops 6039797760 | bytes 13762560 | tf_op jit(solution)/shard_map/pallas_call | solution.py:115
  49.2 2.7 %shard_map.114 = (f32[128,1280]{1,0:T(8,128)S(1)}, f32[128,1280]{1,0:T(8,128)S(1)}, f32[256,1280]{1,0:T(8,128)S(1)}) custom-call(s32[32,15]{1,0:T(8,128)S(1)} %copy.33.col_slots, bf16[512,512]{1,0:T(8,128)(2,1)S(1)} %get-tuple-element.37.panel, f32[512,3840]{1,0:T(8,128)S(1)} %get-tuple-element.38.early, bf16[512,1280]{1,0:T(8,128)(2,1)S(1)} %collective-permute-done.7.refs_0_), custom_call_target="tpu_custom_call" | custom-call | flops 671088640 | bytes 6553600 | tf_op jit(solution)/shard_map/pallas_call | solution.py:172
  52.2 1.3 %collective-permute-start.8 = (f16[128,1280]{1,0:T(8,128)(2,1)S(1)}, f16[128,1280]{1,0:T(8,128)(2,1)S(1)}, u32[]{:S(2)}, u32[]{:S(2)}) collective-permute-start(f16[128,1280]{1,0:T(8,128)(2,1)S(1)} %get-tuple-element.50), channel_id=1, source_target_pairs={{0,16},{4,12},{8,24},{12,4},{16,0},{20,28},{24,8},{28,20},{1,17},{... | collective-permute-start | bytes 983048 | tf_op jit(solution)/shard_map/ppermute | solution.py:22
  54.8 2.8 %shard_map.115 = (f32[128,1280]{1,0:T(8,128)S(1)}, f32[128,1280]{1,0:T(8,128)S(1)}, f32[256,1280]{1,0:T(8,128)S(1)}) custom-call(s32[32,15]{1,0:T(8,128)S(1)} %copy.33.col_slots, bf16[512,512]{1,0:T(8,128)(2,1)S(1)} %get-tuple-element.37.panel, f32[512,3840]{1,0:T(8,128)S(1)} %get-tuple-element.38.early, ...), custom_call_target="tpu_custom_call" | custom-call | flops 671088640 | bytes 7208960 | tf_op jit(solution)/shard_map/pallas_call | solution.py:172
  57.8 2.1 %collective-permute-start.12 = (f16[128,1280]{1,0:T(8,128)(2,1)S(1)}, f16[128,1280]{1,0:T(8,128)(2,1)S(1)}, u32[]{:S(2)}, u32[]{:S(2)}) collective-permute-start(f16[128,1280]{1,0:T(8,128)(2,1)S(1)} %get-tuple-element.52), channel_id=1, source_target_pairs={{0,16},{4,12},{8,24},{12,4},{16,0},{20,28},{24,8},{28,20},{1,17},{... | collective-permute-start | bytes 983048 | tf_op jit(solution)/shard_map/ppermute | solution.py:22
  60.8 2.8 %shard_map.116 = (f32[128,1280]{1,0:T(8,128)S(1)}, f32[128,1280]{1,0:T(8,128)S(1)}, f32[256,1280]{1,0:T(8,128)S(1)}) custom-call(s32[32,15]{1,0:T(8,128)S(1)} %copy.33.col_slots, bf16[512,512]{1,0:T(8,128)(2,1)S(1)} %get-tuple-element.37.panel, f32[512,3840]{1,0:T(8,128)S(1)} %get-tuple-element.38.early, ...), custom_call_target="tpu_custom_call" | custom-call | flops 671088640 | bytes 7208960 | tf_op jit(solution)/shard_map/pallas_call | solution.py:172
  63.8 1.2 %collective-permute-start.13 = (f32[128,1280]{1,0:T(8,128)S(1)}, f32[128,1280]{1,0:T(8,128)S(1)}, u32[]{:S(2)}, u32[]{:S(2)}) collective-permute-start(f32[128,1280]{1,0:T(8,128)S(1)} %get-tuple-element.44), channel_id=1, source_target_pairs={{0,4},{4,0},{8,12},{12,8},{16,20},{20,16},{24,28},{28,24},{1,5},{5... | collective-permute-start | bytes 1966088 | tf_op jit(solution)/shard_map/ppermute | solution.py:22
  66.2 2.9 %collective-permute-done.14 = f16[128,1280]{1,0:T(8,128)(2,1)S(1)} collective-permute-done((f16[128,1280]{1,0:T(8,128)(2,1)S(1)}, f16[128,1280]{1,0:T(8,128)(2,1)S(1)}, u32[]{:S(2)}, u32[]{:S(2)}) %collective-permute-start.14) | collective-permute-done | bytes 327712 | tf_op jit(solution)/shard_map/ppermute | solution.py:22
  69.7 2.8 %collective-permute-done.15 = f16[128,1280]{1,0:T(8,128)(2,1)S(1)} collective-permute-done((f16[128,1280]{1,0:T(8,128)(2,1)S(1)}, f16[128,1280]{1,0:T(8,128)(2,1)S(1)}, u32[]{:S(2)}, u32[]{:S(2)}) %collective-permute-start.15) | collective-permute-done | bytes 327712 | tf_op jit(solution)/shard_map/ppermute | solution.py:22
  72.5 3.7 %collective-permute-done.17 = f16[128,1280]{1,0:T(8,128)(2,1)S(1)} collective-permute-done((f16[128,1280]{1,0:T(8,128)(2,1)S(1)}, f16[128,1280]{1,0:T(8,128)(2,1)S(1)}, u32[]{:S(2)}, u32[]{:S(2)}) %collective-permute-start.17) | collective-permute-done | bytes 327712 | tf_op jit(solution)/shard_map/ppermute | solution.py:22
  77.6 5.8 %all-to-all-start = ((f32[32,1,4]{2,1,0:T(1,128)}), f32[32,1,4]{2,1,0:T(1,128)S(1)}, u32[]{:S(2)}, u32[]{:S(2)}) async-start(f32[32,1,4]{2,1,0:T(1,128)} %broadcast_in_dim.37), calls=%async_computation | async-start | bytes 32768 | tf_op jit(solution)/shard_map/all_to_all | solution.py:203
  84.5 6.2 %all-to-all-done = f32[32,1,4]{2,1,0:T(1,128)S(1)} async-done(((f32[32,1,4]{2,1,0:T(1,128)}), f32[32,1,4]{2,1,0:T(1,128)S(1)}, u32[]{:S(2)}, u32[]{:S(2)}) %all-to-all-start) | async-done | bytes 544 | tf_op jit(solution)/shard_map/all_to_all | solution.py:203
  (78 shorter events, 12.3 us)
Async XLA Ops:
  2.2 7.0 %collective-permute-start = (bf16[128,4096]{1,0:T(8,128)(2,1)}, bf16[128,4096]{1,0:T(8,128)(2,1)}, u32[]{:S(2)}, u32[]{:S(2)}) collective-permute-start(bf16[128,4096]{1,0:T(8,128)(2,1)} %param.10), channel_id=1, source_target_pairs={{0,4},{4,0},{8,12},{12,8},{16,20},{20,16},{24,28},{28,24},{1,5},{5... | collective-permute-start | bytes 3145736 | tf_op jit(solution)/shard_map/ppermute | solution.py:22
  2.8 13.0 %collective-permute-start.4 = (bf16[192,1920]{1,0:T(8,128)(2,1)S(1)}, bf16[192,1920]{1,0:T(8,128)(2,1)}, u32[]{:S(2)}, u32[]{:S(2)}) collective-permute-start(bf16[192,1920]{1,0:T(8,128)(2,1)S(1)} %slice_select_fusion.2.mine1), channel_id=1, source_target_pairs={{0,8},{4,20},{8,0},{12,28},{16,24},{20,4},{24,16},{28,12},{1,9},{5... | collective-permute-start | bytes 2211848 | tf_op jit(solution)/shard_map/ppermute | solution.py:22
  7.8 11.9 %collective-permute-start.5 = (bf16[512,1280]{1,0:T(8,128)(2,1)}, bf16[512,1280]{1,0:T(8,128)(2,1)S(1)}, u32[]{:S(2)}, u32[]{:S(2)}) collective-permute-start(bf16[512,1280]{1,0:T(8,128)(2,1)} %slice_select_fusion), channel_id=1, source_target_pairs={{0,4},{4,0},{8,12},{12,8},{16,20},{20,16},{24,28},{28,24},{1,5},{5... | collective-permute-start | bytes 3932168 | tf_op jit(solution)/shard_map/ppermute | solution.py:22
  11.0 12.4 %collective-permute-start.1 = (bf16[256,1024]{1,0:T(8,128)(2,1)}, bf16[256,1024]{1,0:T(8,128)(2,1)}, u32[]{:S(2)}, u32[]{:S(2)}) collective-permute-start(bf16[256,1024]{1,0:T(8,128)(2,1)} %pad_maximum_fusion.2), channel_id=1, source_target_pairs={{0,16},{4,12},{8,24},{12,4},{16,0},{20,28},{24,8},{28,20},{1,17},{... | collective-permute-start | bytes 1572872 | tf_op jit(solution)/shard_map/ppermute | solution.py:22
  12.7 12.1 %copy-start.3 = (bf16[128,4096]{1,0:T(8,128)(2,1)S(1)}, bf16[128,4096]{1,0:T(8,128)(2,1)}, u32[]{:S(2)}) copy-start(bf16[128,4096]{1,0:T(8,128)(2,1)} %param.10) | copy-start | bytes 3145732
  15.7 21.4 %collective-permute-start.6 = (bf16[320,1920]{1,0:T(8,128)(2,1)S(1)}, bf16[320,1920]{1,0:T(8,128)(2,1)S(1)}, u32[]{:S(2)}, u32[]{:S(2)}) collective-permute-start(bf16[320,1920]{1,0:T(8,128)(2,1)S(1)} %slice_select_fusion.1.mine2), channel_id=1, source_target_pairs={{0,8},{4,20},{8,0},{12,28},{16,24},{20,4},{24,16},{28,12},{1,9},{5... | collective-permute-start | bytes 3686408 | tf_op jit(solution)/shard_map/ppermute | solution.py:22
  19.7 6.8 %collective-permute-start.2 = (bf16[512,640]{1,0:T(8,128)(2,1)S(1)}, bf16[512,640]{1,0:T(8,128)(2,1)S(1)}, u32[]{:S(2)}, u32[]{:S(2)}) collective-permute-start(bf16[512,640]{1,0:T(8,128)(2,1)S(1)} %slice_select_fusion.3), channel_id=1, source_target_pairs={{0,4},{4,0},{8,12},{12,8},{16,20},{20,16},{24,28},{28,24},{1,5},{5... | collective-permute-start | bytes 1966088 | tf_op jit(solution)/shard_map/ppermute | solution.py:22
  19.8 29.4 %collective-permute-start.7 = (bf16[512,1280]{1,0:T(8,128)(2,1)S(1)}, bf16[512,1280]{1,0:T(8,128)(2,1)S(1)}, u32[]{:S(2)}, u32[]{:S(2)}) collective-permute-start(bf16[512,1280]{1,0:T(8,128)(2,1)S(1)} %collective-permute-done.5.low), channel_id=1, source_target_pairs={{0,8},{4,20},{8,0},{12,28},{16,24},{20,4},{24,16},{28,12},{1,9},{5... | collective-permute-start | bytes 3932168 | tf_op jit(solution)/shard_map/ppermute | solution.py:22
  23.4 12.4 %collective-permute-start.3 = (bf16[256,1024]{1,0:T(8,128)(2,1)}, bf16[256,1024]{1,0:T(8,128)(2,1)S(1)}, u32[]{:S(2)}, u32[]{:S(2)}) collective-permute-start(bf16[256,1024]{1,0:T(8,128)(2,1)} %collective-permute-done.1.direct), channel_id=1, source_target_pairs={{0,1},{1,0},{2,3},{3,2},{4,5},{5,4},{6,7},{7,6},{8,9},{9,8},{10,11... | collective-permute-start | bytes 1572872 | tf_op jit(solution)/shard_map/ppermute | solution.py:255
  35.8 19.0 %collective-permute-start.11 = (bf16[512,640]{1,0:T(8,128)(2,1)S(1)}, bf16[512,640]{1,0:T(8,128)(2,1)S(1)}, u32[]{:S(2)}, u32[]{:S(2)}) collective-permute-start(bf16[512,640]{1,0:T(8,128)(2,1)S(1)} %collective-permute-done.2.high), channel_id=1, source_target_pairs={{0,8},{4,20},{8,0},{12,28},{16,24},{20,4},{24,16},{28,12},{1,9},{5... | collective-permute-start | bytes 1966088 | tf_op jit(solution)/shard_map/ppermute | solution.py:22
  52.1 11.7 %collective-permute-start.10 = (f16[128,1280]{1,0:T(8,128)(2,1)S(1)}, f16[128,1280]{1,0:T(8,128)(2,1)S(1)}, u32[]{:S(2)}, u32[]{:S(2)}) collective-permute-start(f16[128,1280]{1,0:T(8,128)(2,1)S(1)} %get-tuple-element.51), channel_id=1, source_target_pairs={{0,20},{4,8},{8,28},{12,0},{16,4},{20,24},{24,12},{28,16},{1,21},{... | collective-permute-start | bytes 983048 | tf_op jit(solution)/shard_map/ppermute | solution.py:22
  52.2 12.9 %collective-permute-start.8 = (f16[128,1280]{1,0:T(8,128)(2,1)S(1)}, f16[128,1280]{1,0:T(8,128)(2,1)S(1)}, u32[]{:S(2)}, u32[]{:S(2)}) collective-permute-start(f16[128,1280]{1,0:T(8,128)(2,1)S(1)} %get-tuple-element.50), channel_id=1, source_target_pairs={{0,16},{4,12},{8,24},{12,4},{16,0},{20,28},{24,8},{28,20},{1,17},{... | collective-permute-start | bytes 983048 | tf_op jit(solution)/shard_map/ppermute | solution.py:22
  53.5 12.1 %collective-permute-start.9 = (f32[128,1280]{1,0:T(8,128)S(1)}, f32[128,1280]{1,0:T(8,128)S(1)}, u32[]{:S(2)}, u32[]{:S(2)}) collective-permute-start(f32[128,1280]{1,0:T(8,128)S(1)} %get-tuple-element.41), channel_id=1, source_target_pairs={{0,4},{4,0},{8,12},{12,8},{16,20},{20,16},{24,28},{28,24},{1,5},{5... | collective-permute-start | bytes 1966088 | tf_op jit(solution)/shard_map/ppermute | solution.py:22
  57.8 8.3 %collective-permute-start.12 = (f16[128,1280]{1,0:T(8,128)(2,1)S(1)}, f16[128,1280]{1,0:T(8,128)(2,1)S(1)}, u32[]{:S(2)}, u32[]{:S(2)}) collective-permute-start(f16[128,1280]{1,0:T(8,128)(2,1)S(1)} %get-tuple-element.52), channel_id=1, source_target_pairs={{0,16},{4,12},{8,24},{12,4},{16,0},{20,28},{24,8},{28,20},{1,17},{... | collective-permute-start | bytes 983048 | tf_op jit(solution)/shard_map/ppermute | solution.py:22
  60.0 9.2 %collective-permute-start.14 = (f16[128,1280]{1,0:T(8,128)(2,1)S(1)}, f16[128,1280]{1,0:T(8,128)(2,1)S(1)}, u32[]{:S(2)}, u32[]{:S(2)}) collective-permute-start(f16[128,1280]{1,0:T(8,128)(2,1)S(1)} %get-tuple-element.53), channel_id=1, source_target_pairs={{0,20},{4,8},{8,28},{12,0},{16,4},{20,24},{24,12},{28,16},{1,21},{... | collective-permute-start | bytes 983048 | tf_op jit(solution)/shard_map/ppermute | solution.py:22
  63.8 5.4 %collective-permute-start.13 = (f32[128,1280]{1,0:T(8,128)S(1)}, f32[128,1280]{1,0:T(8,128)S(1)}, u32[]{:S(2)}, u32[]{:S(2)}) collective-permute-start(f32[128,1280]{1,0:T(8,128)S(1)} %get-tuple-element.44), channel_id=1, source_target_pairs={{0,4},{4,0},{8,12},{12,8},{16,20},{20,16},{24,28},{28,24},{1,5},{5... | collective-permute-start | bytes 1966088 | tf_op jit(solution)/shard_map/ppermute | solution.py:22
  65.0 7.5 %collective-permute-start.15 = (f16[128,1280]{1,0:T(8,128)(2,1)S(1)}, f16[128,1280]{1,0:T(8,128)(2,1)S(1)}, u32[]{:S(2)}, u32[]{:S(2)}) collective-permute-start(f16[128,1280]{1,0:T(8,128)(2,1)S(1)} %get-tuple-element.54), channel_id=1, source_target_pairs={{0,16},{4,12},{8,24},{12,4},{16,0},{20,28},{24,8},{28,20},{1,17},{... | collective-permute-start | bytes 983048 | tf_op jit(solution)/shard_map/ppermute | solution.py:22
  65.6 10.6 %collective-permute-start.17 = (f16[128,1280]{1,0:T(8,128)(2,1)S(1)}, f16[128,1280]{1,0:T(8,128)(2,1)S(1)}, u32[]{:S(2)}, u32[]{:S(2)}) collective-permute-start(f16[128,1280]{1,0:T(8,128)(2,1)S(1)} %get-tuple-element.55), channel_id=1, source_target_pairs={{0,20},{4,8},{8,28},{12,0},{16,4},{20,24},{24,12},{28,16},{1,21},{... | collective-permute-start | bytes 983048 | tf_op jit(solution)/shard_map/ppermute | solution.py:22
  66.1 10.1 %collective-permute-start.16 = (f32[128,1280]{1,0:T(8,128)S(1)}, f32[128,1280]{1,0:T(8,128)S(1)}, u32[]{:S(2)}, u32[]{:S(2)}) collective-permute-start(f32[128,1280]{1,0:T(8,128)S(1)} %get-tuple-element.47), channel_id=1, source_target_pairs={{0,4},{4,0},{8,12},{12,8},{16,20},{20,16},{24,28},{28,24},{1,5},{5... | collective-permute-start | bytes 1966088 | tf_op jit(solution)/shard_map/ppermute | solution.py:22
  69.2 7.4 %copy-start.8 = (f32[128]{0:T(128)S(1)}, f32[128]{0:T(128)}, u32[]{:S(2)}) copy-start(f32[128]{0:T(128)} %param.15) | copy-start | bytes 1540
  69.2 7.4 %copy-start.9 = (f32[128]{0:T(128)S(1)}, f32[128]{0:T(128)}, u32[]{:S(2)}) copy-start(f32[128]{0:T(128)} %param.16) | copy-start | bytes 1540
  76.2 14.5 %copy-start.6 = (s32[2,2]{1,0:T(2,128)S(1)}, s32[2,2]{1,0:T(2,128)}, u32[]{:S(2)}) copy-start(s32[2,2]{1,0:T(2,128)} %param.18) | copy-start | bytes 52
  76.2 14.8 %copy-start.10 = (s32[2]{0:T(128)S(1)}, s32[2]{0:T(128)}, u32[]{:S(2)}) copy-start(s32[2]{0:T(128)} %param.19) | copy-start | bytes 28
  77.6 13.0 %all-to-all-start = ((f32[32,1,4]{2,1,0:T(1,128)}), f32[32,1,4]{2,1,0:T(1,128)S(1)}, u32[]{:S(2)}, u32[]{:S(2)}) async-start(f32[32,1,4]{2,1,0:T(1,128)} %broadcast_in_dim.37), calls=%async_computation | async-start | bytes 32768 | tf_op jit(solution)/shard_map/all_to_all | solution.py:203
  (6 other events, 29.1 us)

commit v7 on v6

--- a/solution.py
+++ b/solution.py
@@ -167,7 +167,7 @@
     count, depth = panel.shape
     width = sum(part.shape[1] for part in parts)
     out_rows = (count // 4, count // 4, count // 2)
-    step = pairs * BLK
+    step = 2 * pairs * BLK
     first = 2 * first_pair * BLK // step
     return pl.pallas_call(
         functools.partial(late_kernel, 2 * first_pair),
@@ -276,7 +276,8 @@
         )
         count = own.shape[0]
         near = (near * scale).astype(jnp.float16)
-        same, cross = swap(near[:count], Y, X), swap(near[count:], Y | CORE, X | CORE)
+        cross = swap(near[count:], Y | CORE, X | CORE)
+        same = swap(near[:count], Y, X)
         own = own + same.astype(jnp.float32) * (1 / scale)
         other = swap(other, CORE, CORE) + cross.astype(jnp.float32) * (1 / scale)
         parts.append((jnp.where(on_gate, own, other), jnp.where(on_gate, other, own)))

time: 91.9 us -> 91.9 us (level)
  Pallas kernels: 20.2 us -> 18.1 us
  waiting for transfers between devices: 32.4 us -> 34 us
    pallas_call x3, Pallas kernels: 8.23 us -> 6.1 us  [late_sums(): pl.pallas_call(functools.partial(late_kernel, 2 * first_pair), grid=(pair...]
    ppermute x17, waiting for transfers between devices: 16.8 us -> 18.5 us  [swap(): lax.ppermute(value, 'fsdp', [(i, i ^ (core1 if i & CORE else core0)) for...]
  transfers between devices with their start and end apart: 19 -> 19, of which waited for: 8 -> 8; matrix products, arithmetic and copies ran while one was open for 12% -> 12% of each run, Pallas kernels for 22% -> 20%
where the time goes in v7:
time: 91.9 us; the launch traced here: 91.6 us
  waiting for transfers between devices  34 us (37%)
  starting transfers between devices  23.3 us (25%)
  Pallas kernels  18.1 us (20%)
  other arithmetic  10.1 us (11%)
  local copies, waits for them, and re-layouts  4.61 us (5%)
  between operations  1.01 us (1%)
    ppermute x17, waiting for transfers between devices, swap(): lax.ppermute(value, 'fsdp', [(i, i ^ (core1 if i & CORE else core0)) for...  18.5 us
    ppermute x17, starting transfers between devices, swap(): lax.ppermute(value, 'fsdp', [(i, i ^ (core1 if i & CORE else core0)) for...  15.5 us
    pallas_call x1, Pallas kernels, early_sums(): pl.pallas_call(early_kernel, grid=(columns * BLK // step,), out_shape=(ja...  12 us
    ppermute x1, waiting for transfers between devices, exchanged_parts(): lax.ppermute(direct, 'tp', [(i, i ^ 1) for i in range(lax.axis_size('tp'))])  9.39 us
    all_to_all x1, starting transfers between devices, pair_losses(): shares = lax.all_to_all(spread, ('fsdp', 'tp'), 0, 0, tiled=True)  6.38 us
    all_to_all x1, waiting for transfers between devices, pair_losses(): shares = lax.all_to_all(spread, ('fsdp', 'tp'), 0, 0, tiled=True)  6.15 us
    pallas_call x3, Pallas kernels, late_sums(): pl.pallas_call(functools.partial(late_kernel, 2 * first_pair), grid=(pair...  6.1 us
    select_n x1, other arithmetic, exchanged_parts(): jnp.where(on_gate, up_packed[:, :split], gate_packed[:, :split])  2.51 us
  transfers between devices with their start and end apart: 19, of which 8 were waited for; matrix products, arithmetic and copies ran while one was open for 12% of the time, Pallas kernels for 20%

profile of v7, /device:TPU:0, one launch (start us, length us, event | category | flops | bytes accessed | tf_op | source)
XLA Modules:
  0.0 91.6 jit_solution(16734361347625281780)
XLA Ops:
  0.6 1.6 %slice_select_fusion.2.mine1 = bf16[192,1920]{1,0:T(8,128)(2,1)S(1)} fusion(bf16[512,1920]{1,0:T(8,128)(2,1)} %param.12, bf16[512,1920]{1,0:T(8,128)(2,1)} %param.11, pred[]{:T(512)S(6)} %eq.19), kind=kLoop, calls=%fused_computation.13 | loop fusion | flops 368640 | bytes 2211841 | tf_op jit(solution)/shard_map/jit(_where)/select_n | solution.py:240
  2.8 2.6 %collective-permute-start.4 = (bf16[192,1920]{1,0:T(8,128)(2,1)S(1)}, bf16[192,1920]{1,0:T(8,128)(2,1)}, u32[]{:S(2)}, u32[]{:S(2)}) collective-permute-start(bf16[192,1920]{1,0:T(8,128)(2,1)S(1)} %slice_select_fusion.2.mine1), channel_id=1, source_target_pairs={{0,8},{4,20},{8,0},{12,28},{16,24},{20,4},{24,16},{28,12},{1,9},{5... | collective-permute-start | bytes 2211848 | tf_op jit(solution)/shard_map/ppermute | solution.py:22
  5.3 2.5 %slice_select_fusion = bf16[512,1280]{1,0:T(8,128)(2,1)} fusion(bf16[512,1920]{1,0:T(8,128)(2,1)} %param.11, bf16[512,1920]{1,0:T(8,128)(2,1)S(1)} %copy-done, pred[]{:T(512)S(6)} %eq.19), kind=kLoop, calls=%fused_computation.3 | loop fusion | flops 655360 | bytes 3932161 | tf_op jit(solution)/shard_map/jit(_where)/select_n | solution.py:257
  11.0 1.4 %collective-permute-start.1 = (bf16[256,1024]{1,0:T(8,128)(2,1)}, bf16[256,1024]{1,0:T(8,128)(2,1)}, u32[]{:S(2)}, u32[]{:S(2)}) collective-permute-start(bf16[256,1024]{1,0:T(8,128)(2,1)} %pad_maximum_fusion.2), channel_id=1, source_target_pairs={{0,16},{4,12},{8,24},{12,4},{16,0},{20,28},{24,8},{28,20},{1,17},{... | collective-permute-start | bytes 1572872 | tf_op jit(solution)/shard_map/ppermute | solution.py:22
  12.7 3.0 %collective-permute-done.4.first1 = bf16[192,1920]{1,0:T(8,128)(2,1)} collective-permute-done((bf16[192,1920]{1,0:T(8,128)(2,1)S(1)}, bf16[192,1920]{1,0:T(8,128)(2,1)}, u32[]{:S(2)}, u32[]{:S(2)}) %collective-permute-start.4) | collective-permute-done | bytes 737312 | tf_op jit(solution)/shard_map/ppermute | solution.py:22
  15.7 2.6 %collective-permute-start.6 = (bf16[320,1920]{1,0:T(8,128)(2,1)S(1)}, bf16[320,1920]{1,0:T(8,128)(2,1)S(1)}, u32[]{:S(2)}, u32[]{:S(2)}) collective-permute-start(bf16[320,1920]{1,0:T(8,128)(2,1)S(1)} %slice_select_fusion.1.mine2), channel_id=1, source_target_pairs={{0,8},{4,20},{8,0},{12,28},{16,24},{20,4},{24,16},{28,12},{1,9},{5... | collective-permute-start | bytes 3686408 | tf_op jit(solution)/shard_map/ppermute | solution.py:22
  18.3 1.4 %slice_select_fusion.3 = bf16[512,640]{1,0:T(8,128)(2,1)S(1)} fusion(bf16[512,1920]{1,0:T(8,128)(2,1)} %param.11, bf16[512,1920]{1,0:T(8,128)(2,1)} %param.12, pred[]{:T(512)S(6)} %eq.19), kind=kLoop, calls=%fused_computation.17 | loop fusion | flops 327680 | bytes 1966081 | tf_op jit(solution)/shard_map/jit(_where)/select_n | solution.py:258
  19.8 3.6 %collective-permute-done.1.direct = bf16[256,1024]{1,0:T(8,128)(2,1)} collective-permute-done((bf16[256,1024]{1,0:T(8,128)(2,1)}, bf16[256,1024]{1,0:T(8,128)(2,1)}, u32[]{:S(2)}, u32[]{:S(2)}) %collective-permute-start.1) | collective-permute-done | bytes 524320 | tf_op jit(solution)/shard_map/ppermute | solution.py:22
  23.4 1.4 %collective-permute-start.3 = (bf16[256,1024]{1,0:T(8,128)(2,1)}, bf16[256,1024]{1,0:T(8,128)(2,1)S(1)}, u32[]{:S(2)}, u32[]{:S(2)}) collective-permute-start(bf16[256,1024]{1,0:T(8,128)(2,1)} %collective-permute-done.1.direct), channel_id=1, source_target_pairs={{0,1},{1,0},{2,3},{3,2},{4,5},{5,4},{6,7},{7,6},{8,9},{9,8},{10,11... | collective-permute-start | bytes 1572872 | tf_op jit(solution)/shard_map/ppermute | solution.py:255
  24.9 1.3 %constant_dynamic-update-slice_fusion = bf16[256,4096]{1,0:T(8,128)(2,1)S(1)} fusion(bf16[256,4096]{1,0:T(8,128)(2,1)S(1)} %constant_dynamic-update-slice_fusion.1, bf16[128,4096]{1,0:T(8,128)(2,1)} %collective-permute-done), kind=kLoop, calls=%fused_computation.19 | loop fusion | bytes 2097152 | tf_op jit(solution)/shard_map/concatenate | solution.py:264
  26.4 9.4 %collective-permute-done.3.passed = bf16[256,1024]{1,0:T(8,128)(2,1)S(1)} collective-permute-done((bf16[256,1024]{1,0:T(8,128)(2,1)}, bf16[256,1024]{1,0:T(8,128)(2,1)S(1)}, u32[]{:S(2)}, u32[]{:S(2)}) %collective-permute-start.3) | collective-permute-done | bytes 524320 | tf_op jit(solution)/shard_map/ppermute | solution.py:255
  35.8 1.3 %collective-permute-start.11 = (bf16[512,640]{1,0:T(8,128)(2,1)S(1)}, bf16[512,640]{1,0:T(8,128)(2,1)S(1)}, u32[]{:S(2)}, u32[]{:S(2)}) collective-permute-start(bf16[512,640]{1,0:T(8,128)(2,1)S(1)} %collective-permute-done.2.high), channel_id=1, source_target_pairs={{0,8},{4,20},{8,0},{12,28},{16,24},{20,4},{24,16},{28,12},{1,9},{5... | collective-permute-start | bytes 1966088 | tf_op jit(solution)/shard_map/ppermute | solution.py:22
  37.1 12.0 %shard_map.113 = (f32[512,3840]{1,0:T(8,128)S(1)}, bf16[512,512]{1,0:T(8,128)(2,1)S(1)}) custom-call(s32[32,15]{1,0:T(8,128)S(1)} %copy.33.col_slots, bf16[256,2048]{1,0:T(8,128)(2,1)S(1)} %pad_maximum_fusion.own, bf16[256,1024]{1,0:T(8,128)(2,1)} %collective-permute-done.1.direct, bf16[256,1024]{1,0:T(8,128)(2,1)S(1)} %collective-permute-done.3.passed, ...), custom_call_target="tpu_custom_call" | custom-call | flops 6039797760 | bytes 13762560 | tf_op jit(solution)/shard_map/pallas_call | solution.py:115
  49.2 2.0 %shard_map.114 = (f32[128,1280]{1,0:T(8,128)S(1)}, f32[128,1280]{1,0:T(8,128)S(1)}, f32[256,1280]{1,0:T(8,128)S(1)}) custom-call(s32[32,15]{1,0:T(8,128)S(1)} %copy.33.col_slots, bf16[512,512]{1,0:T(8,128)(2,1)S(1)} %get-tuple-element.37.panel, f32[512,3840]{1,0:T(8,128)S(1)} %get-tuple-element.38.early, bf16[512,1280]{1,0:T(8,128)(2,1)S(1)} %collective-permute-done.7.refs_0_), custom_call_target="tpu_custom_call" | custom-call | flops 671088640 | bytes 6553600 | tf_op jit(solution)/shard_map/pallas_call | solution.py:172
  51.4 1.3 %collective-permute-start.8 = (f16[128,1280]{1,0:T(8,128)(2,1)S(1)}, f16[128,1280]{1,0:T(8,128)(2,1)S(1)}, u32[]{:S(2)}, u32[]{:S(2)}) collective-permute-start(f16[128,1280]{1,0:T(8,128)(2,1)S(1)} %get-tuple-element.50), channel_id=1, source_target_pairs={{0,16},{4,12},{8,24},{12,4},{16,0},{20,28},{24,8},{28,20},{1,17},{... | collective-permute-start | bytes 983048 | tf_op jit(solution)/shard_map/ppermute | solution.py:22
  53.3 2.3 %collective-permute-done.11.refs_1_ = bf16[512,640]{1,0:T(8,128)(2,1)S(1)} collective-permute-done((bf16[512,640]{1,0:T(8,128)(2,1)S(1)}, bf16[512,640]{1,0:T(8,128)(2,1)S(1)}, u32[]{:S(2)}, u32[]{:S(2)}) %collective-permute-start.11) | collective-permute-done | bytes 655392 | tf_op jit(solution)/shard_map/ppermute | solution.py:22
  55.5 2.1 %shard_map.115 = (f32[128,1280]{1,0:T(8,128)S(1)}, f32[128,1280]{1,0:T(8,128)S(1)}, f32[256,1280]{1,0:T(8,128)S(1)}) custom-call(s32[32,15]{1,0:T(8,128)S(1)} %copy.33.col_slots, bf16[512,512]{1,0:T(8,128)(2,1)S(1)} %get-tuple-element.37.panel, f32[512,3840]{1,0:T(8,128)S(1)} %get-tuple-element.38.early, ...), custom_call_target="tpu_custom_call" | custom-call | flops 671088640 | bytes 7208960 | tf_op jit(solution)/shard_map/pallas_call | solution.py:172
  57.8 2.2 %collective-permute-start.12 = (f16[128,1280]{1,0:T(8,128)(2,1)S(1)}, f16[128,1280]{1,0:T(8,128)(2,1)S(1)}, u32[]{:S(2)}, u32[]{:S(2)}) collective-permute-start(f16[128,1280]{1,0:T(8,128)(2,1)S(1)} %get-tuple-element.52), channel_id=1, source_target_pairs={{0,16},{4,12},{8,24},{12,4},{16,0},{20,28},{24,8},{28,20},{1,17},{... | collective-permute-start | bytes 983048 | tf_op jit(solution)/shard_map/ppermute | solution.py:22
  60.8 2.1 %shard_map.116 = (f32[128,1280]{1,0:T(8,128)S(1)}, f32[128,1280]{1,0:T(8,128)S(1)}, f32[256,1280]{1,0:T(8,128)S(1)}) custom-call(s32[32,15]{1,0:T(8,128)S(1)} %copy.33.col_slots, bf16[512,512]{1,0:T(8,128)(2,1)S(1)} %get-tuple-element.37.panel, f32[512,3840]{1,0:T(8,128)S(1)} %get-tuple-element.38.early, ...), custom_call_target="tpu_custom_call" | custom-call | flops 671088640 | bytes 7208960 | tf_op jit(solution)/shard_map/pallas_call | solution.py:172
  65.6 3.1 %collective-permute-done.14 = f16[128,1280]{1,0:T(8,128)(2,1)S(1)} collective-permute-done((f16[128,1280]{1,0:T(8,128)(2,1)S(1)}, f16[128,1280]{1,0:T(8,128)(2,1)S(1)}, u32[]{:S(2)}, u32[]{:S(2)}) %collective-permute-start.14) | collective-permute-done | bytes 327712 | tf_op jit(solution)/shard_map/ppermute | solution.py:22
  69.2 3.0 %collective-permute-done.15 = f16[128,1280]{1,0:T(8,128)(2,1)S(1)} collective-permute-done((f16[128,1280]{1,0:T(8,128)(2,1)S(1)}, f16[128,1280]{1,0:T(8,128)(2,1)S(1)}, u32[]{:S(2)}, u32[]{:S(2)}) %collective-permute-start.15) | collective-permute-done | bytes 327712 | tf_op jit(solution)/shard_map/ppermute | solution.py:22
  72.2 3.5 %collective-permute-done.17 = f16[128,1280]{1,0:T(8,128)(2,1)S(1)} collective-permute-done((f16[128,1280]{1,0:T(8,128)(2,1)S(1)}, f16[128,1280]{1,0:T(8,128)(2,1)S(1)}, u32[]{:S(2)}, u32[]{:S(2)}) %collective-permute-start.17) | collective-permute-done | bytes 327712 | tf_op jit(solution)/shard_map/ppermute | solution.py:22
  77.1 6.4 %all-to-all-start = ((f32[32,1,4]{2,1,0:T(1,128)}), f32[32,1,4]{2,1,0:T(1,128)S(1)}, u32[]{:S(2)}, u32[]{:S(2)}) async-start(f32[32,1,4]{2,1,0:T(1,128)} %broadcast_in_dim.37), calls=%async_computation | async-start | bytes 32768 | tf_op jit(solution)/shard_map/all_to_all | solution.py:203
  84.5 6.2 %all-to-all-done = f32[32,1,4]{2,1,0:T(1,128)S(1)} async-done(((f32[32,1,4]{2,1,0:T(1,128)}), f32[32,1,4]{2,1,0:T(1,128)S(1)}, u32[]{:S(2)}, u32[]{:S(2)}) %all-to-all-start) | async-done | bytes 544 | tf_op jit(solution)/shard_map/all_to_all | solution.py:203
  (78 shorter events, 12.7 us)
Async XLA Ops:
  2.2 7.0 %collective-permute-start = (bf16[128,4096]{1,0:T(8,128)(2,1)}, bf16[128,4096]{1,0:T(8,128)(2,1)}, u32[]{:S(2)}, u32[]{:S(2)}) collective-permute-start(bf16[128,4096]{1,0:T(8,128)(2,1)} %param.10), channel_id=1, source_target_pairs={{0,4},{4,0},{8,12},{12,8},{16,20},{20,16},{24,28},{28,24},{1,5},{5... | collective-permute-start | bytes 3145736 | tf_op jit(solution)/shard_map/ppermute | solution.py:22
  2.8 13.0 %collective-permute-start.4 = (bf16[192,1920]{1,0:T(8,128)(2,1)S(1)}, bf16[192,1920]{1,0:T(8,128)(2,1)}, u32[]{:S(2)}, u32[]{:S(2)}) collective-permute-start(bf16[192,1920]{1,0:T(8,128)(2,1)S(1)} %slice_select_fusion.2.mine1), channel_id=1, source_target_pairs={{0,8},{4,20},{8,0},{12,28},{16,24},{20,4},{24,16},{28,12},{1,9},{5... | collective-permute-start | bytes 2211848 | tf_op jit(solution)/shard_map/ppermute | solution.py:22
  7.8 11.9 %collective-permute-start.5 = (bf16[512,1280]{1,0:T(8,128)(2,1)}, bf16[512,1280]{1,0:T(8,128)(2,1)S(1)}, u32[]{:S(2)}, u32[]{:S(2)}) collective-permute-start(bf16[512,1280]{1,0:T(8,128)(2,1)} %slice_select_fusion), channel_id=1, source_target_pairs={{0,4},{4,0},{8,12},{12,8},{16,20},{20,16},{24,28},{28,24},{1,5},{5... | collective-permute-start | bytes 3932168 | tf_op jit(solution)/shard_map/ppermute | solution.py:22
  11.0 12.4 %collective-permute-start.1 = (bf16[256,1024]{1,0:T(8,128)(2,1)}, bf16[256,1024]{1,0:T(8,128)(2,1)}, u32[]{:S(2)}, u32[]{:S(2)}) collective-permute-start(bf16[256,1024]{1,0:T(8,128)(2,1)} %pad_maximum_fusion.2), channel_id=1, source_target_pairs={{0,16},{4,12},{8,24},{12,4},{16,0},{20,28},{24,8},{28,20},{1,17},{... | collective-permute-start | bytes 1572872 | tf_op jit(solution)/shard_map/ppermute | solution.py:22
  12.7 12.1 %copy-start.3 = (bf16[128,4096]{1,0:T(8,128)(2,1)S(1)}, bf16[128,4096]{1,0:T(8,128)(2,1)}, u32[]{:S(2)}) copy-start(bf16[128,4096]{1,0:T(8,128)(2,1)} %param.10) | copy-start | bytes 3145732
  15.7 21.4 %collective-permute-start.6 = (bf16[320,1920]{1,0:T(8,128)(2,1)S(1)}, bf16[320,1920]{1,0:T(8,128)(2,1)S(1)}, u32[]{:S(2)}, u32[]{:S(2)}) collective-permute-start(bf16[320,1920]{1,0:T(8,128)(2,1)S(1)} %slice_select_fusion.1.mine2), channel_id=1, source_target_pairs={{0,8},{4,20},{8,0},{12,28},{16,24},{20,4},{24,16},{28,12},{1,9},{5... | collective-permute-start | bytes 3686408 | tf_op jit(solution)/shard_map/ppermute | solution.py:22
  19.7 6.8 %collective-permute-start.2 = (bf16[512,640]{1,0:T(8,128)(2,1)S(1)}, bf16[512,640]{1,0:T(8,128)(2,1)S(1)}, u32[]{:S(2)}, u32[]{:S(2)}) collective-permute-start(bf16[512,640]{1,0:T(8,128)(2,1)S(1)} %slice_select_fusion.3), channel_id=1, source_target_pairs={{0,4},{4,0},{8,12},{12,8},{16,20},{20,16},{24,28},{28,24},{1,5},{5... | collective-permute-start | bytes 1966088 | tf_op jit(solution)/shard_map/ppermute | solution.py:22
  19.8 29.4 %collective-permute-start.7 = (bf16[512,1280]{1,0:T(8,128)(2,1)S(1)}, bf16[512,1280]{1,0:T(8,128)(2,1)S(1)}, u32[]{:S(2)}, u32[]{:S(2)}) collective-permute-start(bf16[512,1280]{1,0:T(8,128)(2,1)S(1)} %collective-permute-done.5.low), channel_id=1, source_target_pairs={{0,8},{4,20},{8,0},{12,28},{16,24},{20,4},{24,16},{28,12},{1,9},{5... | collective-permute-start | bytes 3932168 | tf_op jit(solution)/shard_map/ppermute | solution.py:22
  23.4 12.4 %collective-permute-start.3 = (bf16[256,1024]{1,0:T(8,128)(2,1)}, bf16[256,1024]{1,0:T(8,128)(2,1)S(1)}, u32[]{:S(2)}, u32[]{:S(2)}) collective-permute-start(bf16[256,1024]{1,0:T(8,128)(2,1)} %collective-permute-done.1.direct), channel_id=1, source_target_pairs={{0,1},{1,0},{2,3},{3,2},{4,5},{5,4},{6,7},{7,6},{8,9},{9,8},{10,11... | collective-permute-start | bytes 1572872 | tf_op jit(solution)/shard_map/ppermute | solution.py:255
  35.8 19.7 %collective-permute-start.11 = (bf16[512,640]{1,0:T(8,128)(2,1)S(1)}, bf16[512,640]{1,0:T(8,128)(2,1)S(1)}, u32[]{:S(2)}, u32[]{:S(2)}) collective-permute-start(bf16[512,640]{1,0:T(8,128)(2,1)S(1)} %collective-permute-done.2.high), channel_id=1, source_target_pairs={{0,8},{4,20},{8,0},{12,28},{16,24},{20,4},{24,16},{28,12},{1,9},{5... | collective-permute-start | bytes 1966088 | tf_op jit(solution)/shard_map/ppermute | solution.py:22
  51.4 11.8 %collective-permute-start.10 = (f16[128,1280]{1,0:T(8,128)(2,1)S(1)}, f16[128,1280]{1,0:T(8,128)(2,1)S(1)}, u32[]{:S(2)}, u32[]{:S(2)}) collective-permute-start(f16[128,1280]{1,0:T(8,128)(2,1)S(1)} %get-tuple-element.51), channel_id=1, source_target_pairs={{0,20},{4,8},{8,28},{12,0},{16,4},{20,24},{24,12},{28,16},{1,21},{... | collective-permute-start | bytes 983048 | tf_op jit(solution)/shard_map/ppermute | solution.py:22
  51.4 12.9 %collective-permute-start.8 = (f16[128,1280]{1,0:T(8,128)(2,1)S(1)}, f16[128,1280]{1,0:T(8,128)(2,1)S(1)}, u32[]{:S(2)}, u32[]{:S(2)}) collective-permute-start(f16[128,1280]{1,0:T(8,128)(2,1)S(1)} %get-tuple-element.50), channel_id=1, source_target_pairs={{0,16},{4,12},{8,24},{12,4},{16,0},{20,28},{24,8},{28,20},{1,17},{... | collective-permute-start | bytes 983048 | tf_op jit(solution)/shard_map/ppermute | solution.py:22
  52.7 12.2 %collective-permute-start.9 = (f32[128,1280]{1,0:T(8,128)S(1)}, f32[128,1280]{1,0:T(8,128)S(1)}, u32[]{:S(2)}, u32[]{:S(2)}) collective-permute-start(f32[128,1280]{1,0:T(8,128)S(1)} %get-tuple-element.41), channel_id=1, source_target_pairs={{0,4},{4,0},{8,12},{12,8},{16,20},{20,16},{24,28},{28,24},{1,5},{5... | collective-permute-start | bytes 1966088 | tf_op jit(solution)/shard_map/ppermute | solution.py:22
  57.8 7.6 %collective-permute-start.12 = (f16[128,1280]{1,0:T(8,128)(2,1)S(1)}, f16[128,1280]{1,0:T(8,128)(2,1)S(1)}, u32[]{:S(2)}, u32[]{:S(2)}) collective-permute-start(f16[128,1280]{1,0:T(8,128)(2,1)S(1)} %get-tuple-element.52), channel_id=1, source_target_pairs={{0,16},{4,12},{8,24},{12,4},{16,0},{20,28},{24,8},{28,20},{1,17},{... | collective-permute-start | bytes 983048 | tf_op jit(solution)/shard_map/ppermute | solution.py:22
  60.0 8.7 %collective-permute-start.14 = (f16[128,1280]{1,0:T(8,128)(2,1)S(1)}, f16[128,1280]{1,0:T(8,128)(2,1)S(1)}, u32[]{:S(2)}, u32[]{:S(2)}) collective-permute-start(f16[128,1280]{1,0:T(8,128)(2,1)S(1)} %get-tuple-element.53), channel_id=1, source_target_pairs={{0,20},{4,8},{8,28},{12,0},{16,4},{20,24},{24,12},{28,16},{1,21},{... | collective-permute-start | bytes 983048 | tf_op jit(solution)/shard_map/ppermute | solution.py:22
  63.2 5.5 %collective-permute-start.13 = (f32[128,1280]{1,0:T(8,128)S(1)}, f32[128,1280]{1,0:T(8,128)S(1)}, u32[]{:S(2)}, u32[]{:S(2)}) collective-permute-start(f32[128,1280]{1,0:T(8,128)S(1)} %get-tuple-element.44), channel_id=1, source_target_pairs={{0,4},{4,0},{8,12},{12,8},{16,20},{20,16},{24,28},{28,24},{1,5},{5... | collective-permute-start | bytes 1966088 | tf_op jit(solution)/shard_map/ppermute | solution.py:22
  64.4 7.8 %collective-permute-start.15 = (f16[128,1280]{1,0:T(8,128)(2,1)S(1)}, f16[128,1280]{1,0:T(8,128)(2,1)S(1)}, u32[]{:S(2)}, u32[]{:S(2)}) collective-permute-start(f16[128,1280]{1,0:T(8,128)(2,1)S(1)} %get-tuple-element.54), channel_id=1, source_target_pairs={{0,16},{4,12},{8,24},{12,4},{16,0},{20,28},{24,8},{28,20},{1,17},{... | collective-permute-start | bytes 983048 | tf_op jit(solution)/shard_map/ppermute | solution.py:22
  64.9 10.7 %collective-permute-start.17 = (f16[128,1280]{1,0:T(8,128)(2,1)S(1)}, f16[128,1280]{1,0:T(8,128)(2,1)S(1)}, u32[]{:S(2)}, u32[]{:S(2)}) collective-permute-start(f16[128,1280]{1,0:T(8,128)(2,1)S(1)} %get-tuple-element.55), channel_id=1, source_target_pairs={{0,20},{4,8},{8,28},{12,0},{16,4},{20,24},{24,12},{28,16},{1,21},{... | collective-permute-start | bytes 983048 | tf_op jit(solution)/shard_map/ppermute | solution.py:22
  65.4 10.3 %collective-permute-start.16 = (f32[128,1280]{1,0:T(8,128)S(1)}, f32[128,1280]{1,0:T(8,128)S(1)}, u32[]{:S(2)}, u32[]{:S(2)}) collective-permute-start(f32[128,1280]{1,0:T(8,128)S(1)} %get-tuple-element.47), channel_id=1, source_target_pairs={{0,4},{4,0},{8,12},{12,8},{16,20},{20,16},{24,28},{28,24},{1,5},{5... | collective-permute-start | bytes 1966088 | tf_op jit(solution)/shard_map/ppermute | solution.py:22
  68.7 7.4 %copy-start.8 = (f32[128]{0:T(128)S(1)}, f32[128]{0:T(128)}, u32[]{:S(2)}) copy-start(f32[128]{0:T(128)} %param.15) | copy-start | bytes 1540
  68.7 7.4 %copy-start.9 = (f32[128]{0:T(128)S(1)}, f32[128]{0:T(128)}, u32[]{:S(2)}) copy-start(f32[128]{0:T(128)} %param.16) | copy-start | bytes 1540
  75.7 15.0 %copy-start.6 = (s32[2,2]{1,0:T(2,128)S(1)}, s32[2,2]{1,0:T(2,128)}, u32[]{:S(2)}) copy-start(s32[2,2]{1,0:T(2,128)} %param.18) | copy-start | bytes 52
  75.7 15.4 %copy-start.10 = (s32[2]{0:T(128)S(1)}, s32[2]{0:T(128)}, u32[]{:S(2)}) copy-start(s32[2]{0:T(128)} %param.19) | copy-start | bytes 28
  77.1 13.5 %all-to-all-start = ((f32[32,1,4]{2,1,0:T(1,128)}), f32[32,1,4]{2,1,0:T(1,128)S(1)}, u32[]{:S(2)}, u32[]{:S(2)}) async-start(f32[32,1,4]{2,1,0:T(1,128)} %broadcast_in_dim.37), calls=%async_computation | async-start | bytes 32768 | tf_op jit(solution)/shard_map/all_to_all | solution.py:203
  (6 other events, 29.1 us)
